TPU v7x, 512 devices: a whole 4x8x8 slice. The times are simulated.
512 devices in a mesh: gz: 16 (over z_lo, x, core), xy: 32 (over z_hi, y).
Axes of the slice: x: 4, y: 8, z: 8 (z_hi: 4, z_lo: 2; z = z_hi * 2 + z_lo), core: 2. Of those that a mesh axis runs over, the one named last changes fastest.
Arguments:
- loaded_planes: bfloat16 [4, 16, 1, 32, 64, 128], P(None, 'gz', None, 'xy'), may hold values from -6 to 6
- first_kernel: bfloat16 [16, 4, 3, 3, 3], replicated, may hold values from -0.625 to 0.625
- first_bias: float32 [16], replicated, may hold values from -3 to 3
- second_kernel: bfloat16 [32, 16, 3, 3, 3], replicated, may hold values from -0.3125 to 0.3125
- second_bias: float32 [32], replicated, may hold values from -3 to 3
- cotangent: bfloat16 [32, 256, 32, 64], P(None, 'gz', 'xy'), may hold values from -6 to 6
Outputs:
- features: bfloat16 [32, 256, 32, 64], P(None, 'gz', 'xy')
- input_grad: bfloat16 [4, 512, 64, 128], P(None, 'gz', 'xy')
- first_kernel_grad: float32 [16, 4, 3, 3, 3], replicated
- first_bias_grad: float32 [16], replicated
- second_kernel_grad: float32 [32, 16, 3, 3, 3], replicated
- second_bias_grad: float32 [32], replicated
All inputs are finite; a program needn't handle non-finite values.
Results may differ from a plain program's by a relative error of at most 0.009.
Values may be sent and summed in bfloat16 or wider, within the bound.
No kernel may reach another device: no remote copies, remote signals or barrier semaphores. Data moves between devices by JAX's collectives and lax.ppermute only.
A program may use at most 128 MiB of HBM per device.

v0:
```python
import math

import jax
import jax.numpy as jnp
from jax import lax
from jax.sharding import PartitionSpec as P

NUMS = ("NCDHW", "OIDHW", "NCDHW")


def with_halo(block, sides, width):
    for axis, dim in sides:
        count = lax.axis_size(axis)
        forward = [(i, i + 1) for i in range(count - 1)]
        backward = [(target, source) for source, target in forward]
        low = lax.ppermute(
            lax.slice_in_dim(block, block.shape[dim] - width, None, axis=dim), axis, forward
        )
        high = lax.ppermute(lax.slice_in_dim(block, 0, width, axis=dim), axis, backward)
        block = jnp.concatenate([low, block, high], axis=dim)
    return block


def shifted(value, axis, steps):
    count = lax.axis_size(axis)
    first, last = (max(0, -steps), min(count, count - steps))
    return lax.ppermute(value, axis, [(source, source + steps) for source in range(first, last)])


def conv_first(tensor, kernel):
    return lax.conv_general_dilated(
        tensor[None],
        kernel,
        (1, 1, 1),
        ((0, 0), (0, 0), (1, 1)),
        dimension_numbers=NUMS,
        preferred_element_type=jnp.float32,
    )[0]


def conv_second(tensor, kernel):
    return lax.conv_general_dilated(
        tensor[None],
        kernel,
        (2, 2, 2),
        ((0, 0), (0, 0), (1, 0)),
        dimension_numbers=NUMS,
        preferred_element_type=jnp.float32,
    )[0]


def back_first(tensor, kernel):
    flipped = kernel[:, :, ::-1, ::-1, ::-1].transpose(1, 0, 2, 3, 4)
    return lax.conv_general_dilated(
        tensor[None],
        flipped,
        (1, 1, 1),
        ((0, 0), (0, 0), (1, 1)),
        dimension_numbers=NUMS,
        preferred_element_type=jnp.float32,
    )[0]


def back_second(grads, kernel, padding):
    flipped = kernel[:, :, ::-1, ::-1, ::-1].transpose(1, 0, 2, 3, 4)
    return lax.conv_general_dilated(
        grads[None],
        flipped,
        (1, 1, 1),
        padding,
        lhs_dilation=(2, 2, 2),
        dimension_numbers=NUMS,
        preferred_element_type=jnp.float32,
    )[0]


def kernel_first(source, grads):
    result = lax.conv_general_dilated(
        source[:, None],
        grads[:, None],
        (1, 1, 1),
        ((0, 0), (0, 0), (1, 1)),
        dimension_numbers=NUMS,
        preferred_element_type=jnp.float32,
    )
    return result.transpose(1, 0, 2, 3, 4)


def kernel_second(source, grads):
    result = lax.conv_general_dilated(
        source[:, None],
        grads[:, None],
        (1, 1, 1),
        ((0, 0), (0, 0), (1, 0)),
        rhs_dilation=(2, 2, 2),
        dimension_numbers=NUMS,
        preferred_element_type=jnp.float32,
    )
    return result.transpose(1, 0, 2, 3, 4)


def silu_slope(values):
    sigma = jax.nn.sigmoid(values)
    return sigma * (1.0 + values * (1.0 - sigma))


def shards(loaded_planes, first_kernel, first_bias, second_kernel, second_bias, cotangent):
    channels = loaded_planes.shape[0]
    planes_dev = loaded_planes.shape[2]
    tile_count = lax.axis_size("xy")
    width_x = loaded_planes.shape[4] // tile_count
    depth_y = loaded_planes.shape[5]
    depth_z = planes_dev * tile_count
    margin = 1
    stacked = loaded_planes.reshape(channels, planes_dev, tile_count, width_x, depth_y)
    regrouped = lax.all_to_all(stacked, "xy", split_axis=2, concat_axis=2, tiled=True)
    volume = regrouped.reshape(channels, depth_z, width_x, depth_y)
    extended = with_halo(volume, (("gz", 1), ("xy", 2)), margin)
    bias_one = first_bias[:, None, None, None]
    preact_full = conv_first(extended, first_kernel) + bias_one
    edge = margin - 1
    preact = preact_full[:, edge : edge + depth_z, edge : edge + width_x]
    hidden = jax.nn.silu(preact).astype(jnp.bfloat16)
    lower_rim = shifted(hidden[:, -1:], "gz", 1)
    taller = jnp.concatenate([lower_rim, hidden], 1)
    beside = shifted(taller[:, :, -1:], "xy", 1)
    framed_hidden = jnp.concatenate([beside, taller], 2)
    features = (
        conv_second(framed_hidden, second_kernel) + second_bias[:, None, None, None]
    ).astype(jnp.bfloat16)
    upper_rim = shifted(cotangent[:, :1], "gz", -1)
    deeper = jnp.concatenate([cotangent, upper_rim], 1)
    side_rim = shifted(deeper, "xy", -1)
    framed_grad = jnp.concatenate([deeper, side_rim], 2)
    raw_grad = back_second(framed_grad, second_kernel, ((1, 0), (1, 0), (1, 2)))
    hidden_grad = (raw_grad * silu_slope(preact)).astype(jnp.bfloat16)
    rimmed = with_halo(hidden_grad, (("gz", 1), ("xy", 2)), 1)
    second_term = kernel_second(framed_hidden, cotangent)
    second_bias_term = jnp.sum(cotangent.astype(jnp.float32), axis=(1, 2, 3))
    input_grad = back_first(rimmed, first_kernel).astype(jnp.bfloat16)
    first_term = kernel_first(extended, hidden_grad)
    first_bias_term = jnp.sum(hidden_grad.astype(jnp.float32), axis=(1, 2, 3))
    summed = lax.psum((first_term, first_bias_term, second_term, second_bias_term), ("gz", "xy"))
    positions = lax.axis_size("gz") * depth_z * tile_count * width_x * depth_y
    grad_scale = 1.0 / math.sqrt(positions)
    return (
        features,
        input_grad,
        summed[0] * grad_scale,
        summed[1] * grad_scale,
        summed[2] * grad_scale,
        summed[3] * grad_scale,
    )


def solution(mesh):
    return jax.shard_map(
        shards,
        mesh=mesh,
        in_specs=(
            P(None, "gz", None, "xy", None, None),
            P(),
            P(),
            P(),
            P(),
            P(None, "gz", "xy", None),
        ),
        out_specs=(P(None, "gz", "xy", None), P(None, "gz", "xy", None), P(), P(), P(), P()),
        check_vma=False,
    )
```

profile of v0, /device:TPU:1, one launch (start us, length us, event | category | flops | bytes accessed | tf_op | source)
XLA Modules:
  0.0 500.6 jit_solution(14795127235032250812)
XLA Ops:
  1.6 8.8 %collective-permute-start.6 = (bf16[32,1,1,64]{3,1,2,0:T(2,128)(2,1)S(1)}, bf16[32,1,1,64]{3,1,2,0:T(2,128)(2,1)S(1)}, u32[]{:S(2)}, u32[]{:S(2)}) collective-permute-start(bf16[32,1,1,64]{3,1,2,0:T(2,128)(2,1)S(1)} %slice.39), channel_id=1, source_target_pairs={{32,0},{64,32},{96,64},{128,96},{160,128},{192,160},{224,192},{256... | collective-permute-start | bytes 12296 | tf_op jit(solution)/shard_map/ppermute | solution.py:27
  10.4 1.5 copy.128
  11.9 10.3 %all-to-all-start = ((bf16[4,1,32,2,128]{4,3,0,1,2:T(2,128)(2,1)}), bf16[4,1,32,2,128]{4,3,0,1,2:T(2,128)(2,1)S(1)}, u32[]{:S(2)}, u32[]{:S(2)}) async-start(bf16[4,1,32,2,128]{4,3,0,1,2:T(2,128)(2,1)} %copy.128), calls=%async_computation | async-start | bytes 131072 | tf_op jit(solution)/shard_map/all_to_all | solution.py:116
  22.2 1.7 convert_reduce_fusion.1
  23.9 0.9 constant_dynamic-update-slice_fusion.2
  24.8 2.1 copy.161
  27.0 1.3 collective-permute-start.7
  28.3 5.4 %all-to-all-done = bf16[4,1,32,2,128]{4,3,0,1,2:T(2,128)(2,1)S(1)} async-done(((bf16[4,1,32,2,128]{4,3,0,1,2:T(2,128)(2,1)}), bf16[4,1,32,2,128]{4,3,0,1,2:T(2,128)(2,1)S(1)}, u32[]{:S(2)}, u32[]{:S(2)}) %all-to-all-start) | async-done | bytes 65568 | tf_op jit(solution)/shard_map/all_to_all | solution.py:116
  33.6 4.3 collective-permute-start
  37.9 1.9 collective-permute-start.1
  40.0 0.9 copy.169
  41.6 1.2 collective-permute-done.1
  43.0 2.6 collective-permute-start.2
  45.6 1.5 collective-permute-start.3
  47.2 3.8 broadcast_select_fusion
  51.0 4.2 copy.143
  55.2 1.5 slice.63
  56.7 2.5 copy.167
  60.1 6.3 %copy.131 = bf16[4,34,4,1,8,17]{4,0,5,2,1,3:T(4,128)(2,1)} copy(bf16[4,34,4,1,8,17]{1,2,5,4,0,3:T(4,128)(2,1)S(1)} %bitcast.107) | data formatting | bytes 295936 | tf_op jit(solution)/shard_map/conv_general_dilated | solution.py:31
  66.4 1.2 slice.56
  67.6 12.1 %broadcast_select_fusion.1 = f32[32,2,8,17,16]{4,2,3,1,0:T(8,128)} fusion(pred[8,17]{0,1:T(8,128)(4,1)S(1)} %copy-done.5, bf16[16,4,3,3,3]{0,1,4,3,2:T(4,128)(2,1)S(1)} %copy-done.11, bf16[4,34,4,1,7,2]{4,0,5,2,1,3:T(4,128)(2,1)S(1)} %slice.56, bf16[4,34,4,1,8,17]{4,0,5,2,1,3:T(4,128)(2,1)} %copy.131), kind=kOutput, calls=%fused_computation.20 | convolution fusion | flops 30716416 | bytes 723848 | tf_op jit(solution)/shard_map/conv_general_dilated | solution.py:31
  79.7 4.3 copy.132
  84.0 1.5 slice.57
  85.4 2.5 copy.166
  88.2 1.0 convert_reduce_fusion
  89.2 2.7 collective-permute-start.4
  92.0 2.7 collective-permute-start.8
  94.7 2.3 collective-permute-start.9
  97.1 4.7 copy.159
  102.0 15.5 %copy.158 = bf16[4,1,34,4,128]{0,1,4,3,2:T(2,128)(2,1)} copy(bf16[4,1,34,4,128]{4,3,0,2,1:T(4,128)(2,1)S(1)} %fusion.69) | data formatting | bytes 278528 | tf_op jit(solution)/shard_map/broadcast_in_dim | solution.py:79
  117.4 62.4 %fusion.59 = f32[16,4,3,3,3]{0,1,4,3,2:T(4,128)S(1)} fusion(bf16[4,1,34,4,128]{0,1,4,3,2:T(2,128)(2,1)} %copy.158, bf16[16,1,32,2,128]{0,1,4,3,2:T(2,128)(2,1)} %copy.159), kind=kOutput, calls=%fused_computation.86 | convolution fusion | flops 28164096 | bytes 408320 | tf_op jit(solution)/shard_map/transpose | solution.py:86
  180.1 4.0 collective-permute-start.5
  185.1 2.7 collective-permute-start.10
  187.8 1.5 collective-permute-start.11
  190.1 1.2 copy.136
  191.7 4.7 copy.138
  196.4 1.1 slice.60
  197.6 4.2 fusion.24
  202.0 1.0 copy.162
  202.9 10.4 %copy.160 = bf16[16,1,33,3,128]{0,1,4,3,2:T(2,128)(2,1)} copy(bf16[16,1,33,3,128]{4,0,3,2,1:T(8,128)(2,1)S(1)} %copy-done.1) | data formatting | bytes 811008 | tf_op jit(solution)/shard_map/broadcast_in_dim | solution.py:91
  213.4 15.3 %fusion.60 = f32[32,16,3,3,3]{0,1,4,3,2:T(8,128)S(1)} fusion(bf16[16,1,33,3,128]{0,1,4,3,2:T(2,128)(2,1)} %copy.160, bf16[32,1,16,1,64]{0,1,4,3,2:T(2,128)(2,1)S(1)} %copy-done.4), kind=kOutput, calls=%fused_computation.87 | convolution fusion | flops 28164096 | bytes 526336 | tf_op jit(solution)/shard_map/transpose | solution.py:99
  228.7 111.6 %all-reduce = (f32[16,4,3,3,3]{0,1,4,3,2:T(4,128)S(1)}, f32[16]{0:T(128)S(1)}, f32[32,16,3,3,3]{0,1,4,3,2:T(8,128)S(1)}, f32[32]{0:T(128)S(1)}) all-reduce(f32[16,4,3,3,3]{0,1,4,3,2:T(4,128)S(1)} %fusion.59, f32[16]{0:T(128)S(1)} %copy-done.9, f32[32,16,3,3,3]{0,1,4,3,2:T(8,128)S(1)} %fusion.60, ...), channel_id=1, replica_groups=mesh['gz'=16,'xy'=32] {'gz','xy'}, use_global_device_ids=true, to_apply=%region_0.1 | all-reduce | flops 15600 | bytes 124800 | tf_op jit(solution)/shard_map/psum | solution.py:143
  342.7 1.1 pad_maximum_fusion
  343.7 2.8 copy.148
  346.6 2.0 pad.6
  348.6 10.1 %copy.150 = bf16[16,34,4,1,8,17]{0,4,5,2,1,3:T(8,128)(2,1)} copy(bf16[16,34,4,1,8,17]{1,0,5,4,2,3:T(8,128)(2,1)S(1)} %bitcast.100) | data formatting | bytes 1183744 | tf_op jit(solution)/shard_map/conv_general_dilated | solution.py:54
  358.6 1.2 slice.68
  359.9 138.6 %fusion.4 = bf16[32,2,8,17,4]{2,4,3,1,0:T(4,128)(2,1)S(1)} fusion(bf16[16,4,3,3,3]{0,1,4,3,2:T(4,128)(2,1)S(1)} %copy-done.12, bf16[16,34,4,1,7,2]{0,4,5,2,1,3:T(8,128)(2,1)S(1)} %slice.68, bf16[16,34,4,1,8,17]{0,4,5,2,1,3:T(8,128)(2,1)} %copy.150), kind=kOutput, calls=%fused_computation.6 | convolution fusion | flops 32065536 | bytes 725888 | tf_op jit(solution)/shard_map/conv_general_dilated | solution.py:54
  (80 shorter events, 10.0 us)
Async XLA Ops:
  0.6 46.5 %copy-start = (bf16[32,16,3,3,3]{0,1,4,3,2:T(8,128)(2,1)S(1)}, bf16[32,16,3,3,3]{0,1,4,3,2:T(8,128)(2,1)}, u32[]{:S(2)}) copy-start(bf16[32,16,3,3,3]{0,1,4,3,2:T(8,128)(2,1)} %param.9) | copy-start | bytes 82948
  0.6 46.5 %copy-start.13 = (pred[8,18]{0,1:T(8,128)(4,1)S(1)}, pred[8,18]{0,1:T(8,128)(4,1)}, u32[]{:S(2)}) copy-start(pred[8,18]{0,1:T(8,128)(4,1)} %constant.32) | copy-start | bytes 436
  1.6 25.4 %collective-permute-start.6 = (bf16[32,1,1,64]{3,1,2,0:T(2,128)(2,1)S(1)}, bf16[32,1,1,64]{3,1,2,0:T(2,128)(2,1)S(1)}, u32[]{:S(2)}, u32[]{:S(2)}) collective-permute-start(bf16[32,1,1,64]{3,1,2,0:T(2,128)(2,1)S(1)} %slice.39), channel_id=1, source_target_pairs={{32,0},{64,32},{96,64},{128,96},{160,128},{192,160},{224,192},{256... | collective-permute-start | bytes 12296 | tf_op jit(solution)/shard_map/ppermute | solution.py:27
  11.9 21.8 %all-to-all-start = ((bf16[4,1,32,2,128]{4,3,0,1,2:T(2,128)(2,1)}), bf16[4,1,32,2,128]{4,3,0,1,2:T(2,128)(2,1)S(1)}, u32[]{:S(2)}, u32[]{:S(2)}) async-start(bf16[4,1,32,2,128]{4,3,0,1,2:T(2,128)(2,1)} %copy.128), calls=%async_computation | async-start | bytes 131072 | tf_op jit(solution)/shard_map/all_to_all | solution.py:116
  27.0 12.9 %collective-permute-start.7 = (bf16[32,17,1,64]{3,1,2,0:T(8,128)(2,1)S(1)}, bf16[32,17,1,64]{3,1,2,0:T(8,128)(2,1)S(1)}, u32[]{:S(2)}, u32[]{:S(2)}) collective-permute-start(bf16[32,17,1,64]{3,1,2,0:T(8,128)(2,1)S(1)} %constant_dynamic-update-slice_fusion.1), channel_id=1, source_target_pairs={{1,0},{2,1},{3,2},{4,3},{5,4},{6,5},{7,6},{8,7},{9,8},{10,9},{11,1... | collective-permute-start | bytes 208904 | tf_op jit(solution)/shard_map/ppermute | solution.py:27
  33.6 7.9 %collective-permute-start = (bf16[4,1,2,128]{3,2,0,1:T(2,128)(2,1)S(1)}, bf16[4,1,2,128]{3,2,0,1:T(2,128)(2,1)S(1)}, u32[]{:S(2)}, u32[]{:S(2)}) collective-permute-start(bf16[4,1,2,128]{3,2,0,1:T(2,128)(2,1)S(1)} %get-tuple-element.51), channel_id=1, source_target_pairs={{0,32},{32,64},{64,96},{96,128},{128,160},{160,192},{192,224},{224... | collective-permute-start | bytes 6152 | tf_op jit(solution)/shard_map/ppermute | solution.py:16
  37.9 4.9 collective-permute-start.1
  43.0 16.2 %collective-permute-start.2 = (bf16[4,34,1,128]{3,2,0,1:T(2,128)(2,1)S(1)}, bf16[4,34,1,128]{3,2,0,1:T(2,128)(2,1)S(1)}, u32[]{:S(2)}, u32[]{:S(2)}) collective-permute-start(bf16[4,34,1,128]{3,2,0,1:T(2,128)(2,1)S(1)} %get-tuple-element.49), channel_id=1, source_target_pairs={{0,1},{1,2},{2,3},{3,4},{4,5},{5,6},{6,7},{7,8},{8,9},{9,10},{10,1... | collective-permute-start | bytes 104456 | tf_op jit(solution)/shard_map/ppermute | solution.py:16
  45.6 13.6 %collective-permute-start.3 = (bf16[4,34,1,128]{3,2,0,1:T(2,128)(2,1)S(1)}, bf16[4,34,1,128]{3,2,0,1:T(2,128)(2,1)S(1)}, u32[]{:S(2)}, u32[]{:S(2)}) collective-permute-start(bf16[4,34,1,128]{3,2,0,1:T(2,128)(2,1)S(1)} %get-tuple-element.50), channel_id=1, source_target_pairs={{1,0},{2,1},{3,2},{4,3},{5,4},{6,5},{7,6},{8,7},{9,8},{10,9},{11,1... | collective-permute-start | bytes 104456 | tf_op jit(solution)/shard_map/ppermute | solution.py:19
  56.7 10.9 %copy-start.5 = (pred[8,17]{0,1:T(8,128)(4,1)S(1)}, pred[8,17]{0,1:T(8,128)(4,1)}, u32[]{:S(2)}) copy-start(pred[8,17]{0,1:T(8,128)(4,1)} %constant.30) | copy-start | bytes 412
  56.7 10.9 %copy-start.11 = (bf16[16,4,3,3,3]{0,1,4,3,2:T(4,128)(2,1)S(1)}, bf16[16,4,3,3,3]{0,1,4,3,2:T(4,128)(2,1)}, u32[]{:S(2)}) copy-start(bf16[16,4,3,3,3]{0,1,4,3,2:T(4,128)(2,1)} %param.7) | copy-start | bytes 10372
  84.0 4.0 copy-start.7
  89.2 90.6 %collective-permute-start.4 = (bf16[16,1,2,128]{3,0,2,1:T(8,128)(2,1)S(1)}, bf16[16,1,2,128]{3,0,2,1:T(8,128)(2,1)S(1)}, u32[]{:S(2)}, u32[]{:S(2)}) collective-permute-start(bf16[16,1,2,128]{3,0,2,1:T(8,128)(2,1)S(1)} %copy.134), channel_id=1, source_target_pairs={{0,32},{32,64},{64,96},{96,128},{128,160},{160,192},{192,224},{224... | collective-permute-start | bytes 24584 | tf_op jit(solution)/shard_map/ppermute | solution.py:27
  92.0 92.1 %collective-permute-start.8 = (bf16[16,1,2,128]{3,0,2,1:T(8,128)(2,1)S(1)}, bf16[16,1,2,128]{3,0,2,1:T(8,128)(2,1)S(1)}, u32[]{:S(2)}, u32[]{:S(2)}) collective-permute-start(bf16[16,1,2,128]{3,0,2,1:T(8,128)(2,1)S(1)} %copy.145), channel_id=1, source_target_pairs={{0,32},{32,64},{64,96},{96,128},{128,160},{160,192},{192,224},{224... | collective-permute-start | bytes 24584 | tf_op jit(solution)/shard_map/ppermute | solution.py:16
  94.7 89.6 %collective-permute-start.9 = (bf16[16,1,2,128]{3,0,2,1:T(8,128)(2,1)S(1)}, bf16[16,1,2,128]{3,0,2,1:T(8,128)(2,1)S(1)}, u32[]{:S(2)}, u32[]{:S(2)}) collective-permute-start(bf16[16,1,2,128]{3,0,2,1:T(8,128)(2,1)S(1)} %copy.146), channel_id=1, source_target_pairs={{32,0},{64,32},{96,64},{128,96},{160,128},{192,160},{224,192},{256... | collective-permute-start | bytes 24584 | tf_op jit(solution)/shard_map/ppermute | solution.py:19
  180.1 9.2 %collective-permute-start.5 = (bf16[16,33,1,128]{3,0,2,1:T(8,128)(2,1)S(1)}, bf16[16,33,1,128]{3,0,2,1:T(8,128)(2,1)S(1)}, u32[]{:S(2)}, u32[]{:S(2)}) collective-permute-start(bf16[16,33,1,128]{3,0,2,1:T(8,128)(2,1)S(1)} %slice.59), channel_id=1, source_target_pairs={{0,1},{1,2},{2,3},{3,4},{4,5},{5,6},{6,7},{7,8},{8,9},{9,10},{10,1... | collective-permute-start | bytes 405512 | tf_op jit(solution)/shard_map/ppermute | solution.py:27
  184.3 5.0 copy-start.2
  185.1 157.6 %collective-permute-start.10 = (bf16[16,34,1,128]{3,0,2,1:T(8,128)(2,1)}, bf16[16,34,1,128]{3,0,2,1:T(8,128)(2,1)}, u32[]{:S(2)}, u32[]{:S(2)}) collective-permute-start(bf16[16,34,1,128]{3,0,2,1:T(8,128)(2,1)} %get-tuple-element.45), channel_id=1, source_target_pairs={{0,1},{1,2},{2,3},{3,4},{4,5},{5,6},{6,7},{7,8},{8,9},{9,10},{10,1... | collective-permute-start | bytes 417800 | tf_op jit(solution)/shard_map/ppermute | solution.py:16
  187.8 154.9 %collective-permute-start.11 = (bf16[16,34,1,128]{3,0,2,1:T(8,128)(2,1)}, bf16[16,34,1,128]{3,0,2,1:T(8,128)(2,1)}, u32[]{:S(2)}, u32[]{:S(2)}) collective-permute-start(bf16[16,34,1,128]{3,0,2,1:T(8,128)(2,1)} %get-tuple-element.46), channel_id=1, source_target_pairs={{1,0},{2,1},{3,2},{4,3},{5,4},{6,5},{7,6},{8,7},{9,8},{10,9},{11,1... | collective-permute-start | bytes 417800 | tf_op jit(solution)/shard_map/ppermute | solution.py:19
  191.3 6.2 %copy-start.14 = (pred[8,9]{0,1:T(8,128)(4,1)S(1)}, pred[8,9]{0,1:T(8,128)(4,1)}, u32[]{:S(2)}) copy-start(pred[8,9]{0,1:T(8,128)(4,1)} %constant.29) | copy-start | bytes 220
  197.5 4.4 copy-start.10
  197.6 5.4 %copy-start.1 = (bf16[16,1,33,3,128]{4,0,3,2,1:T(8,128)(2,1)S(1)}, bf16[16,1,33,3,128]{4,0,3,2,1:T(8,128)(2,1)}, u32[]{:S(2)}) copy-start(bf16[16,1,33,3,128]{4,0,3,2,1:T(8,128)(2,1)} %get-tuple-element.43) | copy-start | bytes 1216516
  201.9 11.5 %copy-start.4 = (bf16[32,1,16,1,64]{0,1,4,3,2:T(2,128)(2,1)S(1)}, bf16[32,1,16,1,64]{0,1,4,3,2:T(2,128)(2,1)}, u32[]{:S(2)}) copy-start(bf16[32,1,16,1,64]{0,1,4,3,2:T(2,128)(2,1)} %copy.161) | copy-start | bytes 196612
  213.4 15.4 %copy-start.8 = (f32[32]{0:T(128)S(1)}, f32[32]{0:T(128)}, u32[]{:S(2)}) copy-start(f32[32]{0:T(128)} %convert_reduce_fusion.1) | copy-start | bytes 388
  213.4 15.4 %copy-start.9 = (f32[16]{0:T(128)S(1)}, f32[16]{0:T(128)}, u32[]{:S(2)}) copy-start(f32[16]{0:T(128)} %get-tuple-element.40) | copy-start | bytes 196
  213.4 129.3 %copy-start.3 = (bf16[16,34,2,128]{3,0,2,1:T(8,128)(2,1)S(1)}, bf16[16,34,2,128]{3,0,2,1:T(8,128)(2,1)}, u32[]{:S(2)}) copy-start(bf16[16,34,2,128]{3,0,2,1:T(8,128)(2,1)} %copy-done.2) | copy-start | bytes 835588
  348.6 11.3 %copy-start.12 = (bf16[16,4,3,3,3]{0,1,4,3,2:T(4,128)(2,1)S(1)}, bf16[16,4,3,3,3]{0,1,4,3,2:T(4,128)(2,1)}, u32[]{:S(2)}) copy-start(bf16[16,4,3,3,3]{0,1,4,3,2:T(4,128)(2,1)} %param.7) | copy-start | bytes 10372
  359.9 139.2 %copy-start.6 = (pred[8,17]{0,1:T(8,128)(4,1)S(1)}, pred[8,17]{0,1:T(8,128)(4,1)}, u32[]{:S(2)}) copy-start(pred[8,17]{0,1:T(8,128)(4,1)} %constant.30) | copy-start | bytes 412
where the time goes:
time: 504 us; the launch traced here: 501 us
  matrix products  236 us (47%)
  blocking collectives  112 us (22%)
  local copies, waits for them, and re-layouts  89.8 us (18%)
  starting transfers between devices  46.6 us (9%)
  other arithmetic  8.05 us (2%)
  waiting for transfers between devices  6.64 us (1%)
    conv_general_dilated x1, matrix products, back_first(): lax.conv_general_dilated(tensor[None], flipped, (1, 1, 1), ((0, 0), (0, 0...  139 us
    psum x1, blocking collectives, shards(): lax.psum((first_term, first_bias_term, second_term, second_bias_term), ('...  112 us
    transpose x1, matrix products, kernel_first(): return result.transpose(1, 0, 2, 3, 4)  62.4 us
    ppermute x4, starting transfers between devices, shifted(): lax.ppermute(value, axis, [(source, source + steps) for source in range(f...  16.8 us
    broadcast_in_dim x1, local copies, waits for them, and re-layouts, kernel_first(): source[:, None]  15.5 us
    transpose x1, matrix products, kernel_second(): return result.transpose(1, 0, 2, 3, 4)  15.3 us
    conv_general_dilated x4, local copies, waits for them, and re-layouts, conv_first(): lax.conv_general_dilated(tensor[None], kernel, (1, 1, 1), ((0, 0), (0, 0)...  13.2 us
    ppermute x4, starting transfers between devices, with_halo(): lax.ppermute(lax.slice_in_dim(block, block.shape[dim] - width, None, axis...  12.3 us
  transfers between devices with their start and end apart: 13, of which 2 were waited for; matrix products, arithmetic and copies ran while one was open for 29% of the time, Pallas kernels for 0%

commit v1 on v0

v1 whole, which is shorter than its diff:
```python
import functools
import math

import jax
import jax.numpy as jnp
import numpy as np
from jax import lax
from jax.experimental import pallas as pl
from jax.experimental.pallas import tpu as pltpu
from jax.sharding import PartitionSpec as P

BF16 = jnp.bfloat16
F32 = jnp.float32
WINDOW = 8
COLUMNS = 4
VMEM_LIMIT = 48 * 1024 * 1024


def shifted(value, axis, steps):
    count = lax.axis_size(axis)
    first, last = (max(0, -steps), min(count, count - steps))
    return lax.ppermute(value, axis, [(source, source + steps) for source in range(first, last)])


def mm(left, right):
    return jnp.dot(left, right, preferred_element_type=F32)


def mm_nt(left, right):
    return lax.dot_general(left, right, (((1,), (1,)), ((), ())), preferred_element_type=F32)


def from_left(value):
    lane = lax.broadcasted_iota(jnp.int32, value.shape, 1)
    return jnp.where(lane == 0, 0.0, pltpu.roll(value, 1, 1))


def from_right(value):
    lane = lax.broadcasted_iota(jnp.int32, value.shape, 1)
    last = value.shape[1] - 1
    return jnp.where(lane == last, 0.0, pltpu.roll(value, last, 1))


def pack_kernel(planes_ref, out_ref, wide_ref):
    channels, width, _ = planes_ref.shape
    wide_ref[...] = jnp.zeros_like(wide_ref)
    wide_ref[:, 8 : 8 + width, :] = planes_ref[...].astype(F32)
    targets = out_ref.shape[0]
    row = lax.broadcasted_iota(jnp.int32, (WINDOW, out_ref.shape[2]), 0)
    for t in range(targets):
        parts = [wide_ref[i, 6 + 2 * t : 6 + 2 * t + WINDOW, :] for i in range(channels)]
        parts = [jnp.where(row >= WINDOW - 2, 1.0, part) for part in parts]
        out_ref[t] = jnp.concatenate(parts, axis=0).astype(BF16)


def pack(planes, targets):
    channels, width, depth_y = planes.shape
    shape = (targets, channels * WINDOW, depth_y)
    return pl.pallas_call(
        pack_kernel,
        out_shape=jax.ShapeDtypeStruct(shape, BF16),
        scratch_shapes=[pltpu.VMEM((channels, width + 16, depth_y), F32)],
        compiler_params=pltpu.CompilerParams(vmem_limit_bytes=VMEM_LIMIT),
        name="pack_windows",
    )(planes)


def prep_kernel(left_ref, mid_ref, right_ref, odd_ref, even_ref, raw_ref, shifts_ref, wide_ref):
    levels, ch2, half_y = mid_ref.shape
    rows = 3 * ch2
    depth_y = 2 * half_y
    spread = (
        2 * lax.broadcasted_iota(jnp.int32, (half_y, depth_y), 0)
        == lax.broadcasted_iota(jnp.int32, (half_y, depth_y), 1)
    ).astype(F32).astype(BF16)
    for q in range(levels):
        block = jnp.concatenate([left_ref[q], mid_ref[q], right_ref[q]], axis=0)
        wide = mm(block, spread)
        wide_ref[pl.ds(q * rows, rows), :] = wide.astype(BF16)
        if 0 < q < levels - 1:
            own = wide[ch2 : 2 * ch2]
            base = (q - 1) * rows
            shifts_ref[pl.ds(base, ch2), :] = from_right(own).astype(BF16)
            shifts_ref[pl.ds(base + ch2, ch2), :] = own.astype(BF16)
            shifts_ref[pl.ds(base + 2 * ch2, ch2), :] = from_left(own).astype(BF16)
    size = raw_ref.shape[0] // (2 * (levels - 1))

    def combine(terms):
        return from_right(terms[:size]) + terms[size : 2 * size] + from_left(terms[2 * size :])

    def level(m, _):
        base = pl.multiple_of(m * rows, rows)
        odd = mm(odd_ref[...], wide_ref[pl.ds(base, 2 * rows), :])
        out = pl.multiple_of(m * 2 * size, 2 * size)
        raw_ref[pl.ds(out, size), :] = combine(odd)
        even = mm(even_ref[...], wide_ref[pl.ds(base + rows, rows), :])
        raw_ref[pl.ds(out + size, size), :] = combine(even)
        return 0

    lax.fori_loop(0, levels - 1, level, 0)


def prep(left, mid, right, odd, even, ch1):
    levels, ch2, half_y = mid.shape
    depth_y = 2 * half_y
    return pl.pallas_call(
        prep_kernel,
        out_shape=(
            jax.ShapeDtypeStruct((2 * (levels - 1) * COLUMNS * ch1, depth_y), F32),
            jax.ShapeDtypeStruct(((levels - 2) * 3 * ch2, depth_y), BF16),
        ),
        scratch_shapes=[pltpu.VMEM((levels * 3 * ch2, depth_y), BF16)],
        compiler_params=pltpu.CompilerParams(vmem_limit_bytes=VMEM_LIMIT),
        name="spread_cotangent",
    )(left, mid, right, odd, even)


def main_kernel(
    place_ref,
    low_ref,
    mid_ref,
    high_ref,
    raw_ref,
    shifts_ref,
    w1_ref,
    b1_ref,
    hidden_ref,
    grad_ref,
    sums_ref,
    vol_ref,
    *,
    ch1,
    ch2,
):
    depth_z, rows, depth_y = mid_ref.shape
    size = COLUMNS * ch1
    vol_ref[pl.ds(0, 2 * rows), :] = low_ref[...].reshape(2 * rows, depth_y)
    vol_ref[pl.ds(2 * rows, depth_z * rows), :] = mid_ref[...].reshape(depth_z * rows, depth_y)
    vol_ref[pl.ds((depth_z + 2) * rows, 2 * rows), :] = high_ref[...].reshape(2 * rows, depth_y)
    at_first_z, at_last_z, at_first_x, at_last_x = (place_ref[k] for k in range(4))
    row = lax.broadcasted_iota(jnp.int32, (size, depth_y), 0)
    outside = ((row < ch1) & (at_first_x != 0)) | ((row >= 3 * ch1) & (at_last_x != 0))
    bias = jnp.broadcast_to(b1_ref[...], (size, depth_y))

    def level(z, _):
        base = pl.multiple_of(z * rows, rows)
        terms = mm(w1_ref[...], vol_ref[pl.ds(base, 3 * rows), :])
        pre = from_left(terms[:size]) + terms[size : 2 * size] + from_right(terms[2 * size :]) + bias
        sigma = 1.0 / (1.0 + jnp.exp(-pre))
        gone = ((z == 0) & (at_first_z != 0)) | ((z == depth_z + 1) & (at_last_z != 0))
        drop = outside | gone
        hidden = jnp.where(drop, 0.0, pre * sigma)
        out = pl.multiple_of(z * size, size)
        raw = raw_ref[pl.ds(out, size), :]
        grad = jnp.where(drop, 0.0, raw * (sigma * (1.0 + pre * (1.0 - sigma))))
        hidden_ref[pl.ds(out, size), :] = jnp.where(row >= 3 * ch1, 1.0, hidden).astype(BF16)
        grad_ref[pl.ds(out, size), :] = grad.astype(BF16)
        return 0

    lax.fori_loop(0, depth_z + 2, level, 0)

    def first(z, total):
        out = pl.multiple_of((z + 1) * size, size)
        own = grad_ref[pl.ds(out + ch1, 2 * ch1), :].astype(F32)
        parts = [from_right(own), own, from_left(own)]
        sides = [part[x * ch1 : (x + 1) * ch1] for x in range(2) for part in parts]
        moved = jnp.concatenate(sides, axis=0).astype(BF16)
        base = pl.multiple_of((z + 1) * rows, rows)
        return total + mm_nt(vol_ref[pl.ds(base, 3 * rows), :], moved)

    first_sum = lax.fori_loop(0, depth_z, first, jnp.zeros((3 * rows, 6 * ch1), F32))

    def second(q, total):
        base = pl.multiple_of(q * 2 * size, 2 * size)
        own = pl.multiple_of(q * 3 * ch2, 3 * ch2)
        return total + mm_nt(hidden_ref[pl.ds(base, 3 * size), :], shifts_ref[pl.ds(own, 3 * ch2), :])

    second_sum = lax.fori_loop(0, depth_z // 2, second, jnp.zeros((3 * size, 3 * ch2), F32))
    folded = first_sum[:, : 3 * ch1] + pltpu.roll(first_sum, 3 * rows - 1, 0)[:, 3 * ch1 :]
    sums_ref[:, : 3 * ch2] = second_sum
    sums_ref[: 3 * rows, 3 * ch2 : 3 * ch2 + ch1] = folded[:, :ch1]
    sums_ref[: 3 * rows, 3 * ch2 + ch1 :] = folded[:, ch1 : 2 * ch1]
    sums_ref[3 * rows :, 3 * ch2 : 3 * ch2 + ch1] = folded[:, 2 * ch1 :]
    sums_ref[3 * rows :, 3 * ch2 + ch1 :] = jnp.zeros((3 * size - 3 * rows, ch1), F32)


def main(place, low, mid, high, raw, shifts, w1, b1, ch1, ch2):
    depth_z, rows, depth_y = mid.shape
    size = COLUMNS * ch1
    vmem = pl.BlockSpec(memory_space=pltpu.VMEM)
    return pl.pallas_call(
        functools.partial(main_kernel, ch1=ch1, ch2=ch2),
        in_specs=[pl.BlockSpec(memory_space=pltpu.SMEM)] + [vmem] * 7,
        out_specs=(vmem, vmem, vmem),
        out_shape=(
            jax.ShapeDtypeStruct(((depth_z + 2) * size, depth_y), BF16),
            jax.ShapeDtypeStruct(((depth_z + 2) * size, depth_y), BF16),
            jax.ShapeDtypeStruct((3 * size, 128), F32),
        ),
        scratch_shapes=[pltpu.VMEM(((depth_z + 4) * rows, depth_y), BF16)],
        compiler_params=pltpu.CompilerParams(vmem_limit_bytes=VMEM_LIMIT),
        name="hidden_and_sums",
    )(place, low, mid, high, raw, shifts, w1, b1)


def last_kernel(hidden_ref, grad_ref, w2_ref, b2_ref, w4_ref, feat_ref, gin_ref, featw_ref, ginw_ref):
    ch2, depth_q, half_y = feat_ref.shape
    c_in, _, depth_y = gin_ref.shape
    size = hidden_ref.shape[0] // (2 * depth_q + 2)
    bias = jnp.broadcast_to(b2_ref[...], (ch2, depth_y))
    pick = (
        lax.broadcasted_iota(jnp.int32, (depth_y, half_y), 0)
        == 2 * lax.broadcasted_iota(jnp.int32, (depth_y, half_y), 1)
    ).astype(F32).astype(BF16)

    for q in range(depth_q):
        base = q * 2 * size
        terms = mm(w2_ref[...], hidden_ref[pl.ds(base, 3 * size), :])
        full = from_left(terms[:ch2]) + terms[ch2 : 2 * ch2] + from_right(terms[2 * ch2 :]) + bias
        featw_ref[pl.ds(q, ch2, stride=depth_q), :] = mm(full.astype(BF16), pick)
    feat_ref[...] = featw_ref[...].reshape(feat_ref.shape).astype(BF16)

    two = 2 * c_in
    for z in range(2 * depth_q):
        base = z * size
        terms = mm(w4_ref[...], grad_ref[pl.ds(base, 3 * size), :])
        full = from_right(terms[:two]) + terms[two : 2 * two] + from_left(terms[2 * two :])
        for x in range(2):
            ginw_ref[pl.ds(2 * z + x, c_in, stride=4 * depth_q), :] = full[x * c_in : (x + 1) * c_in]
    gin_ref[...] = ginw_ref[...].reshape(gin_ref.shape).astype(BF16)


def last(hidden, grad, w2, b2, w4, c_in, ch2):
    depth_y = hidden.shape[1]
    ch1 = w2.shape[1] // (3 * COLUMNS)
    depth_z = hidden.shape[0] // (COLUMNS * ch1) - 2
    depth_q = depth_z // 2
    return pl.pallas_call(
        last_kernel,
        out_shape=(
            jax.ShapeDtypeStruct((ch2, depth_q, depth_y // 2), BF16),
            jax.ShapeDtypeStruct((c_in, 2 * depth_z, depth_y), BF16),
        ),
        scratch_shapes=[
            pltpu.VMEM((ch2 * depth_q, depth_y // 2), F32),
            pltpu.VMEM((c_in * 2 * depth_z, depth_y), F32),
        ],
        compiler_params=pltpu.CompilerParams(vmem_limit_bytes=VMEM_LIMIT),
        name="features_and_input_grad",
    )(hidden, grad, w2, b2, w4)


def unpack_kernel(sums_ref, first_ref, second_ref, bias1_ref, bias2_ref, *, scale):
    _, c_in, ch1 = first_ref.shape
    ch2 = second_ref.shape[2]
    rows = 3 * c_in * WINDOW
    size = COLUMNS * ch1
    at = 3 * ch2
    corners = ((0, at), (0, at + ch1), (rows, at))
    for a in range(3):
        for b in range(3):
            for c in range(3):
                k = 9 * a + 3 * b + c
                block = sums_ref[a * size + b * ch1 : a * size + (b + 1) * ch1, c * ch2 : (c + 1) * ch2]
                second_ref[k] = block * scale
                down, right = corners[c]
                base = down + a * c_in * WINDOW + b + 1
                block = sums_ref[pl.ds(base, c_in, stride=WINDOW), :]
                first_ref[k] = block[:, right : right + ch1] * scale
    bias2_ref[...] = sums_ref[size + 3 * ch1 : size + 3 * ch1 + 1, ch2 : 2 * ch2] * scale
    down, right = corners[1]
    base = down + c_in * WINDOW + WINDOW - 2
    bias1_ref[...] = sums_ref[base : base + 1, right : right + ch1] * scale


def unpack(sums, scale, c_in, ch1, ch2):
    first, bias1, second, bias2 = (
        jax.ShapeDtypeStruct(shape, F32) for shape in ((27, c_in, ch1), (1, ch1), (27, ch1, ch2), (1, ch2))
    )
    first, second, bias1, bias2 = pl.pallas_call(
        functools.partial(unpack_kernel, scale=scale),
        out_shape=(first, second, bias1, bias2),
        name="unpack_sums",
    )(sums)
    first = first.reshape(3, 3, 3, c_in, ch1).transpose(4, 3, 0, 1, 2)
    second = second.reshape(3, 3, 3, ch1, ch2).transpose(4, 3, 0, 1, 2)
    return first, bias1[0], second, bias2[0]


def total_over_devices(sums):
    slabs, tiles = lax.axis_size("gz"), lax.axis_size("xy")
    near, row = slabs // 2, tiles // 4
    far, cols = slabs // near, tiles // row
    both = ("gz", "xy")
    near_groups = [[f * near + k for k in range(near)] for f in range(far)]
    far_groups = [
        [(f * near + k) * tiles + c * row + r for c in range(cols) for f in range(far)]
        for k in range(near)
        for r in range(row)
    ]
    row_groups = [[c * row + r for r in range(row)] for c in range(cols)]

    def exchange(value, axis, groups):
        return lax.all_to_all(value, axis, 0, 0, tiled=True, axis_index_groups=groups)

    def spread(value, axis, groups):
        count = len(groups[0])
        return exchange(jnp.broadcast_to(value[None], (count,) + value.shape), axis, groups)

    part = exchange(sums.reshape(near, -1, sums.shape[1]), "gz", near_groups).sum(0)
    part = spread(part, both, far_groups).sum(0)
    part = spread(part, "xy", row_groups).sum(0)
    return spread(part, "gz", near_groups).reshape(sums.shape)


def one_hot(shape, test):
    return jnp.asarray(np.fromfunction(np.vectorize(test), shape, dtype=int).astype(np.float32)).astype(BF16)


def weight_matrices(first_kernel, second_kernel):
    ch1, c_in = first_kernel.shape[:2]
    ch2 = second_kernel.shape[0]
    size = COLUMNS * ch1
    to_window = one_hot((COLUMNS, 3, WINDOW), lambda x, b, w: w == x + b)
    w1 = jnp.einsum("oiabc,xbw->cxoaiw", first_kernel, to_window, preferred_element_type=BF16)
    w1 = w1.reshape(3 * size, 3 * c_in * WINDOW)
    padded = jnp.pad(second_kernel, ((0, 0), (0, 0), (0, 0), (0, COLUMNS - 3), (0, 0)))
    w2 = padded.transpose(4, 0, 2, 3, 1).reshape(3 * ch2, 3 * size)
    from_cot = one_hot((COLUMNS, 3, 3), lambda x, q, b: x - 1 == 2 * (q - 1) + b - 1)
    w3 = jnp.einsum("oiabc,xqb->acxiqo", second_kernel, from_cot, preferred_element_type=BF16)
    w3 = w3.reshape(3, 3 * size, 3 * ch2)
    odd = jnp.concatenate([w3[2], w3[0]], axis=1)
    own = one_hot((2, COLUMNS, 3), lambda x, w, b: w == x + 2 - b)
    w4 = jnp.einsum("oiabc,xwb->cxiawo", first_kernel[:, :, ::-1], own, preferred_element_type=BF16)
    w4 = w4.reshape(3 * 2 * c_in, 3 * size)
    return w1, w2, odd, w3[1], w4


def shards(loaded_planes, first_kernel, first_bias, second_kernel, second_bias, cotangent):
    channels, _, planes_dev, _, width, depth_y = loaded_planes.shape
    tiles = lax.axis_size("xy")
    slabs = lax.axis_size("gz")
    ch1, ch2 = first_kernel.shape[0], second_kernel.shape[0]
    depth_z = planes_dev * tiles

    windows = pack(loaded_planes.reshape(channels, width, depth_y), tiles)
    mid = lax.all_to_all(windows, "xy", split_axis=0, concat_axis=0, tiled=True)

    cot = cotangent[:, :, 0].transpose(1, 0, 2)
    cot = jnp.concatenate([shifted(cot[-1:], "gz", 1), cot, shifted(cot[:1], "gz", -1)], axis=0)
    left, right = shifted(cot, "xy", 1), shifted(cot, "xy", -1)
    w1, w2, odd, even, w4 = weight_matrices(first_kernel, second_kernel)
    raw, shifts = prep(left, cot, right, odd, even, ch1)

    low, high = shifted(mid[-2:], "gz", 1), shifted(mid[:2], "gz", -1)
    g, t = lax.axis_index("gz"), lax.axis_index("xy")
    place = jnp.stack([g == 0, g == slabs - 1, t == 0, t == tiles - 1]).astype(jnp.int32)
    b1 = jnp.tile(first_bias, COLUMNS)[:, None]
    hidden, grad, sums = main(place, low, mid, high, raw, shifts, w1, b1, ch1, ch2)
    sums = total_over_devices(sums)
    features, input_grad = last(hidden, grad, w2, second_bias[:, None], w4, channels, ch2)
    scale = 1.0 / math.sqrt(slabs * depth_z * width * depth_y)
    first_grad, first_bias_grad, second_grad, second_bias_grad = unpack(sums, scale, channels, ch1, ch2)
    return (
        features[:, :, None, :],
        input_grad.reshape(channels, depth_z, 2, depth_y),
        first_grad,
        first_bias_grad,
        second_grad,
        second_bias_grad,
    )


def solution(mesh):
    return jax.shard_map(
        shards,
        mesh=mesh,
        in_specs=(
            P(None, "gz", None, "xy", None, None),
            P(),
            P(),
            P(),
            P(),
            P(None, "gz", "xy", None),
        ),
        out_specs=(P(None, "gz", "xy", None), P(None, "gz", "xy", None), P(), P(), P(), P()),
        check_vma=False,
    )
```

time: 504 us -> 122 us (0.24)
  matrix products: 236 us -> 0.73 us
  blocking collectives: 112 us -> 9.54 us
  local copies, waits for them, and re-layouts: 89.8 us -> 6.53 us
  Pallas kernels: 0 us -> 29.1 us
  waiting for transfers between devices: 6.64 us -> 24.3 us
  other arithmetic: 8.05 us -> 0.25 us
    conv_general_dilated x4 -> x0, matrix products: 159 us -> none  [the longest x1 139 us: back_first(): lax.conv_general_dilated(tensor[None], flipped, (1, 1, 1), ((0, 0), (0, 0...]
    psum x1 -> x0, blocking collectives: 112 us -> none  [shards(): lax.psum((first_term, first_bias_term, second_term, second_bias_term), ('...]
    transpose x2 -> x0, matrix products: 77.7 us -> none  [the longest x1 62.4 us: kernel_first(): return result.transpose(1, 0, 2, 3, 4)]
    conv_general_dilated x14 -> x0, local copies, waits for them, and re-layouts: 36.9 us -> none  [the longest x4 13.2 us: conv_first(): lax.conv_general_dilated(tensor[None], kernel, (1, 1, 1), ((0, 0), (0, 0)...]
    pallas_call x0 -> x5, Pallas kernels: none -> 29.1 us  [the longest x1 18.3 us: main(): pl.pallas_call(functools.partial(main_kernel, ch1=ch1, ch2=ch2), in_specs...]
    broadcast_in_dim x7 -> x4, local copies, waits for them, and re-layouts: 31.2 us -> 2.03 us  [the longest x3 1.94 us: spread(): jnp.broadcast_to(value[None], (count,) + value.shape)]
    ppermute x8 -> x0, starting transfers between devices: 19.5 us -> none  [the longest x4 12.3 us: with_halo(): lax.ppermute(lax.slice_in_dim(block, block.shape[dim] - width, None, axis...]
    all_to_all x1 -> x4, waiting for transfers between devices: 5.38 us -> 24.3 us  [the longest x3 15.9 us: exchange(): lax.all_to_all(value, axis, 0, 0, tiled=True, axis_index_groups=groups)]
  transfers between devices with their start and end apart: 13 -> 10, of which waited for: 2 -> 4; matrix products, arithmetic and copies ran while one was open for 29% -> 3% of each run, Pallas kernels for 0% -> 8%
where the time goes in v1:
time: 122 us; the launch traced here: 121 us
  starting transfers between devices  49.2 us (40%)
  Pallas kernels  29.1 us (24%)
  waiting for transfers between devices  24.3 us (20%)
  blocking collectives  9.54 us (8%)
  local copies, waits for them, and re-layouts  6.53 us (5%)
    ppermute x6, starting transfers between devices, shifted(): lax.ppermute(value, axis, [(source, source + steps) for source in range(f...  23.4 us
    pallas_call x1, Pallas kernels, main(): pl.pallas_call(functools.partial(main_kernel, ch1=ch1, ch2=ch2), in_specs...  18.3 us
    all_to_all x3, waiting for transfers between devices, exchange(): lax.all_to_all(value, axis, 0, 0, tiled=True, axis_index_groups=groups)  15.9 us
    all_to_all x3, starting transfers between devices, exchange(): lax.all_to_all(value, axis, 0, 0, tiled=True, axis_index_groups=groups)  13.8 us
    all_to_all x1, starting transfers between devices, shards(): mid = lax.all_to_all(windows, 'xy', split_axis=0, concat_axis=0, tiled=True)  12 us
    all_to_all x1, blocking collectives, exchange(): lax.all_to_all(value, axis, 0, 0, tiled=True, axis_index_groups=groups)  9.54 us
    all_to_all x1, waiting for transfers between devices, shards(): mid = lax.all_to_all(windows, 'xy', split_axis=0, concat_axis=0, tiled=True)  8.39 us
    pallas_call x1, Pallas kernels, prep(): pl.pallas_call(prep_kernel, out_shape=(jax.ShapeDtypeStruct((2 * (levels...  4.77 us
  transfers between devices with their start and end apart: 10, of which 4 were waited for; matrix products, arithmetic and copies ran while one was open for 3% of the time, Pallas kernels for 8%

profile of v1, /device:TPU:1, one launch (start us, length us, event | category | flops | bytes accessed | tf_op | source)
XLA Modules:
  0.0 120.8 jit_solution(7435494618045613742)
XLA Ops:
  0.6 0.0 copy-start.5
  0.7 1.0 copy.74
  1.6 4.5 %collective-permute-start.2 = (bf16[1,32,64]{2,1,0:T(8,128)(2,1)S(1)}, bf16[1,32,64]{2,1,0:T(8,128)(2,1)S(1)}, u32[]{:S(2)}, u32[]{:S(2)}) collective-permute-start(bf16[1,32,64]{2,1,0:T(8,128)(2,1)S(1)} %get-tuple-element.51), channel_id=1, source_target_pairs={{0,32},{32,64},{64,96},{96,128},{128,160},{160,192},{192,224},{224... | collective-permute-start | bytes 12296 | tf_op jit(solution)/shard_map/ppermute | solution.py:22
  6.2 5.6 %collective-permute-start.3 = (bf16[1,32,64]{2,1,0:T(8,128)(2,1)S(1)}, bf16[1,32,64]{2,1,0:T(8,128)(2,1)S(1)}, u32[]{:S(2)}, u32[]{:S(2)}) collective-permute-start(bf16[1,32,64]{2,1,0:T(8,128)(2,1)S(1)} %get-tuple-element.52), channel_id=1, source_target_pairs={{32,0},{64,32},{96,64},{128,96},{160,128},{192,160},{224,192},{256... | collective-permute-start | bytes 12296 | tf_op jit(solution)/shard_map/ppermute | solution.py:22
  11.7 0.8 copy-done
  12.6 0.7 pack_windows.1
  13.3 12.0 %all-to-all-start = ((bf16[32,32,128]{2,1,0:T(8,128)(2,1)}), bf16[32,32,128]{2,1,0:T(8,128)(2,1)S(1)}, u32[]{:S(2)}, u32[]{:S(2)}) async-start(bf16[32,32,128]{2,1,0:T(8,128)(2,1)} %pack_windows.1), calls=%async_computation | async-start | bytes 524288 | tf_op jit(solution)/shard_map/all_to_all | solution.py:347
  25.4 0.3 convolution_bitcast_fusion
  25.7 0.2 fusion.6
  25.9 0.1 copy.45
  26.0 0.1 squeeze.19
  26.2 0.1 copy.46
  26.3 0.1 squeeze.20
  26.5 0.3 convolution_bitcast_fusion.1
  26.8 0.1 pad_maximum_fusion.1.odd_ref
  26.9 3.1 %collective-permute-start.4 = (bf16[18,32,64]{2,1,0:T(8,128)(2,1)S(1)}, bf16[18,32,64]{2,1,0:T(8,128)(2,1)S(1)}, u32[]{:S(2)}, u32[]{:S(2)}) collective-permute-start(bf16[18,32,64]{2,1,0:T(8,128)(2,1)S(1)} %pad_maximum_fusion.mid_ref), channel_id=1, source_target_pairs={{0,1},{1,2},{2,3},{3,4},{4,5},{5,6},{6,7},{7,8},{8,9},{9,10},{10,1... | collective-permute-start | bytes 221192 | tf_op jit(solution)/shard_map/ppermute | solution.py:22
  30.1 1.3 %collective-permute-start.5 = (bf16[18,32,64]{2,1,0:T(8,128)(2,1)S(1)}, bf16[18,32,64]{2,1,0:T(8,128)(2,1)S(1)}, u32[]{:S(2)}, u32[]{:S(2)}) collective-permute-start(bf16[18,32,64]{2,1,0:T(8,128)(2,1)S(1)} %pad_maximum_fusion.mid_ref), channel_id=1, source_target_pairs={{1,0},{2,1},{3,2},{4,3},{5,4},{6,5},{7,6},{8,7},{9,8},{10,9},{11,1... | collective-permute-start | bytes 221192 | tf_op jit(solution)/shard_map/ppermute | solution.py:22
  31.4 8.4 %all-to-all-done.mid_ref = bf16[32,32,128]{2,1,0:T(8,128)(2,1)S(1)} async-done(((bf16[32,32,128]{2,1,0:T(8,128)(2,1)}), bf16[32,32,128]{2,1,0:T(8,128)(2,1)S(1)}, u32[]{:S(2)}, u32[]{:S(2)}) %all-to-all-start) | async-done | bytes 262176 | tf_op jit(solution)/shard_map/all_to_all | solution.py:347
  39.8 7.0 %collective-permute-start = (bf16[2,32,128]{2,1,0:T(8,128)(2,1)S(1)}, bf16[2,32,128]{2,1,0:T(8,128)(2,1)S(1)}, u32[]{:S(2)}, u32[]{:S(2)}) collective-permute-start(bf16[2,32,128]{2,1,0:T(8,128)(2,1)S(1)} %get-tuple-element.50), channel_id=1, source_target_pairs={{0,32},{32,64},{64,96},{96,128},{128,160},{160,192},{192,224},{224... | collective-permute-start | bytes 49160 | tf_op jit(solution)/shard_map/ppermute | solution.py:22
  46.8 1.9 %collective-permute-start.1 = (bf16[2,32,128]{2,1,0:T(8,128)(2,1)S(1)}, bf16[2,32,128]{2,1,0:T(8,128)(2,1)S(1)}, u32[]{:S(2)}, u32[]{:S(2)}) collective-permute-start(bf16[2,32,128]{2,1,0:T(8,128)(2,1)S(1)} %get-tuple-element.49), channel_id=1, source_target_pairs={{32,0},{64,32},{96,64},{128,96},{160,128},{192,160},{224,192},{256... | collective-permute-start | bytes 49160 | tf_op jit(solution)/shard_map/ppermute | solution.py:22
  48.7 0.1 add_convert_fusion.place_ref
  48.8 0.1 copy.47
  48.9 0.1 squeeze.21.even_ref
  49.1 0.2 copy.49
  49.2 0.2 reshape.51
  49.4 0.1 copy.50.w1_ref
  49.6 0.1 broadcast_in_dim_tile.4.b1_ref
  49.7 4.8 %spread_cotangent.1 = (f32[2176,128]{1,0:T(8,128)S(1)}, bf16[1536,128]{1,0:T(8,128)(2,1)S(1)}) custom-call(bf16[18,32,64]{2,1,0:T(8,128)(2,1)S(1)} %collective-permute-done.4.left_ref, bf16[18,32,64]{2,1,0:T(8,128)(2,1)S(1)} %pad_maximum_fusion.mid_ref, bf16[18,32,64]{2,1,0:T(8,128)(2,1)S(1)} %collective-permute-done.5.right_ref, ...), custom_call_target="tpu_custom_call" | custom-call | tf_op jit(solution)/shard_map/spread_cotangent/pallas_call | solution.py:106
  54.5 18.3 %hidden_and_sums.1 = (bf16[2176,128]{1,0:T(8,128)(2,1)S(1)}, bf16[2176,128]{1,0:T(8,128)(2,1)S(1)}, f32[192,128]{1,0:T(8,128)S(1)}) custom-call(s32[4]{0:T(128)S(1)} %add_convert_fusion.place_ref, bf16[2,32,128]{2,1,0:T(8,128)(2,1)S(1)} %collective-permute-done.low_ref, bf16[32,32,128]{2,1,0:T(8,128)(2,1)S(1)} %all-to-all-done.mid_ref, ...), custom_call_target="tpu_custom_call" | custom-call | tf_op jit(solution)/shard_map/hidden_and_sums/pallas_call | solution.py:191
  72.8 9.5 %all_to_all.25 = f32[8,24,128]{2,1,0:T(8,128)S(1)} all-to-all(f32[8,24,128]{2,1,0:T(8,128)S(1)} %bitcast.58), channel_id=1, replica_groups={{0,32,64,96,128,160,192,224},{256,288,320,352,384,416,448,480},{1,33,65..., dimensions={0} | all-to-all | bytes 196608 | tf_op jit(solution)/shard_map/all_to_all | solution.py:304
  82.4 0.6 broadcast_in_dim.12
  83.0 3.6 %all-to-all-start.2 = ((f32[8,24,128]{2,1,0:T(8,128)}), f32[8,24,128]{2,1,0:T(8,128)S(1)}, u32[]{:S(2)}, u32[]{:S(2)}) async-start(f32[8,24,128]{2,1,0:T(8,128)} %broadcast_in_dim.12), calls=%async_computation.2 | async-start | bytes 196608 | tf_op jit(solution)/shard_map/all_to_all | solution.py:304
  86.6 7.7 %all-to-all-done.2 = f32[8,24,128]{2,1,0:T(8,128)S(1)} async-done(((f32[8,24,128]{2,1,0:T(8,128)}), f32[8,24,128]{2,1,0:T(8,128)S(1)}, u32[]{:S(2)}, u32[]{:S(2)}) %all-to-all-start.2) | async-done | bytes 98336 | tf_op jit(solution)/shard_map/all_to_all | solution.py:304
  94.3 0.6 broadcast_in_dim.13
  94.9 3.4 %all-to-all-start.3 = ((f32[8,24,128]{2,1,0:T(8,128)}), f32[8,24,128]{2,1,0:T(8,128)S(1)}, u32[]{:S(2)}, u32[]{:S(2)}) async-start(f32[8,24,128]{2,1,0:T(8,128)} %broadcast_in_dim.13), calls=%async_computation.3 | async-start | bytes 196608 | tf_op jit(solution)/shard_map/all_to_all | solution.py:304
  98.3 0.1 convolution_bitcast_fusion.2
  98.5 7.4 %all-to-all-done.3 = f32[8,24,128]{2,1,0:T(8,128)S(1)} async-done(((f32[8,24,128]{2,1,0:T(8,128)}), f32[8,24,128]{2,1,0:T(8,128)S(1)}, u32[]{:S(2)}, u32[]{:S(2)}) %all-to-all-start.3) | async-done | bytes 98336 | tf_op jit(solution)/shard_map/all_to_all | solution.py:304
  105.9 0.6 broadcast_in_dim.28
  106.6 6.8 %all-to-all-start.4 = ((f32[8,24,128]{2,1,0:T(8,128)}), f32[8,24,128]{2,1,0:T(8,128)S(1)}, u32[]{:S(2)}, u32[]{:S(2)}) async-start(f32[8,24,128]{2,1,0:T(8,128)} %broadcast_in_dim.28), calls=%async_computation.4 | async-start | bytes 196608 | tf_op jit(solution)/shard_map/all_to_all | solution.py:304
  113.4 0.1 copy.52
  113.5 0.1 reshape.52
  113.7 0.1 copy.55.w2_ref
  113.8 0.1 reshape.53.w4_ref
  113.9 0.1 copy.56.b2_ref
  114.0 3.6 %features_and_input_grad.1 = (bf16[32,16,64]{2,1,0:T(8,128)(2,1)}, bf16[4,64,128]{2,1,0:T(8,128)(2,1)}) custom-call(bf16[2176,128]{1,0:T(8,128)(2,1)S(1)} %get-tuple-element.19.hidden_ref, bf16[2176,128]{1,0:T(8,128)(2,1)S(1)} %get-tuple-element.20.grad_ref, bf16[96,192]{1,0:T(8,128)(2,1)S(1)} %copy.55.w2_ref, f32[32,1]{1,0:T(8,128)S(1)} %copy.56.b2_ref, ...), custom_call_target="tpu_custom_call" | custom-call | tf_op jit(solution)/shard_map/features_and_input_grad/pallas_call | solution.py:238
  117.6 0.8 all-to-all-done.4
  118.4 0.6 copy-done.2
  119.0 1.7 %unpack_sums.1 = (f32[27,4,16]{2,1,0:T(4,128)}, f32[27,16,32]{2,1,0:T(8,128)}, f32[1,16]{1,0:T(1,128)}, f32[1,32]{1,0:T(1,128)}) custom-call(f32[192,128]{1,0:T(8,128)} %bitcast.62), custom_call_target="tpu_custom_call" | custom-call | tf_op jit(solution)/shard_map/unpack_sums/pallas_call | solution.py:280
  (31 shorter events, 0.2 us)
Async XLA Ops:
  0.6 24.7 %copy-start.5 = (bf16[4,3,3,1,1,1]{2,0,5,4,3,1:T(4,128)(2,1)S(1)}, bf16[4,3,3,1,1,1]{2,0,5,4,3,1:T(4,128)(2,1)}, u32[]{:S(2)}) copy-start(bf16[4,3,3,1,1,1]{2,0,5,4,3,1:T(4,128)(2,1)} %constant.35) | copy-start | bytes 220
  0.6 24.7 %copy-start.1 = (bf16[32,16,3,3,3]{0,1,4,3,2:T(8,128)(2,1)S(1)}, bf16[32,16,3,3,3]{0,1,4,3,2:T(8,128)(2,1)}, u32[]{:S(2)}) copy-start(bf16[32,16,3,3,3]{0,1,4,3,2:T(8,128)(2,1)} %param.12) | copy-start | bytes 82948
  1.6 25.2 %collective-permute-start.2 = (bf16[1,32,64]{2,1,0:T(8,128)(2,1)S(1)}, bf16[1,32,64]{2,1,0:T(8,128)(2,1)S(1)}, u32[]{:S(2)}, u32[]{:S(2)}) collective-permute-start(bf16[1,32,64]{2,1,0:T(8,128)(2,1)S(1)} %get-tuple-element.51), channel_id=1, source_target_pairs={{0,32},{32,64},{64,96},{96,128},{128,160},{160,192},{192,224},{224... | collective-permute-start | bytes 12296 | tf_op jit(solution)/shard_map/ppermute | solution.py:22
  6.2 20.7 %collective-permute-start.3 = (bf16[1,32,64]{2,1,0:T(8,128)(2,1)S(1)}, bf16[1,32,64]{2,1,0:T(8,128)(2,1)S(1)}, u32[]{:S(2)}, u32[]{:S(2)}) collective-permute-start(bf16[1,32,64]{2,1,0:T(8,128)(2,1)S(1)} %get-tuple-element.52), channel_id=1, source_target_pairs={{32,0},{64,32},{96,64},{128,96},{160,128},{192,160},{224,192},{256... | collective-permute-start | bytes 12296 | tf_op jit(solution)/shard_map/ppermute | solution.py:22
  11.7 0.8 copy-start
  13.3 26.5 %all-to-all-start = ((bf16[32,32,128]{2,1,0:T(8,128)(2,1)}), bf16[32,32,128]{2,1,0:T(8,128)(2,1)S(1)}, u32[]{:S(2)}, u32[]{:S(2)}) async-start(bf16[32,32,128]{2,1,0:T(8,128)(2,1)} %pack_windows.1), calls=%async_computation | async-start | bytes 524288 | tf_op jit(solution)/shard_map/all_to_all | solution.py:347
  25.7 0.8 copy-start.3
  25.7 0.8 copy-start.4
  26.7 22.8 %copy-start.7 = (f32[16]{0:T(128)S(1)}, f32[16]{0:T(128)}, u32[]{:S(2)}) copy-start(f32[16]{0:T(128)} %param.11) | copy-start | bytes 196
  26.9 22.7 %collective-permute-start.4 = (bf16[18,32,64]{2,1,0:T(8,128)(2,1)S(1)}, bf16[18,32,64]{2,1,0:T(8,128)(2,1)S(1)}, u32[]{:S(2)}, u32[]{:S(2)}) collective-permute-start(bf16[18,32,64]{2,1,0:T(8,128)(2,1)S(1)} %pad_maximum_fusion.mid_ref), channel_id=1, source_target_pairs={{0,1},{1,2},{2,3},{3,4},{4,5},{5,6},{6,7},{7,8},{8,9},{9,10},{10,1... | collective-permute-start | bytes 221192 | tf_op jit(solution)/shard_map/ppermute | solution.py:22
  30.1 19.6 %collective-permute-start.5 = (bf16[18,32,64]{2,1,0:T(8,128)(2,1)S(1)}, bf16[18,32,64]{2,1,0:T(8,128)(2,1)S(1)}, u32[]{:S(2)}, u32[]{:S(2)}) collective-permute-start(bf16[18,32,64]{2,1,0:T(8,128)(2,1)S(1)} %pad_maximum_fusion.mid_ref), channel_id=1, source_target_pairs={{1,0},{2,1},{3,2},{4,3},{5,4},{6,5},{7,6},{8,7},{9,8},{10,9},{11,1... | collective-permute-start | bytes 221192 | tf_op jit(solution)/shard_map/ppermute | solution.py:22
  39.8 14.7 %collective-permute-start = (bf16[2,32,128]{2,1,0:T(8,128)(2,1)S(1)}, bf16[2,32,128]{2,1,0:T(8,128)(2,1)S(1)}, u32[]{:S(2)}, u32[]{:S(2)}) collective-permute-start(bf16[2,32,128]{2,1,0:T(8,128)(2,1)S(1)} %get-tuple-element.50), channel_id=1, source_target_pairs={{0,32},{32,64},{64,96},{96,128},{128,160},{160,192},{192,224},{224... | collective-permute-start | bytes 49160 | tf_op jit(solution)/shard_map/ppermute | solution.py:22
  46.8 7.7 %collective-permute-start.1 = (bf16[2,32,128]{2,1,0:T(8,128)(2,1)S(1)}, bf16[2,32,128]{2,1,0:T(8,128)(2,1)S(1)}, u32[]{:S(2)}, u32[]{:S(2)}) collective-permute-start(bf16[2,32,128]{2,1,0:T(8,128)(2,1)S(1)} %get-tuple-element.49), channel_id=1, source_target_pairs={{32,0},{64,32},{96,64},{128,96},{160,128},{192,160},{224,192},{256... | collective-permute-start | bytes 49160 | tf_op jit(solution)/shard_map/ppermute | solution.py:22
  54.5 43.9 %copy-start.6 = (bf16[2,4,3,1,1,1]{2,1,5,4,3,0:T(4,128)(2,1)S(1)}, bf16[2,4,3,1,1,1]{2,1,5,4,3,0:T(4,128)(2,1)}, u32[]{:S(2)}) copy-start(bf16[2,4,3,1,1,1]{2,1,5,4,3,0:T(4,128)(2,1)} %constant.37) | copy-start | bytes 148
  83.0 11.3 %all-to-all-start.2 = ((f32[8,24,128]{2,1,0:T(8,128)}), f32[8,24,128]{2,1,0:T(8,128)S(1)}, u32[]{:S(2)}, u32[]{:S(2)}) async-start(f32[8,24,128]{2,1,0:T(8,128)} %broadcast_in_dim.12), calls=%async_computation.2 | async-start | bytes 196608 | tf_op jit(solution)/shard_map/all_to_all | solution.py:304
  86.6 27.3 %copy-start.8 = (f32[32]{0:T(128)S(1)}, f32[32]{0:T(128)}, u32[]{:S(2)}) copy-start(f32[32]{0:T(128)} %param.13) | copy-start | bytes 388
  94.9 11.0 %all-to-all-start.3 = ((f32[8,24,128]{2,1,0:T(8,128)}), f32[8,24,128]{2,1,0:T(8,128)S(1)}, u32[]{:S(2)}, u32[]{:S(2)}) async-start(f32[8,24,128]{2,1,0:T(8,128)} %broadcast_in_dim.13), calls=%async_computation.3 | async-start | bytes 196608 | tf_op jit(solution)/shard_map/all_to_all | solution.py:304
  106.6 11.8 %all-to-all-start.4 = ((f32[8,24,128]{2,1,0:T(8,128)}), f32[8,24,128]{2,1,0:T(8,128)S(1)}, u32[]{:S(2)}, u32[]{:S(2)}) async-start(f32[8,24,128]{2,1,0:T(8,128)} %broadcast_in_dim.28), calls=%async_computation.4 | async-start | bytes 196608 | tf_op jit(solution)/shard_map/all_to_all | solution.py:304
  118.4 0.6 copy-start.2

commit v2 on v1

v2 whole, which is shorter than its diff:
```python
import functools
import math

import jax
import jax.numpy as jnp
from jax import lax
from jax.experimental import pallas as pl
from jax.experimental.pallas import tpu as pltpu
from jax.sharding import PartitionSpec as P

BF16 = jnp.bfloat16
F32 = jnp.float32
WINDOW = 8
COLUMNS = 4
VMEM_LIMIT = 48 * 1024 * 1024


def shifted(value, axis, steps):
    count = lax.axis_size(axis)
    first, last = (max(0, -steps), min(count, count - steps))
    return lax.ppermute(value, axis, [(source, source + steps) for source in range(first, last)])


def mm(left, right):
    return jnp.dot(left, right, preferred_element_type=F32)


def mm_nt(left, right):
    return lax.dot_general(left, right, (((1,), (1,)), ((), ())), preferred_element_type=F32)


def from_left(value):
    lane = lax.broadcasted_iota(jnp.int32, value.shape, 1)
    return jnp.where(lane == 0, 0.0, pltpu.roll(value, 1, 1))


def from_right(value):
    lane = lax.broadcasted_iota(jnp.int32, value.shape, 1)
    last = value.shape[1] - 1
    return jnp.where(lane == last, 0.0, pltpu.roll(value, last, 1))


def lanes(blocks):
    return blocks[0] if len(blocks) == 1 else jnp.concatenate(blocks, axis=1)


def pack_kernel(planes_ref, out_ref, wide_ref):
    channels, width, _ = planes_ref.shape
    wide_ref[...] = jnp.zeros_like(wide_ref)
    wide_ref[:, 8 : 8 + width, :] = planes_ref[...].astype(F32)
    targets = out_ref.shape[0]
    row = lax.broadcasted_iota(jnp.int32, (WINDOW, out_ref.shape[2]), 0)
    for t in range(targets):
        parts = [wide_ref[i, 6 + 2 * t : 6 + 2 * t + WINDOW, :] for i in range(channels)]
        parts = [jnp.where(row >= WINDOW - 2, 1.0, part) for part in parts]
        out_ref[t] = jnp.concatenate(parts, axis=0).astype(BF16)


def pack(planes, targets):
    channels, width, depth_y = planes.shape
    shape = (targets, channels * WINDOW, depth_y)
    return pl.pallas_call(
        pack_kernel,
        out_shape=jax.ShapeDtypeStruct(shape, BF16),
        scratch_shapes=[pltpu.VMEM((channels, width + 16, depth_y), F32)],
        compiler_params=pltpu.CompilerParams(vmem_limit_bytes=VMEM_LIMIT),
        name="pack_windows",
    )(planes)


def split_bias(bias):
    high = bias.astype(BF16).astype(F32)
    middle = (bias - high).astype(BF16).astype(F32)
    return high, middle, bias - high - middle


def first_matrix(kernel_ref, bias_ref, turned_ref):
    _, c_in, ch1 = kernel_ref.shape
    size = COLUMNS * ch1
    turned_ref[...] = jnp.zeros_like(turned_ref)
    nothing = jnp.zeros((c_in, ch1), F32)

    def block(a, b, c):
        return kernel_ref[9 * a + 3 * b + c].astype(F32) if 0 <= b < 3 and c < 3 else nothing

    for a in range(3):
        for w in range(COLUMNS + 2):
            at = pl.ds(a * c_in * WINDOW + w, c_in, stride=WINDOW)
            for half in range(2):
                blocks = [block(a, w - x, c) for c in (2 * half, 2 * half + 1) for x in range(COLUMNS)]
                turned_ref[half, at, :] = jnp.concatenate(blocks, axis=1)
    for n, part in enumerate(split_bias(bias_ref[...])):
        row = c_in * WINDOW + n * WINDOW + WINDOW - 2
        for x in range(COLUMNS):
            half, right = divmod(size + x * ch1, 128)
            turned_ref[half, row : row + 1, right : right + ch1] = part
    return jnp.concatenate([turned_ref[0].T, turned_ref[1].T], axis=0)[: 3 * size].astype(BF16)


def spread_matrix(kernel_ref, out_ref, row, a, column):
    _, ch1, ch2 = kernel_ref.shape
    for c in range(3):
        for x in range(COLUMNS):
            for q in range(3):
                b = x - 1 - 2 * (q - 1) + 1
                if 0 <= b <= 2:
                    down, right = row + (c * COLUMNS + x) * ch1, column + q * ch2
                    out_ref[down : down + ch1, right : right + ch2] = kernel_ref[9 * a + 3 * b + c]


def unspread(terms):
    size = terms.shape[0] // 3
    return from_right(terms[:size]) + terms[size : 2 * size] + from_left(terms[2 * size :])


def prep_kernel(
    left_ref,
    mid_ref,
    right_ref,
    k1_ref,
    b1_ref,
    k2_ref,
    raw_ref,
    shifts_ref,
    ends_ref,
    w1_ref,
    odd_ref,
    even_ref,
    wide_ref,
    flat_ref,
    turned_ref,
):
    ch2, cells, half_y = mid_ref.shape
    rows = 3 * ch2
    depth_y = 2 * half_y
    w1_ref[...] = first_matrix(k1_ref, b1_ref, turned_ref)
    odd_ref[...] = jnp.zeros_like(odd_ref)
    even_ref[...] = jnp.zeros_like(even_ref)
    spread_matrix(k2_ref, odd_ref, 0, 2, 0)
    spread_matrix(k2_ref, odd_ref, 0, 0, rows)
    spread_matrix(k2_ref, even_ref, 0, 1, 0)
    spread = (
        2 * lax.broadcasted_iota(jnp.int32, (half_y, depth_y), 0)
        == lax.broadcasted_iota(jnp.int32, (half_y, depth_y), 1)
    ).astype(F32).astype(BF16)
    for n, ref in enumerate((left_ref, mid_ref, right_ref)):
        flat_ref[n * ch2 * cells : (n + 1) * ch2 * cells, :] = ref[...].astype(F32).reshape(ch2 * cells, half_y)
    for q in range(cells):
        block = jnp.concatenate(
            [flat_ref[pl.ds(n * ch2 * cells + q, ch2, stride=cells), :] for n in range(3)], axis=0
        )
        wide = mm(block.astype(BF16), spread)
        wide_ref[q * rows : (q + 1) * rows, :] = wide.astype(BF16)
        own = wide[ch2 : 2 * ch2]
        base = q * rows
        shifts_ref[base : base + ch2, :] = from_right(own).astype(BF16)
        shifts_ref[base + ch2 : base + 2 * ch2, :] = own.astype(BF16)
        shifts_ref[base + 2 * ch2 : base + 3 * ch2, :] = from_left(own).astype(BF16)
    ends_ref[:rows, :] = wide_ref[:rows, :]
    ends_ref[rows:, :] = wide_ref[(cells - 1) * rows :, :]
    size = even_ref.shape[0] // 3

    def store(z, terms):
        raw_ref[(z - 1) * size : z * size, :] = unspread(terms)

    for m in range(0, cells - 1, 2):
        group = [k for k in (m, m + 1) if k < cells - 1]
        odd = mm(odd_ref[...], lanes([wide_ref[k * rows : (k + 2) * rows, :] for k in group]))
        even = mm(even_ref[...], lanes([wide_ref[(k + 1) * rows : (k + 2) * rows, :] for k in group]))
        for n, k in enumerate(group):
            store(2 * k + 1, odd[:, n * depth_y : (n + 1) * depth_y])
            store(2 * k + 2, even[:, n * depth_y : (n + 1) * depth_y])


def prep(left, mid, right, k1, b1, k2):
    ch2, cells, half_y = mid.shape
    _, c_in, ch1 = k1.shape
    depth_y = 2 * half_y
    size, rows = COLUMNS * ch1, 3 * ch2
    return pl.pallas_call(
        prep_kernel,
        out_shape=(
            jax.ShapeDtypeStruct((2 * (cells - 1) * size, depth_y), F32),
            jax.ShapeDtypeStruct((cells * rows, depth_y), BF16),
            jax.ShapeDtypeStruct((2 * rows, depth_y), BF16),
            jax.ShapeDtypeStruct((3 * size, 3 * c_in * WINDOW), BF16),
            jax.ShapeDtypeStruct((3 * size, 2 * rows), BF16),
            jax.ShapeDtypeStruct((3 * size, rows), BF16),
        ),
        scratch_shapes=[
            pltpu.VMEM((cells * rows, depth_y), BF16),
            pltpu.VMEM((rows * cells, half_y), F32),
            pltpu.VMEM((2, 3 * c_in * WINDOW, 128), F32),
        ],
        compiler_params=pltpu.CompilerParams(vmem_limit_bytes=VMEM_LIMIT),
        cost_estimate=pl.CostEstimate(flops=800_000_000, bytes_accessed=10_000_000, transcendentals=0),
        name="spread_cotangent",
    )(left, mid, right, k1, b1, k2)


def activate(groups, plane, raw, place_ref, w1_ref, depth_z, store):
    size = w1_ref.shape[0] // 3
    ch1 = size // COLUMNS
    at_first_z, at_last_z, at_first_x, at_last_x = (place_ref[k] for k in range(4))
    depth_y = plane(groups[0][0]).shape[1]
    row = lax.broadcasted_iota(jnp.int32, (size, depth_y), 0)
    outside = ((row < ch1) & (at_first_x != 0)) | ((row >= 3 * ch1) & (at_last_x != 0))
    inside = jnp.where(outside, 0.0, 1.0)
    for group in groups:
        source = lanes([jnp.concatenate([plane(z + a) for a in (-1, 0, 1)], axis=0) for z in group])
        products = mm(w1_ref[...], source)
        for n, z in enumerate(group):
            terms = products[:, n * depth_y : (n + 1) * depth_y]
            pre = from_left(terms[:size]) + terms[size : 2 * size] + from_right(terms[2 * size :])
            sigma = 1.0 / (1.0 + jnp.exp(-pre))
            keep = inside
            if z == -1:
                keep = inside * jnp.where(at_first_z != 0, 0.0, 1.0)
            if z == depth_z:
                keep = inside * jnp.where(at_last_z != 0, 0.0, 1.0)
            kept = sigma * keep
            store(z, (pre * kept)[: 3 * ch1], raw(z) * (kept * (1.0 + pre * (1.0 - sigma))))


def side_by_side(grad, ch1):
    own = grad[ch1 : 3 * ch1]
    parts = [from_right(own), own, from_left(own)]
    sides = [part[x * ch1 : (x + 1) * ch1] for x in range(2) for part in parts]
    return jnp.concatenate(sides, axis=0).astype(BF16)


def add_first(levels, plane, moved, total):
    for k in range(0, len(levels), 2):
        group = levels[k : k + 2]
        source = lanes([jnp.concatenate([plane(z + a) for a in (-1, 0, 1)], axis=0) for z in group])
        product = mm_nt(source, lanes([moved(z) for z in group]))
        total = product if total is None else total + product
    return total


def add_second(cells, hidden, shifts_ref, total_cells, total):
    rows = shifts_ref.shape[0] // total_cells
    for k in range(0, len(cells), 2):
        group = cells[k : k + 2]
        source = lanes([jnp.concatenate([hidden(2 * q + a) for a in (-1, 0, 1)], axis=0) for q in group])
        product = mm_nt(source, lanes([shifts_ref[q * rows : (q + 1) * rows, :] for q in group]))
        total = product if total is None else total + product
    return total


def store_level(hidden_ref, grad_ref, moved_ref, at, hidden, grad, own, ch1):
    size = COLUMNS * ch1
    hidden_ref[at * size : at * size + 3 * ch1, :] = hidden.astype(BF16)
    hidden_ref[at * size + 3 * ch1 : (at + 1) * size, :] = jnp.ones((ch1, hidden.shape[1]), BF16)
    grad_ref[at * size : (at + 1) * size, :] = grad.astype(BF16)
    if own:
        moved_ref[at * 6 * ch1 : (at + 1) * 6 * ch1, :] = side_by_side(grad, ch1)


def inner_kernel(
    place_ref, mid_ref, raw_ref, shifts_ref, w1_ref, hidden_ref, grad_ref, first_ref, second_ref, moved_ref
):
    depth_z = mid_ref.shape[0]
    size = w1_ref.shape[0] // 3
    ch1 = size // COLUMNS
    levels = list(range(1, depth_z - 1))

    def store(z, hidden, grad):
        store_level(hidden_ref, grad_ref, moved_ref, z - 1, hidden, grad, True, ch1)

    def plane(z):
        return mid_ref[z]

    def raw(z):
        return raw_ref[(z - 1) * size : z * size, :]

    groups = [levels[k : k + 2] for k in range(0, len(levels), 2)]
    activate(groups, plane, raw, place_ref, w1_ref, depth_z, store)
    six = 6 * ch1
    first_ref[...] = add_first(levels, plane, lambda z: moved_ref[(z - 1) * six : z * six, :], None)
    cells = list(range(1, depth_z // 2 - 1))

    def hidden(z):
        return hidden_ref[(z - 1) * size : z * size, :]

    second_ref[...] = add_second(cells, hidden, shifts_ref, depth_z // 2, None)


def edge_kernel(
    place_ref,
    low_ref,
    mid_ref,
    high_ref,
    ends_ref,
    odd_ref,
    even_ref,
    shifts_ref,
    w1_ref,
    inner_ref,
    first_ref,
    second_ref,
    hidden_ref,
    grad_ref,
    sums_ref,
    moved_ref,
    fold_ref,
):
    depth_z, rows, depth_y = mid_ref.shape
    size = w1_ref.shape[0] // 3
    ch1 = size // COLUMNS
    ch2 = shifts_ref.shape[0] // (3 * (depth_z // 2))
    places = {-1: 0, 0: 1, depth_z - 1: 2, depth_z: 3}
    spread_rows = 3 * ch2
    below = [low_ref[2 * rows :, :], ends_ref[:spread_rows, :]]
    above = [ends_ref[spread_rows:, :], high_ref[2 * rows :, :]]
    odd = mm(odd_ref[...], lanes([jnp.concatenate(pair, axis=0) for pair in (below, above)]))
    even = mm(even_ref[...], lanes([below[1], above[1]]))
    raws = {
        -1: unspread(odd[:, :depth_y]),
        0: unspread(even[:, :depth_y]),
        depth_z - 1: unspread(odd[:, depth_y:]),
        depth_z: unspread(even[:, depth_y:]),
    }

    def plane(z):
        if z < 0:
            return low_ref[(z + 2) * rows : (z + 3) * rows, :]
        if z >= depth_z:
            return high_ref[(z - depth_z) * rows : (z - depth_z + 1) * rows, :]
        return mid_ref[z]

    def store(z, hidden, grad):
        store_level(hidden_ref, grad_ref, moved_ref, places[z], hidden, grad, 0 <= z < depth_z, ch1)

    groups = [[-1, 0], [depth_z - 1, depth_z]]
    activate(groups, plane, lambda z: raws[z], place_ref, w1_ref, depth_z, store)
    six = 6 * ch1

    def moved(z):
        return moved_ref[places[z] * six : (places[z] + 1) * six, :]

    def hidden(z):
        if z in places:
            return hidden_ref[places[z] * size : (places[z] + 1) * size, :]
        return inner_ref[(z - 1) * size : z * size, :]

    first = add_first([0, depth_z - 1], plane, moved, first_ref[...])
    second = add_second([0, depth_z // 2 - 1], hidden, shifts_ref, depth_z // 2, second_ref[...])
    three = 3 * ch1
    wide = 3 * ch2
    main = 7 * ch1
    for a in range(2):
        sums_ref[a * three : (a + 1) * three, :wide] = second[a * size : a * size + three]
    sums_ref[2 * three : main, :wide] = second[2 * size : 2 * size + ch1]
    rest = second[2 * size + ch1 : 2 * size + three]
    sums_ref[6 * ch1 : main, wide:] = jnp.zeros((ch1, 128 - wide), F32)
    sums_ref[main : main + ch1, :] = jnp.zeros((ch1, 128), F32)
    for c in range(3):
        sums_ref[c * 2 * ch1 : (c + 1) * 2 * ch1, wide:] = rest[:, c * ch2 : (c + 1) * ch2]
    count = first.shape[0]
    fold_ref[...] = first[:, :three] + pltpu.roll(first, count - 1, 0)[:, three:]
    groups = count // WINDOW
    for b in range(3):
        block = fold_ref[pl.ds(b + 1, groups, stride=WINDOW), :]
        if b < 2:
            sums_ref[main : main + groups, b * three : (b + 1) * three] = block
        else:
            sums_ref[main : main + groups, wide : wide + ch1] = block[:, :ch1]
            sums_ref[main : main + groups, wide + ch1 :] = block[:, ch1 : 2 * ch1]
            sums_ref[6 * ch1 : 6 * ch1 + groups, wide : wide + ch1] = block[:, 2 * ch1 :]
    at = count // 3 + WINDOW - 2
    sums_ref[main + groups : main + groups + 1, :ch1] = fold_ref[at : at + 1, ch1 : 2 * ch1]
    at = size + three
    sums_ref[main + groups + 1 : main + groups + 2, :ch2] = second[at : at + 1, ch2 : 2 * ch2]


def inner(place, mid, raw, shifts, w1):
    depth_z, rows, depth_y = mid.shape
    size = w1.shape[0] // 3
    ch1 = size // COLUMNS
    ch2 = shifts.shape[0] // (3 * (depth_z // 2))
    vmem = pl.BlockSpec(memory_space=pltpu.VMEM)
    count = depth_z - 2
    return pl.pallas_call(
        inner_kernel,
        in_specs=[pl.BlockSpec(memory_space=pltpu.SMEM)] + [vmem] * 4,
        out_specs=(vmem,) * 4,
        out_shape=(
            jax.ShapeDtypeStruct((count * size, depth_y), BF16),
            jax.ShapeDtypeStruct((count * size, depth_y), BF16),
            jax.ShapeDtypeStruct((3 * rows, 6 * ch1), F32),
            jax.ShapeDtypeStruct((3 * size, 3 * ch2), F32),
        ),
        scratch_shapes=[pltpu.VMEM((count * 6 * ch1, depth_y), BF16)],
        compiler_params=pltpu.CompilerParams(vmem_limit_bytes=VMEM_LIMIT),
        cost_estimate=pl.CostEstimate(flops=800_000_000, bytes_accessed=10_000_000, transcendentals=500_000),
        name="inner_levels",
    )(place, mid, raw, shifts, w1)


def edge(place, low, mid, high, ends, odd, even, shifts, w1, inner_hidden, first, second):
    _, rows, depth_y = mid.shape
    size = w1.shape[0] // 3
    ch1 = size // COLUMNS
    vmem = pl.BlockSpec(memory_space=pltpu.VMEM)
    return pl.pallas_call(
        edge_kernel,
        in_specs=[pl.BlockSpec(memory_space=pltpu.SMEM)] + [vmem] * 11,
        out_specs=(vmem,) * 3,
        out_shape=(
            jax.ShapeDtypeStruct((4 * size, depth_y), BF16),
            jax.ShapeDtypeStruct((4 * size, depth_y), BF16),
            jax.ShapeDtypeStruct((8 * ch1, 128), F32),
        ),
        scratch_shapes=[pltpu.VMEM((4 * 6 * ch1, depth_y), BF16), pltpu.VMEM((3 * rows, 3 * ch1), F32)],
        compiler_params=pltpu.CompilerParams(vmem_limit_bytes=VMEM_LIMIT),
        name="edge_levels_and_sums",
    )(place, low, mid, high, ends, odd, even, shifts, w1, inner_hidden, first, second)


def last_kernel(
    hidden_ref,
    hidden_edge_ref,
    grad_ref,
    grad_edge_ref,
    k1_ref,
    k2_ref,
    b2_ref,
    feat_ref,
    gin_ref,
    featw_ref,
    ginw_ref,
    turned_ref,
    w4_ref,
):
    ch2, depth_q, half_y = feat_ref.shape
    c_in, _, depth_y = gin_ref.shape
    depth_z = 2 * depth_q
    size = hidden_edge_ref.shape[0] // 4
    places = {-1: 0, 0: 1, depth_z - 1: 2, depth_z: 3}

    def level(inner_ref, edge_ref, z):
        if z in places:
            return edge_ref[places[z] * size : (places[z] + 1) * size, :]
        return inner_ref[(z - 1) * size : z * size, :]

    def window(inner_ref, edge_ref, z):
        return jnp.concatenate([level(inner_ref, edge_ref, z + a) for a in (-1, 0, 1)], axis=0)

    ch1 = size // COLUMNS
    turned_ref[...] = jnp.zeros_like(turned_ref)
    w4_ref[...] = jnp.zeros_like(w4_ref)
    for a in range(3):
        for b in range(3):
            for c in range(3):
                k = 9 * a + 3 * b + c
                down = a * size + b * ch1
                turned_ref[down : down + ch1, c * ch2 : (c + 1) * ch2] = k2_ref[k].astype(F32)
                for x in range(2):
                    down, right = (c * 2 + x) * c_in, (2 - a) * size + (x + 2 - b) * ch1
                    w4_ref[down : down + c_in, right : right + ch1] = k1_ref[k].astype(F32)
    for n, part in enumerate(split_bias(b2_ref[...])):
        row = size + 3 * ch1 + n
        turned_ref[row : row + 1, ch2 : 2 * ch2] = part
    w2 = turned_ref[...].T[: 3 * ch2].astype(BF16)
    w4 = w4_ref[...].astype(BF16)
    pick = (
        lax.broadcasted_iota(jnp.int32, (depth_y, half_y), 0)
        == 2 * lax.broadcasted_iota(jnp.int32, (depth_y, half_y), 1)
    ).astype(F32).astype(BF16)

    for q in range(0, depth_q, 2):
        source = lanes([window(hidden_ref, hidden_edge_ref, 2 * k) for k in (q, q + 1)])
        products = mm(w2, source)
        for n in range(2):
            terms = products[:, n * depth_y : (n + 1) * depth_y]
            full = from_left(terms[:ch2]) + terms[ch2 : 2 * ch2] + from_right(terms[2 * ch2 :])
            featw_ref[pl.ds(q + n, ch2, stride=depth_q), :] = mm(full.astype(BF16), pick)
    feat_ref[...] = featw_ref[...].reshape(feat_ref.shape).astype(BF16)

    two = 2 * c_in
    for z in range(0, depth_z, 2):
        source = lanes([window(grad_ref, grad_edge_ref, k) for k in (z, z + 1)])
        products = mm(w4, source)
        for n in range(2):
            terms = products[:, n * depth_y : (n + 1) * depth_y]
            full = from_right(terms[:two]) + terms[two : 2 * two] + from_left(terms[2 * two :])
            for x in range(2):
                at = pl.ds(2 * (z + n) + x, c_in, stride=2 * depth_z)
                ginw_ref[at, :] = full[x * c_in : (x + 1) * c_in]
    gin_ref[...] = ginw_ref[...].reshape(gin_ref.shape).astype(BF16)


def last(hidden, hidden_edge, grad, grad_edge, k1, k2, b2):
    depth_y = hidden.shape[1]
    size = hidden_edge.shape[0] // 4
    _, c_in, ch1 = k1.shape
    ch2 = k2.shape[2]
    depth_z = hidden.shape[0] // size + 2
    depth_q = depth_z // 2
    return pl.pallas_call(
        last_kernel,
        out_shape=(
            jax.ShapeDtypeStruct((ch2, depth_q, depth_y // 2), BF16),
            jax.ShapeDtypeStruct((c_in, 2 * depth_z, depth_y), BF16),
        ),
        scratch_shapes=[
            pltpu.VMEM((ch2 * depth_q, depth_y // 2), F32),
            pltpu.VMEM((c_in * 2 * depth_z, depth_y), F32),
            pltpu.VMEM((3 * size, 128), F32),
            pltpu.VMEM((3 * 2 * c_in, 3 * size), F32),
        ],
        compiler_params=pltpu.CompilerParams(vmem_limit_bytes=VMEM_LIMIT),
        cost_estimate=pl.CostEstimate(flops=800_000_000, bytes_accessed=10_000_000, transcendentals=0),
        name="features_and_input_grad",
    )(hidden, hidden_edge, grad, grad_edge, k1, k2, b2)


def unpack_kernel(sums_ref, first_ref, second_ref, bias1_ref, bias2_ref, *, scale):
    _, c_in, ch1 = first_ref.shape
    ch2 = second_ref.shape[2]
    three, wide, main = 3 * ch1, 3 * ch2, 7 * ch1
    for a in range(3):
        for b in range(3):
            for c in range(3):
                k = 9 * a + 3 * b + c
                at = a * three + b * ch1
                if at < main:
                    block = sums_ref[at : at + ch1, c * ch2 : (c + 1) * ch2]
                else:
                    at = c * 2 * ch1 + at - main
                    block = sums_ref[at : at + ch1, wide:]
                second_ref[k] = block * scale
                down, right = (main, b * three + c * ch1) if b < 2 or c < 2 else (6 * ch1, wide)
                first_ref[k] = sums_ref[down + a * c_in : down + (a + 1) * c_in, right : right + ch1] * scale
    at = main + 3 * c_in
    bias1_ref[...] = sums_ref[at : at + 1, :ch1] * scale
    bias2_ref[...] = sums_ref[at + 1 : at + 2, :ch2] * scale


def unpack(sums, scale, c_in, ch1, ch2):
    first, bias1, second, bias2 = (
        jax.ShapeDtypeStruct(shape, F32) for shape in ((27, c_in, ch1), (1, ch1), (27, ch1, ch2), (1, ch2))
    )
    first, second, bias1, bias2 = pl.pallas_call(
        functools.partial(unpack_kernel, scale=scale),
        out_shape=(first, second, bias1, bias2),
        name="unpack_sums",
    )(sums)
    first = first.reshape(3, 3, 3, c_in, ch1).transpose(4, 3, 0, 1, 2)
    second = second.reshape(3, 3, 3, ch1, ch2).transpose(4, 3, 0, 1, 2)
    return first, bias1[0], second, bias2[0]


def total_over_devices(sums):
    slabs, tiles = lax.axis_size("gz"), lax.axis_size("xy")

    def exchange(value, axis):
        return lax.all_to_all(value, axis, 0, 0, tiled=True)

    def copies(value, count):
        return jnp.broadcast_to(value[None], (count,) + value.shape)

    part = exchange(sums.reshape(slabs, -1, sums.shape[1]), "gz").sum(0).astype(BF16)
    part = exchange(copies(part, tiles), "xy").astype(F32).sum(0)
    parts = exchange(copies(part, slabs), "gz")
    return parts.reshape(sums.shape)


def shards(loaded_planes, first_kernel, first_bias, second_kernel, second_bias, cotangent):
    channels, _, planes_dev, _, width, depth_y = loaded_planes.shape
    tiles = lax.axis_size("xy")
    slabs = lax.axis_size("gz")
    ch1, ch2 = first_kernel.shape[0], second_kernel.shape[0]
    depth_z = planes_dev * tiles
    k1 = first_kernel.transpose(2, 3, 4, 1, 0).reshape(27, channels, ch1)
    k2 = second_kernel.transpose(2, 3, 4, 1, 0).reshape(27, ch1, ch2)
    g, t = lax.axis_index("gz"), lax.axis_index("xy")
    place = jnp.stack([g == 0, g == slabs - 1, t == 0, t == tiles - 1]).astype(jnp.int32)

    windows = pack(loaded_planes.reshape(channels, width, depth_y), tiles)
    mid = lax.all_to_all(windows, "xy", split_axis=0, concat_axis=0, tiled=True)

    cot = cotangent.reshape(ch2, depth_z // 2, depth_y // 2)
    left, right = shifted(cot, "xy", 1), shifted(cot, "xy", -1)
    raw, shifts, ends, w1, odd, even = prep(left, cot, right, k1, first_bias[None], k2)

    rows = mid.shape[1]
    upward = jnp.concatenate([mid[-2:].reshape(2 * rows, depth_y), ends[3 * ch2 :]], axis=0)
    downward = jnp.concatenate([mid[:2].reshape(2 * rows, depth_y), ends[: 3 * ch2]], axis=0)
    low, high = shifted(upward, "gz", 1), shifted(downward, "gz", -1)
    hidden, grad, first, second = inner(place, mid, raw, shifts, w1)
    hidden_edge, grad_edge, sums = edge(
        place, low, mid, high, ends, odd, even, shifts, w1, hidden, first, second
    )
    sums = total_over_devices(sums)
    features, input_grad = last(hidden, hidden_edge, grad, grad_edge, k1, k2, second_bias[None])
    scale = 1.0 / math.sqrt(slabs * depth_z * width * depth_y)
    first_grad, first_bias_grad, second_grad, second_bias_grad = unpack(sums, scale, channels, ch1, ch2)
    return (
        features[:, :, None, :],
        input_grad.reshape(channels, depth_z, 2, depth_y),
        first_grad,
        first_bias_grad,
        second_grad,
        second_bias_grad,
    )


def solution(mesh):
    return jax.shard_map(
        shards,
        mesh=mesh,
        in_specs=(
            P(None, "gz", None, "xy", None, None),
            P(),
            P(),
            P(),
            P(),
            P(None, "gz", "xy", None),
        ),
        out_specs=(P(None, "gz", "xy", None), P(None, "gz", "xy", None), P(), P(), P(), P()),
        check_vma=False,
    )
```

time: 122 us -> 92.9 us (0.76)
  blocking collectives: 9.54 us -> 31.2 us
  Pallas kernels: 29.1 us -> 8.81 us
  starting transfers between devices: 49.2 us -> 36.4 us
  waiting for transfers between devices: 24.3 us -> 11.6 us
  local copies, waits for them, and re-layouts: 6.53 us -> 3.43 us
    all_to_all x1 -> x2, blocking collectives: 9.54 us -> 31.2 us  [exchange(): return lax.all_to_all(value, axis, 0, 0, tiled=True)]
    pallas_call x2 -> x3, Pallas kernels: 23.1 us -> 4.09 us  [the longest x1 1.7 us: inner(): pl.pallas_call(inner_kernel, in_specs=[pl.BlockSpec(memory_space=pltpu.SM...]
    all_to_all x3 -> x1, waiting for transfers between devices: 15.9 us -> 2.91 us  [exchange(): return lax.all_to_all(value, axis, 0, 0, tiled=True)]
    ppermute x6 -> x4, starting transfers between devices: 23.4 us -> 14.6 us  [shifted(): lax.ppermute(value, axis, [(source, source + steps) for source in range(f...]
    all_to_all x3 -> x1, starting transfers between devices: 13.8 us -> 5.16 us  [exchange(): return lax.all_to_all(value, axis, 0, 0, tiled=True)]
    ppermute x6 -> x4, waiting for transfers between devices: 0.02 us -> 6.72 us  [shifted(): lax.ppermute(value, axis, [(source, source + steps) for source in range(f...]
    all_to_all x1, waiting for transfers between devices: 8.39 us -> 1.95 us  [shards(): mid = lax.all_to_all(windows, 'xy', split_axis=0, concat_axis=0, tiled=True)]
    all_to_all x1, starting transfers between devices: 12 us -> 16.6 us  [shards(): mid = lax.all_to_all(windows, 'xy', split_axis=0, concat_axis=0, tiled=True)]
  transfers between devices with their start and end apart: 10 -> 6, of which waited for: 4 -> 5; matrix products, arithmetic and copies ran while one was open for 3% -> 0% of each run, Pallas kernels for 8% -> 6%
where the time goes in v2:
time: 92.9 us; the launch traced here: 92.3 us
  starting transfers between devices  36.4 us (39%)
  blocking collectives  31.2 us (34%)
  waiting for transfers between devices  11.6 us (12%)
  Pallas kernels  8.81 us (9%)
  local copies, waits for them, and re-layouts  3.43 us (4%)
    all_to_all x2, blocking collectives, exchange(): return lax.all_to_all(value, axis, 0, 0, tiled=True)  31.2 us
    all_to_all x1, starting transfers between devices, shards(): mid = lax.all_to_all(windows, 'xy', split_axis=0, concat_axis=0, tiled=True)  16.6 us
    ppermute x4, starting transfers between devices, shifted(): lax.ppermute(value, axis, [(source, source + steps) for source in range(f...  14.6 us
    ppermute x4, waiting for transfers between devices, shifted(): lax.ppermute(value, axis, [(source, source + steps) for source in range(f...  6.72 us
    all_to_all x1, starting transfers between devices, exchange(): return lax.all_to_all(value, axis, 0, 0, tiled=True)  5.16 us
    all_to_all x1, waiting for transfers between devices, exchange(): return lax.all_to_all(value, axis, 0, 0, tiled=True)  2.91 us
    unnamed x14, local copies, waits for them, and re-layouts  2.77 us
    pallas_call x1, Pallas kernels, last(): pl.pallas_call(last_kernel, out_shape=(jax.ShapeDtypeStruct((ch2, depth_q...  2.32 us
  transfers between devices with their start and end apart: 6, of which 5 were waited for; matrix products, arithmetic and copies ran while one was open for 0% of the time, Pallas kernels for 6%

profile of v2, /device:TPU:1, one launch (start us, length us, event | category | flops | bytes accessed | tf_op | source)
XLA Modules:
  0.0 92.3 jit_solution(15332399403213283892)
XLA Ops:
  0.6 0.0 copy-start
  0.6 0.8 copy-done
  1.5 0.7 pack_windows.1
  2.2 0.0 copy-start.1
  2.2 0.0 copy-start.2
  2.2 16.6 %all-to-all-start = ((bf16[32,32,128]{2,1,0:T(8,128)(2,1)}), bf16[32,32,128]{2,1,0:T(8,128)(2,1)S(1)}, u32[]{:S(2)}, u32[]{:S(2)}) async-start(bf16[32,32,128]{2,1,0:T(8,128)(2,1)} %pack_windows.1), calls=%async_computation | async-start | bytes 524288 | tf_op jit(solution)/shard_map/all_to_all | solution.py:582
  18.9 0.0 copy-start.3
  18.9 0.0 copy-done.1
  18.9 3.1 %collective-permute-start = (bf16[32,16,64]{2,1,0:T(8,128)(2,1)S(1)}, bf16[32,16,64]{2,1,0:T(8,128)(2,1)S(1)}, u32[]{:S(2)}, u32[]{:S(2)}) collective-permute-start(bf16[32,16,64]{2,1,0:T(8,128)(2,1)S(1)} %bitcast.32), channel_id=1, source_target_pairs={{0,1},{1,2},{2,3},{3,4},{4,5},{5,6},{6,7},{7,8},{8,9},{9,10},{10,1... | collective-permute-start | bytes 196616 | tf_op jit(solution)/shard_map/ppermute | solution.py:21
  22.0 1.3 %collective-permute-start.1 = (bf16[32,16,64]{2,1,0:T(8,128)(2,1)S(1)}, bf16[32,16,64]{2,1,0:T(8,128)(2,1)S(1)}, u32[]{:S(2)}, u32[]{:S(2)}) collective-permute-start(bf16[32,16,64]{2,1,0:T(8,128)(2,1)S(1)} %bitcast.33), channel_id=1, source_target_pairs={{1,0},{2,1},{3,2},{4,3},{5,4},{6,5},{7,6},{8,7},{9,8},{10,9},{11,1... | collective-permute-start | bytes 196616 | tf_op jit(solution)/shard_map/ppermute | solution.py:21
  23.3 0.1 add_convert_fusion.place_ref
  23.4 3.3 %collective-permute-done.left_ref = bf16[32,16,64]{2,1,0:T(8,128)(2,1)S(1)} collective-permute-done((bf16[32,16,64]{2,1,0:T(8,128)(2,1)S(1)}, bf16[32,16,64]{2,1,0:T(8,128)(2,1)S(1)}, u32[]{:S(2)}, u32[]{:S(2)}) %collective-permute-start) | collective-permute-done | bytes 65568 | tf_op jit(solution)/shard_map/ppermute | solution.py:21
  26.7 1.7 %collective-permute-done.1.right_ref = bf16[32,16,64]{2,1,0:T(8,128)(2,1)S(1)} collective-permute-done((bf16[32,16,64]{2,1,0:T(8,128)(2,1)S(1)}, bf16[32,16,64]{2,1,0:T(8,128)(2,1)S(1)}, u32[]{:S(2)}, u32[]{:S(2)}) %collective-permute-start.1) | collective-permute-done | bytes 65568 | tf_op jit(solution)/shard_map/ppermute | solution.py:21
  28.4 0.0 copy-start.4
  28.4 0.0 copy-done.2
  28.5 0.0 copy-done.3
  28.5 0.6 copy-done.4
  29.1 1.1 %spread_cotangent.1 = (f32[1920,128]{1,0:T(8,128)S(1)}, bf16[1536,128]{1,0:T(8,128)(2,1)S(1)}, bf16[192,128]{1,0:T(8,128)(2,1)S(1)}, bf16[192,96]{1,0:T(8,128)(2...) custom-call(bf16[32,16,64]{2,1,0:T(8,128)(2,1)S(1)} %collective-permute-done.left_ref, ...), custom_call_target="tpu_custom_call" | custom-call | flops 800000000 | bytes 10000000 | tf_op jit(solution)/shard_map/spread_cotangent/pallas_call | solution.py:180
  30.2 2.0 %all-to-all-done.mid_ref = bf16[32,32,128]{2,1,0:T(8,128)(2,1)S(1)} async-done(((bf16[32,32,128]{2,1,0:T(8,128)(2,1)}), bf16[32,32,128]{2,1,0:T(8,128)(2,1)S(1)}, u32[]{:S(2)}, u32[]{:S(2)}) %all-to-all-start) | async-done | bytes 262176 | tf_op jit(solution)/shard_map/all_to_all | solution.py:582
  32.2 8.2 %collective-permute-start.2 = (bf16[160,128]{1,0:T(8,128)(2,1)S(1)}, bf16[160,128]{1,0:T(8,128)(2,1)S(1)}, u32[]{:S(2)}, u32[]{:S(2)}) collective-permute-start(bf16[160,128]{1,0:T(8,128)(2,1)S(1)} %pad_maximum_fusion), channel_id=1, source_target_pairs={{0,32},{32,64},{64,96},{96,128},{128,160},{160,192},{192,224},{224... | collective-permute-start | bytes 122888 | tf_op jit(solution)/shard_map/ppermute | solution.py:21
  40.4 1.9 %collective-permute-start.3 = (bf16[160,128]{1,0:T(8,128)(2,1)S(1)}, bf16[160,128]{1,0:T(8,128)(2,1)S(1)}, u32[]{:S(2)}, u32[]{:S(2)}) collective-permute-start(bf16[160,128]{1,0:T(8,128)(2,1)S(1)} %pad_maximum_fusion.1), channel_id=1, source_target_pairs={{32,0},{64,32},{96,64},{128,96},{160,128},{192,160},{224,192},{256... | collective-permute-start | bytes 122888 | tf_op jit(solution)/shard_map/ppermute | solution.py:21
  42.4 1.7 %inner_levels.1 = (bf16[1920,128]{1,0:T(8,128)(2,1)S(1)}, bf16[1920,128]{1,0:T(8,128)(2,1)S(1)}, f32[96,96]{1,0:T(8,128)S(1)}, f32[192,96]{1,0:T(8,128)S(1)}) custom-call(s32[4]{0:T(128)S(1)} %add_convert_fusion.place_ref, bf16[32,32,128]{2,1,0:T(8,128)(2,1)S(1)} %all-to-all-done.mid_ref, f32[1920,128]{1,0:T(8,128)S(1)} %get-tuple-element.25.raw_ref, ...), custom_call_target="tpu_custom_call" | custom-call | flops 800000000 | bytes 10000000 | tf_op jit(solution)/shard_map/inner_levels/pallas_call | solution.py:384
  44.1 0.0 collective-permute-done.2.low_ref
  44.1 1.7 %collective-permute-done.3.high_ref = bf16[160,128]{1,0:T(8,128)(2,1)S(1)} collective-permute-done((bf16[160,128]{1,0:T(8,128)(2,1)S(1)}, bf16[160,128]{1,0:T(8,128)(2,1)S(1)}, u32[]{:S(2)}, u32[]{:S(2)}) %collective-permute-start.3) | collective-permute-done | bytes 40992 | tf_op jit(solution)/shard_map/ppermute | solution.py:21
  45.8 1.3 %edge_levels_and_sums.1 = (bf16[256,128]{1,0:T(8,128)(2,1)S(1)}, bf16[256,128]{1,0:T(8,128)(2,1)S(1)}, f32[128,128]{1,0:T(8,128)S(1)}) custom-call(s32[4]{0:T(128)S(1)} %add_convert_fusion.place_ref, bf16[160,128]{1,0:T(8,128)(2,1)S(1)} %collective-permute-done.2.low_ref, bf16[32,32,128]{2,1,0:T(8,128)(2,1)S(1)} %all-to-all-done.mid_ref, ...), custom_call_target="tpu_custom_call" | custom-call | tf_op jit(solution)/shard_map/edge_levels_and_sums/pallas_call | solution.py:406
  47.1 9.7 %all_to_all.20 = f32[16,8,128]{2,1,0:T(8,128)S(1)} all-to-all(f32[16,8,128]{2,1,0:T(8,128)S(1)} %bitcast.31), channel_id=1, replica_groups=mesh['gz'=16,'xy'=32] {'gz'}, dimensions={0} | all-to-all | bytes 131072 | tf_op jit(solution)/shard_map/all_to_all | solution.py:559
  56.8 21.4 %all_to_all.21 = bf16[32,8,128]{2,1,0:T(8,128)(2,1)S(1)} all-to-all(bf16[32,8,128]{2,1,0:T(8,128)(2,1)S(1)} %broadcast_in_dim.24), channel_id=1, replica_groups=mesh['gz'=16,'xy'=32] {'xy'}, dimensions={0} | all-to-all | bytes 131072 | tf_op jit(solution)/shard_map/all_to_all | solution.py:559
  78.3 0.6 broadcast_in_dim.25
  78.9 5.2 %all-to-all-start.3 = ((f32[16,8,128]{2,1,0:T(8,128)}), f32[16,8,128]{2,1,0:T(8,128)S(1)}, u32[]{:S(2)}, u32[]{:S(2)}) async-start(f32[16,8,128]{2,1,0:T(8,128)} %broadcast_in_dim.25), calls=%async_computation.3 | async-start | bytes 131072 | tf_op jit(solution)/shard_map/all_to_all | solution.py:559
  84.1 0.0 copy-start.5
  84.1 0.6 copy-done.5
  84.8 2.3 %features_and_input_grad.1 = (bf16[32,16,64]{2,1,0:T(8,128)(2,1)}, bf16[4,64,128]{2,1,0:T(8,128)(2,1)}) custom-call(bf16[1920,128]{1,0:T(8,128)(2,1)S(1)} %get-tuple-element.28.inner_ref.hidden_ref, bf16[256,128]{1,0:T(8,128)(2,1)S(1)} %get-tuple-element.34.hidden_edge_ref, bf16[1920,128]{1,0:T(8,128)(2,1)S(1)} %get-tuple-element.35.grad_ref, ...), custom_call_target="tpu_custom_call" | custom-call | flops 800000000 | bytes 10000000 | tf_op jit(solution)/shard_map/features_and_input_grad/pallas_call | solution.py:501
  87.1 2.9 %all-to-all-done.3 = f32[16,8,128]{2,1,0:T(8,128)S(1)} async-done(((f32[16,8,128]{2,1,0:T(8,128)}), f32[16,8,128]{2,1,0:T(8,128)S(1)}, u32[]{:S(2)}, u32[]{:S(2)}) %all-to-all-start.3) | async-done | bytes 65568 | tf_op jit(solution)/shard_map/all_to_all | solution.py:559
  90.0 0.0 copy-start.6
  90.0 0.6 copy-done.6
  90.6 1.7 %unpack_sums.1 = (f32[27,4,16]{2,1,0:T(4,128)}, f32[27,16,32]{2,1,0:T(8,128)}, f32[1,16]{1,0:T(1,128)}, f32[1,32]{1,0:T(1,128)}) custom-call(f32[128,128]{1,0:T(8,128)} %bitcast.41), custom_call_target="tpu_custom_call" | custom-call | tf_op jit(solution)/shard_map/unpack_sums/pallas_call | solution.py:545
  (7 shorter events, 0.1 us)
Async XLA Ops:
  0.6 0.8 copy-start
  2.2 16.7 %copy-start.1 = (bf16[32,16,1,64]{3,1,2,0:T(8,128)(2,1)S(1)}, bf16[32,16,1,64]{3,1,2,0:T(8,128)(2,1)}, u32[]{:S(2)}) copy-start(bf16[32,16,1,64]{3,1,2,0:T(8,128)(2,1)} %param.11) | copy-start | bytes 196612
  2.2 26.2 %copy-start.2 = (bf16[32,16,3,3,3]{0,1,4,3,2:T(8,128)(2,1)S(1)}, bf16[32,16,3,3,3]{0,1,4,3,2:T(8,128)(2,1)}, u32[]{:S(2)}) copy-start(bf16[32,16,3,3,3]{0,1,4,3,2:T(8,128)(2,1)} %param.9) | copy-start | bytes 82948
  2.2 30.0 %all-to-all-start = ((bf16[32,32,128]{2,1,0:T(8,128)(2,1)}), bf16[32,32,128]{2,1,0:T(8,128)(2,1)S(1)}, u32[]{:S(2)}, u32[]{:S(2)}) async-start(bf16[32,32,128]{2,1,0:T(8,128)(2,1)} %pack_windows.1), calls=%async_computation | async-start | bytes 524288 | tf_op jit(solution)/shard_map/all_to_all | solution.py:582
  18.9 9.6 %copy-start.3 = (bf16[16,4,3,3,3]{0,1,4,3,2:T(4,128)(2,1)S(1)}, bf16[16,4,3,3,3]{0,1,4,3,2:T(4,128)(2,1)}, u32[]{:S(2)}) copy-start(bf16[16,4,3,3,3]{0,1,4,3,2:T(4,128)(2,1)} %param.7) | copy-start | bytes 10372
  18.9 7.9 %collective-permute-start = (bf16[32,16,64]{2,1,0:T(8,128)(2,1)S(1)}, bf16[32,16,64]{2,1,0:T(8,128)(2,1)S(1)}, u32[]{:S(2)}, u32[]{:S(2)}) collective-permute-start(bf16[32,16,64]{2,1,0:T(8,128)(2,1)S(1)} %bitcast.32), channel_id=1, source_target_pairs={{0,1},{1,2},{2,3},{3,4},{4,5},{5,6},{6,7},{7,8},{8,9},{9,10},{10,1... | collective-permute-start | bytes 196616 | tf_op jit(solution)/shard_map/ppermute | solution.py:21
  22.0 6.4 %collective-permute-start.1 = (bf16[32,16,64]{2,1,0:T(8,128)(2,1)S(1)}, bf16[32,16,64]{2,1,0:T(8,128)(2,1)S(1)}, u32[]{:S(2)}, u32[]{:S(2)}) collective-permute-start(bf16[32,16,64]{2,1,0:T(8,128)(2,1)S(1)} %bitcast.33), channel_id=1, source_target_pairs={{1,0},{2,1},{3,2},{4,3},{5,4},{6,5},{7,6},{8,7},{9,8},{10,9},{11,1... | collective-permute-start | bytes 196616 | tf_op jit(solution)/shard_map/ppermute | solution.py:21
  28.4 0.7 copy-start.4
  32.2 11.9 %collective-permute-start.2 = (bf16[160,128]{1,0:T(8,128)(2,1)S(1)}, bf16[160,128]{1,0:T(8,128)(2,1)S(1)}, u32[]{:S(2)}, u32[]{:S(2)}) collective-permute-start(bf16[160,128]{1,0:T(8,128)(2,1)S(1)} %pad_maximum_fusion), channel_id=1, source_target_pairs={{0,32},{32,64},{64,96},{96,128},{128,160},{160,192},{192,224},{224... | collective-permute-start | bytes 122888 | tf_op jit(solution)/shard_map/ppermute | solution.py:21
  40.4 5.3 %collective-permute-start.3 = (bf16[160,128]{1,0:T(8,128)(2,1)S(1)}, bf16[160,128]{1,0:T(8,128)(2,1)S(1)}, u32[]{:S(2)}, u32[]{:S(2)}) collective-permute-start(bf16[160,128]{1,0:T(8,128)(2,1)S(1)} %pad_maximum_fusion.1), channel_id=1, source_target_pairs={{32,0},{64,32},{96,64},{128,96},{160,128},{192,160},{224,192},{256... | collective-permute-start | bytes 122888 | tf_op jit(solution)/shard_map/ppermute | solution.py:21
  78.9 11.1 %all-to-all-start.3 = ((f32[16,8,128]{2,1,0:T(8,128)}), f32[16,8,128]{2,1,0:T(8,128)S(1)}, u32[]{:S(2)}, u32[]{:S(2)}) async-start(f32[16,8,128]{2,1,0:T(8,128)} %broadcast_in_dim.25), calls=%async_computation.3 | async-start | bytes 131072 | tf_op jit(solution)/shard_map/all_to_all | solution.py:559
  84.1 0.7 copy-start.5
  90.0 0.6 copy-start.6

commit v3 on v2

--- a/solution.py
+++ b/solution.py
@@ -12,7 +12,7 @@
 F32 = jnp.float32
 WINDOW = 8
 COLUMNS = 4
-VMEM_LIMIT = 48 * 1024 * 1024
+VMEM_LIMIT = 12 * 1024 * 1024
 
 
 def shifted(value, axis, steps):
@@ -113,52 +113,90 @@
     return from_right(terms[:size]) + terms[size : 2 * size] + from_left(terms[2 * size :])
 
 
-def prep_kernel(
-    left_ref,
-    mid_ref,
-    right_ref,
-    k1_ref,
-    b1_ref,
-    k2_ref,
-    raw_ref,
-    shifts_ref,
-    ends_ref,
-    w1_ref,
-    odd_ref,
-    even_ref,
-    wide_ref,
-    flat_ref,
-    turned_ref,
-):
+def moved_three(value):
+    return jnp.concatenate([from_right(value), value, from_left(value)], axis=0).astype(BF16)
+
+
+def even_plane(pair):
+    lane = lax.broadcasted_iota(jnp.int32, pair.shape, 1)
+    return jnp.where(lane % 2 == 0, pair, 0.0)
+
+
+def odd_plane(pair):
+    return even_plane(from_right(pair))
+
+
+def own_kernel(mid_ref, k1_ref, b1_ref, k2_ref, shifts_ref, pairs_ref, w1_ref, odd_ref, even_ref, flat_ref, turned_ref):
     ch2, cells, half_y = mid_ref.shape
     rows = 3 * ch2
     depth_y = 2 * half_y
+    spread = (
+        2 * lax.broadcasted_iota(jnp.int32, (half_y, depth_y), 0)
+        == lax.broadcasted_iota(jnp.int32, (half_y, depth_y), 1)
+    ).astype(F32).astype(BF16)
+    flat_ref[...] = mid_ref[...].astype(F32).reshape(ch2 * cells, half_y)
+    for q in range(cells):
+        wide = mm(flat_ref[pl.ds(q, ch2, stride=cells), :].astype(BF16), spread)
+        shifts_ref[q * rows : (q + 1) * rows, :] = moved_three(wide)
+        if q % 2 == 0:
+            first = wide
+        else:
+            pairs_ref[q // 2 * ch2 : (q // 2 + 1) * ch2, :] = (first + from_left(wide)).astype(BF16)
     w1_ref[...] = first_matrix(k1_ref, b1_ref, turned_ref)
     odd_ref[...] = jnp.zeros_like(odd_ref)
     even_ref[...] = jnp.zeros_like(even_ref)
     spread_matrix(k2_ref, odd_ref, 0, 2, 0)
     spread_matrix(k2_ref, odd_ref, 0, 0, rows)
     spread_matrix(k2_ref, even_ref, 0, 1, 0)
-    spread = (
-        2 * lax.broadcasted_iota(jnp.int32, (half_y, depth_y), 0)
-        == lax.broadcasted_iota(jnp.int32, (half_y, depth_y), 1)
-    ).astype(F32).astype(BF16)
-    for n, ref in enumerate((left_ref, mid_ref, right_ref)):
-        flat_ref[n * ch2 * cells : (n + 1) * ch2 * cells, :] = ref[...].astype(F32).reshape(ch2 * cells, half_y)
-    for q in range(cells):
-        block = jnp.concatenate(
-            [flat_ref[pl.ds(n * ch2 * cells + q, ch2, stride=cells), :] for n in range(3)], axis=0
-        )
-        wide = mm(block.astype(BF16), spread)
-        wide_ref[q * rows : (q + 1) * rows, :] = wide.astype(BF16)
-        own = wide[ch2 : 2 * ch2]
-        base = q * rows
-        shifts_ref[base : base + ch2, :] = from_right(own).astype(BF16)
-        shifts_ref[base + ch2 : base + 2 * ch2, :] = own.astype(BF16)
-        shifts_ref[base + 2 * ch2 : base + 3 * ch2, :] = from_left(own).astype(BF16)
-    ends_ref[:rows, :] = wide_ref[:rows, :]
-    ends_ref[rows:, :] = wide_ref[(cells - 1) * rows :, :]
+
+
+def prepare_own(mid, k1, b1, k2):
+    ch2, cells, half_y = mid.shape
+    _, c_in, ch1 = k1.shape
+    depth_y = 2 * half_y
+    size, rows = COLUMNS * ch1, 3 * ch2
+    return pl.pallas_call(
+        own_kernel,
+        out_shape=(
+            jax.ShapeDtypeStruct((cells * rows, depth_y), BF16),
+            jax.ShapeDtypeStruct((cells // 2 * ch2, depth_y), BF16),
+            jax.ShapeDtypeStruct((3 * size, 3 * c_in * WINDOW), BF16),
+            jax.ShapeDtypeStruct((3 * size, 2 * rows), BF16),
+            jax.ShapeDtypeStruct((3 * size, rows), BF16),
+        ),
+        scratch_shapes=[
+            pltpu.VMEM((ch2 * cells, half_y), F32),
+            pltpu.VMEM((2, 3 * c_in * WINDOW, 128), F32),
+        ],
+        compiler_params=pltpu.CompilerParams(vmem_limit_bytes=VMEM_LIMIT),
+        cost_estimate=pl.CostEstimate(flops=100_000_000, bytes_accessed=2_000_000, transcendentals=0),
+        name="spread_cotangent",
+    )(mid, k1, b1, k2)
+
+
+def spread_columns(left_ref, shifts_ref, right_ref, wide_ref, cells):
+    rows = wide_ref.shape[0] // cells
+    ch2 = rows // 3
+    for k in range(cells // 2):
+        sides = [ref[k * ch2 : (k + 1) * ch2, :].astype(F32) for ref in (left_ref, right_ref)]
+        for n, plane in enumerate((even_plane, odd_plane)):
+            at = (2 * k + n) * rows
+            wide_ref[at : at + ch2, :] = plane(sides[0]).astype(BF16)
+            wide_ref[at + ch2 : at + 2 * ch2, :] = shifts_ref[at + ch2 : at + 2 * ch2, :]
+            wide_ref[at + 2 * ch2 : at + rows, :] = plane(sides[1]).astype(BF16)
+
+
+def rim_columns(ref, plane, first_row):
+    ch2 = (ref.shape[0] - first_row) // 3
+    left, own, right = (ref[first_row + k * ch2 : first_row + (k + 1) * ch2, :] for k in range(3))
+    left, right = (plane(pair.astype(F32)).astype(BF16) for pair in (left, right))
+    return jnp.concatenate([left, own, right], axis=0)
+
+
+def raw_levels(wide_ref, odd_ref, even_ref, raw_ref, cells):
     size = even_ref.shape[0] // 3
+    rows = wide_ref.shape[0] // cells
+    depth_y = wide_ref.shape[1]
 
     def store(z, terms):
         raw_ref[(z - 1) * size : z * size, :] = unspread(terms)
@@ -170,32 +208,6 @@
         for n, k in enumerate(group):
             store(2 * k + 1, odd[:, n * depth_y : (n + 1) * depth_y])
             store(2 * k + 2, even[:, n * depth_y : (n + 1) * depth_y])
-
-
-def prep(left, mid, right, k1, b1, k2):
-    ch2, cells, half_y = mid.shape
-    _, c_in, ch1 = k1.shape
-    depth_y = 2 * half_y
-    size, rows = COLUMNS * ch1, 3 * ch2
-    return pl.pallas_call(
-        prep_kernel,
-        out_shape=(
-            jax.ShapeDtypeStruct((2 * (cells - 1) * size, depth_y), F32),
-            jax.ShapeDtypeStruct((cells * rows, depth_y), BF16),
-            jax.ShapeDtypeStruct((2 * rows, depth_y), BF16),
-            jax.ShapeDtypeStruct((3 * size, 3 * c_in * WINDOW), BF16),
-            jax.ShapeDtypeStruct((3 * size, 2 * rows), BF16),
-            jax.ShapeDtypeStruct((3 * size, rows), BF16),
-        ),
-        scratch_shapes=[
-            pltpu.VMEM((cells * rows, depth_y), BF16),
-            pltpu.VMEM((rows * cells, half_y), F32),
-            pltpu.VMEM((2, 3 * c_in * WINDOW, 128), F32),
-        ],
-        compiler_params=pltpu.CompilerParams(vmem_limit_bytes=VMEM_LIMIT),
-        cost_estimate=pl.CostEstimate(flops=800_000_000, bytes_accessed=10_000_000, transcendentals=0),
-        name="spread_cotangent",
-    )(left, mid, right, k1, b1, k2)
 
 
 def activate(groups, plane, raw, place_ref, w1_ref, depth_z, store):
@@ -229,44 +241,54 @@
     return jnp.concatenate(sides, axis=0).astype(BF16)
 
 
-def add_first(levels, plane, moved, total):
-    for k in range(0, len(levels), 2):
-        group = levels[k : k + 2]
-        source = lanes([jnp.concatenate([plane(z + a) for a in (-1, 0, 1)], axis=0) for z in group])
-        product = mm_nt(source, lanes([moved(z) for z in group]))
-        total = product if total is None else total + product
-    return total
-
-
-def add_second(cells, hidden, shifts_ref, total_cells, total):
-    rows = shifts_ref.shape[0] // total_cells
-    for k in range(0, len(cells), 2):
-        group = cells[k : k + 2]
-        source = lanes([jnp.concatenate([hidden(2 * q + a) for a in (-1, 0, 1)], axis=0) for q in group])
-        product = mm_nt(source, lanes([shifts_ref[q * rows : (q + 1) * rows, :] for q in group]))
-        total = product if total is None else total + product
-    return total
-
-
-def store_level(hidden_ref, grad_ref, moved_ref, at, hidden, grad, own, ch1):
+def first_terms(levels, plane, moved):
+    source = lanes([jnp.concatenate([plane(z + a) for a in (-1, 0, 1)], axis=0) for z in levels])
+    return mm_nt(source, lanes([moved(z) for z in levels]))
+
+
+def second_terms(cells, hidden, shifts):
+    both = lanes([jnp.concatenate([hidden(2 * q + 1), hidden(2 * q + 2)], axis=0) for q in cells])
+    size = both.shape[0] // 2
+    upper = mm_nt(both, lanes([shifts(q + 1) for q in cells]))
+    return upper, mm_nt(both[:size], lanes([shifts(q) for q in cells]))
+
+
+def store_level(hidden_ref, grad_ref, at, hidden, grad, ch1):
     size = COLUMNS * ch1
     hidden_ref[at * size : at * size + 3 * ch1, :] = hidden.astype(BF16)
     hidden_ref[at * size + 3 * ch1 : (at + 1) * size, :] = jnp.ones((ch1, hidden.shape[1]), BF16)
     grad_ref[at * size : (at + 1) * size, :] = grad.astype(BF16)
-    if own:
-        moved_ref[at * 6 * ch1 : (at + 1) * 6 * ch1, :] = side_by_side(grad, ch1)
 
 
 def inner_kernel(
-    place_ref, mid_ref, raw_ref, shifts_ref, w1_ref, hidden_ref, grad_ref, first_ref, second_ref, moved_ref
+    place_ref,
+    mid_ref,
+    left_ref,
+    shifts_ref,
+    right_ref,
+    odd_ref,
+    even_ref,
+    w1_ref,
+    wide_ref,
+    hidden_ref,
+    grad_ref,
+    first_ref,
+    second_ref,
+    raw_ref,
+    moved_ref,
 ):
     depth_z = mid_ref.shape[0]
     size = w1_ref.shape[0] // 3
     ch1 = size // COLUMNS
     levels = list(range(1, depth_z - 1))
+    six = 6 * ch1
+    three = shifts_ref.shape[0] // (depth_z // 2)
+    spread_columns(left_ref, shifts_ref, right_ref, wide_ref, depth_z // 2)
+    raw_levels(wide_ref, odd_ref, even_ref, raw_ref, depth_z // 2)
 
     def store(z, hidden, grad):
-        store_level(hidden_ref, grad_ref, moved_ref, z - 1, hidden, grad, True, ch1)
+        store_level(hidden_ref, grad_ref, z - 1, hidden, grad, ch1)
+        moved_ref[(z - 1) * six : z * six, :] = side_by_side(grad, ch1)
 
     def plane(z):
         return mid_ref[z]
@@ -274,78 +296,102 @@
     def raw(z):
         return raw_ref[(z - 1) * size : z * size, :]
 
-    groups = [levels[k : k + 2] for k in range(0, len(levels), 2)]
-    activate(groups, plane, raw, place_ref, w1_ref, depth_z, store)
-    six = 6 * ch1
-    first_ref[...] = add_first(levels, plane, lambda z: moved_ref[(z - 1) * six : z * six, :], None)
-    cells = list(range(1, depth_z // 2 - 1))
+    def moved(z):
+        return moved_ref[(z - 1) * six : z * six, :]
 
     def hidden(z):
         return hidden_ref[(z - 1) * size : z * size, :]
 
-    second_ref[...] = add_second(cells, hidden, shifts_ref, depth_z // 2, None)
+    def shifts(q):
+        return shifts_ref[q * three : (q + 1) * three, :]
+
+    pairs = [levels[k : k + 2] for k in range(0, len(levels), 2)]
+    activate(pairs, plane, raw, place_ref, w1_ref, depth_z, store)
+    total = None
+    for pair in pairs:
+        term = first_terms(pair, plane, moved)
+        total = term if total is None else total + term
+    first_ref[...] = total
+    upper = lower = None
+    cells = list(range(depth_z // 2 - 1))
+    for k in range(0, len(cells), 2):
+        add_upper, add_lower = second_terms(cells[k : k + 2], hidden, shifts)
+        upper = add_upper if upper is None else upper + add_upper
+        lower = add_lower if lower is None else lower + add_lower
+    second_ref[: 2 * size, :] = upper
+    second_ref[2 * size :, :] = lower
 
 
 def edge_kernel(
     place_ref,
-    low_ref,
     mid_ref,
     high_ref,
-    ends_ref,
+    wide_ref,
     odd_ref,
     even_ref,
     shifts_ref,
     w1_ref,
-    inner_ref,
     first_ref,
     second_ref,
     hidden_ref,
     grad_ref,
     sums_ref,
+    begin_ref,
     moved_ref,
     fold_ref,
 ):
     depth_z, rows, depth_y = mid_ref.shape
     size = w1_ref.shape[0] // 3
     ch1 = size // COLUMNS
-    ch2 = shifts_ref.shape[0] // (3 * (depth_z // 2))
-    places = {-1: 0, 0: 1, depth_z - 1: 2, depth_z: 3}
-    spread_rows = 3 * ch2
-    below = [low_ref[2 * rows :, :], ends_ref[:spread_rows, :]]
-    above = [ends_ref[spread_rows:, :], high_ref[2 * rows :, :]]
-    odd = mm(odd_ref[...], lanes([jnp.concatenate(pair, axis=0) for pair in (below, above)]))
-    even = mm(even_ref[...], lanes([below[1], above[1]]))
+    cells = depth_z // 2
+    spread_rows = wide_ref.shape[0] // cells
+    ch2 = spread_rows // 3
+    end = wide_ref[(cells - 1) * spread_rows :, :]
+    above = rim_columns(high_ref, even_plane, 2 * rows)
+    even = mm(even_ref[...], lanes([wide_ref[:spread_rows, :], above]))
     raws = {
-        -1: unspread(odd[:, :depth_y]),
         0: unspread(even[:, :depth_y]),
-        depth_z - 1: unspread(odd[:, depth_y:]),
+        depth_z - 1: unspread(mm(odd_ref[...], jnp.concatenate([end, above], axis=0))),
         depth_z: unspread(even[:, depth_y:]),
     }
+    places = {depth_z - 1: 0, depth_z: 1, 0: 2}
+    six = 6 * ch1
 
     def plane(z):
         if z < 0:
-            return low_ref[(z + 2) * rows : (z + 3) * rows, :]
+            return jnp.zeros((rows, depth_y), BF16)
         if z >= depth_z:
             return high_ref[(z - depth_z) * rows : (z - depth_z + 1) * rows, :]
         return mid_ref[z]
 
     def store(z, hidden, grad):
-        store_level(hidden_ref, grad_ref, moved_ref, places[z], hidden, grad, 0 <= z < depth_z, ch1)
-
-    groups = [[-1, 0], [depth_z - 1, depth_z]]
-    activate(groups, plane, lambda z: raws[z], place_ref, w1_ref, depth_z, store)
-    six = 6 * ch1
+        at = places[z]
+        if z > 0:
+            store_level(hidden_ref, grad_ref, at, hidden, grad, ch1)
+        else:
+            begin_ref[: 3 * ch1, :] = hidden.astype(BF16)
+            begin_ref[3 * ch1 :, :] = jnp.ones((ch1, depth_y), BF16)
+        moved_ref[at * six : (at + 1) * six, :] = side_by_side(grad, ch1)
 
     def moved(z):
         return moved_ref[places[z] * six : (places[z] + 1) * six, :]
 
     def hidden(z):
-        if z in places:
-            return hidden_ref[places[z] * size : (places[z] + 1) * size, :]
-        return inner_ref[(z - 1) * size : z * size, :]
-
-    first = add_first([0, depth_z - 1], plane, moved, first_ref[...])
-    second = add_second([0, depth_z // 2 - 1], hidden, shifts_ref, depth_z // 2, second_ref[...])
+        return hidden_ref[places[z] * size : (places[z] + 1) * size, :]
+
+    def shifts(q):
+        if q < cells:
+            return shifts_ref[q * spread_rows : (q + 1) * spread_rows, :]
+        return moved_three(above[ch2 : 2 * ch2].astype(F32))
+
+    groups = [[depth_z - 1, depth_z], [0]]
+    activate(groups, plane, lambda z: raws[z], place_ref, w1_ref, depth_z, store)
+    at_bottom = jnp.where(place_ref[0] != 0, 1.0, 0.0)
+    first = first_ref[...] + first_terms([depth_z - 1, depth_z], plane, moved)
+    first = first + at_bottom * first_terms([0], plane, moved)
+    upper, lower = second_terms([cells - 1], hidden, shifts)
+    bottom = at_bottom * mm_nt(begin_ref[...], shifts(0))
+    second = second_ref[...] + jnp.concatenate([upper[:size], upper[size:] + bottom, lower], axis=0)
     three = 3 * ch1
     wide = 3 * ch2
     main = 7 * ch1
@@ -374,7 +420,7 @@
     sums_ref[main + groups + 1 : main + groups + 2, :ch2] = second[at : at + 1, ch2 : 2 * ch2]
 
 
-def inner(place, mid, raw, shifts, w1):
+def inner(place, mid, left, shifts, right, odd, even, w1):
     depth_z, rows, depth_y = mid.shape
     size = w1.shape[0] // 3
     ch1 = size // COLUMNS
@@ -383,51 +429,65 @@
     count = depth_z - 2
     return pl.pallas_call(
         inner_kernel,
-        in_specs=[pl.BlockSpec(memory_space=pltpu.SMEM)] + [vmem] * 4,
-        out_specs=(vmem,) * 4,
+        in_specs=[pl.BlockSpec(memory_space=pltpu.SMEM)] + [vmem] * 7,
+        out_specs=(vmem,) * 5,
         out_shape=(
+            jax.ShapeDtypeStruct(shifts.shape, BF16),
             jax.ShapeDtypeStruct((count * size, depth_y), BF16),
             jax.ShapeDtypeStruct((count * size, depth_y), BF16),
             jax.ShapeDtypeStruct((3 * rows, 6 * ch1), F32),
             jax.ShapeDtypeStruct((3 * size, 3 * ch2), F32),
         ),
-        scratch_shapes=[pltpu.VMEM((count * 6 * ch1, depth_y), BF16)],
+        scratch_shapes=[pltpu.VMEM((count * size, depth_y), F32), pltpu.VMEM((count * 6 * ch1, depth_y), BF16)],
         compiler_params=pltpu.CompilerParams(vmem_limit_bytes=VMEM_LIMIT),
         cost_estimate=pl.CostEstimate(flops=800_000_000, bytes_accessed=10_000_000, transcendentals=500_000),
         name="inner_levels",
-    )(place, mid, raw, shifts, w1)
-
-
-def edge(place, low, mid, high, ends, odd, even, shifts, w1, inner_hidden, first, second):
+    )(place, mid, left, shifts, right, odd, even, w1)
+
+
+def edge(place, mid, high, wide, odd, even, shifts, w1, first, second):
     _, rows, depth_y = mid.shape
     size = w1.shape[0] // 3
     ch1 = size // COLUMNS
     vmem = pl.BlockSpec(memory_space=pltpu.VMEM)
     return pl.pallas_call(
         edge_kernel,
-        in_specs=[pl.BlockSpec(memory_space=pltpu.SMEM)] + [vmem] * 11,
+        in_specs=[pl.BlockSpec(memory_space=pltpu.SMEM)] + [vmem] * 9,
         out_specs=(vmem,) * 3,
         out_shape=(
-            jax.ShapeDtypeStruct((4 * size, depth_y), BF16),
-            jax.ShapeDtypeStruct((4 * size, depth_y), BF16),
+            jax.ShapeDtypeStruct((2 * size, depth_y), BF16),
+            jax.ShapeDtypeStruct((2 * size, depth_y), BF16),
             jax.ShapeDtypeStruct((8 * ch1, 128), F32),
         ),
-        scratch_shapes=[pltpu.VMEM((4 * 6 * ch1, depth_y), BF16), pltpu.VMEM((3 * rows, 3 * ch1), F32)],
+        scratch_shapes=[
+            pltpu.VMEM((size, depth_y), BF16),
+            pltpu.VMEM((3 * 6 * ch1, depth_y), BF16),
+            pltpu.VMEM((3 * rows, 3 * ch1), F32),
+        ],
         compiler_params=pltpu.CompilerParams(vmem_limit_bytes=VMEM_LIMIT),
         name="edge_levels_and_sums",
-    )(place, low, mid, high, ends, odd, even, shifts, w1, inner_hidden, first, second)
+    )(place, mid, high, wide, odd, even, shifts, w1, first, second)
 
 
 def last_kernel(
+    place_ref,
+    low_ref,
+    mid_ref,
+    wide_ref,
+    w1_ref,
+    odd_ref,
+    even_ref,
     hidden_ref,
+    grad_ref,
     hidden_edge_ref,
-    grad_ref,
     grad_edge_ref,
     k1_ref,
     k2_ref,
     b2_ref,
     feat_ref,
     gin_ref,
+    hidden_low_ref,
+    grad_low_ref,
     featw_ref,
     ginw_ref,
     turned_ref,
@@ -435,19 +495,41 @@
 ):
     ch2, depth_q, half_y = feat_ref.shape
     c_in, _, depth_y = gin_ref.shape
-    depth_z = 2 * depth_q
-    size = hidden_edge_ref.shape[0] // 4
-    places = {-1: 0, 0: 1, depth_z - 1: 2, depth_z: 3}
-
-    def level(inner_ref, edge_ref, z):
-        if z in places:
-            return edge_ref[places[z] * size : (places[z] + 1) * size, :]
-        return inner_ref[(z - 1) * size : z * size, :]
-
-    def window(inner_ref, edge_ref, z):
-        return jnp.concatenate([level(inner_ref, edge_ref, z + a) for a in (-1, 0, 1)], axis=0)
-
+    depth_z, rows, _ = mid_ref.shape
+    size = hidden_edge_ref.shape[0] // 2
     ch1 = size // COLUMNS
+
+    def plane(z):
+        return low_ref[(z + 2) * rows : (z + 3) * rows, :] if z < 0 else mid_ref[z]
+
+    below, here = rim_columns(low_ref, odd_plane, 2 * rows), wide_ref[: 3 * ch2, :]
+    raws = {
+        -1: unspread(mm(odd_ref[...], jnp.concatenate([below, here], axis=0))),
+        0: unspread(mm(even_ref[...], here)),
+    }
+
+    def store(z, hidden, grad):
+        store_level(hidden_low_ref, grad_low_ref, z + 1, hidden, grad, ch1)
+
+    activate([[-1, 0]], plane, lambda z: raws[z], place_ref, w1_ref, depth_z, store)
+
+    def hidden(z):
+        if z < 1:
+            return hidden_low_ref[(z + 1) * size : (z + 2) * size, :]
+        if z < depth_z - 1:
+            return hidden_ref[(z - 1) * size : z * size, :]
+        return hidden_edge_ref[(z - depth_z + 1) * size : (z - depth_z + 2) * size, :]
+
+    def grad(z):
+        if z < 1:
+            return grad_low_ref[(z + 1) * size : (z + 2) * size, :]
+        if z < depth_z - 1:
+            return grad_ref[(z - 1) * size : z * size, :]
+        return grad_edge_ref[(z - depth_z + 1) * size : (z - depth_z + 2) * size, :]
+
+    def window(level, z):
+        return jnp.concatenate([level(z + a) for a in (-1, 0, 1)], axis=0)
+
     turned_ref[...] = jnp.zeros_like(turned_ref)
     w4_ref[...] = jnp.zeros_like(w4_ref)
     for a in range(3):
@@ -470,7 +552,7 @@
     ).astype(F32).astype(BF16)
 
     for q in range(0, depth_q, 2):
-        source = lanes([window(hidden_ref, hidden_edge_ref, 2 * k) for k in (q, q + 1)])
+        source = lanes([window(hidden, 2 * k) for k in (q, q + 1)])
         products = mm(w2, source)
         for n in range(2):
             terms = products[:, n * depth_y : (n + 1) * depth_y]
@@ -480,7 +562,7 @@
 
     two = 2 * c_in
     for z in range(0, depth_z, 2):
-        source = lanes([window(grad_ref, grad_edge_ref, k) for k in (z, z + 1)])
+        source = lanes([window(grad, k) for k in (z, z + 1)])
         products = mm(w4, source)
         for n in range(2):
             terms = products[:, n * depth_y : (n + 1) * depth_y]
@@ -491,20 +573,24 @@
     gin_ref[...] = ginw_ref[...].reshape(gin_ref.shape).astype(BF16)
 
 
-def last(hidden, hidden_edge, grad, grad_edge, k1, k2, b2):
-    depth_y = hidden.shape[1]
-    size = hidden_edge.shape[0] // 4
+def last(place, low, mid, wide, w1, odd, even, inner_values, edge_values, k1, k2, b2):
+    depth_z, _, depth_y = mid.shape
     _, c_in, ch1 = k1.shape
     ch2 = k2.shape[2]
-    depth_z = hidden.shape[0] // size + 2
+    size = COLUMNS * ch1
     depth_q = depth_z // 2
+    vmem = pl.BlockSpec(memory_space=pltpu.VMEM)
     return pl.pallas_call(
         last_kernel,
+        in_specs=[pl.BlockSpec(memory_space=pltpu.SMEM)] + [vmem] * 13,
+        out_specs=(vmem, vmem),
         out_shape=(
             jax.ShapeDtypeStruct((ch2, depth_q, depth_y // 2), BF16),
             jax.ShapeDtypeStruct((c_in, 2 * depth_z, depth_y), BF16),
         ),
         scratch_shapes=[
+            pltpu.VMEM((2 * size, depth_y), BF16),
+            pltpu.VMEM((2 * size, depth_y), BF16),
             pltpu.VMEM((ch2 * depth_q, depth_y // 2), F32),
             pltpu.VMEM((c_in * 2 * depth_z, depth_y), F32),
             pltpu.VMEM((3 * size, 128), F32),
@@ -513,7 +599,7 @@
         compiler_params=pltpu.CompilerParams(vmem_limit_bytes=VMEM_LIMIT),
         cost_estimate=pl.CostEstimate(flops=800_000_000, bytes_accessed=10_000_000, transcendentals=0),
         name="features_and_input_grad",
-    )(hidden, hidden_edge, grad, grad_edge, k1, k2, b2)
+    )(place, low, mid, wide, w1, odd, even, *inner_values, *edge_values, k1, k2, b2)
 
 
 def unpack_kernel(sums_ref, first_ref, second_ref, bias1_ref, bias2_ref, *, scale):
@@ -544,6 +630,7 @@
     )
     first, second, bias1, bias2 = pl.pallas_call(
         functools.partial(unpack_kernel, scale=scale),
+        in_specs=[pl.BlockSpec(memory_space=pltpu.VMEM)],
         out_shape=(first, second, bias1, bias2),
         name="unpack_sums",
     )(sums)
@@ -552,19 +639,12 @@
     return first, bias1[0], second, bias2[0]
 
 
-def total_over_devices(sums):
-    slabs, tiles = lax.axis_size("gz"), lax.axis_size("xy")
-
-    def exchange(value, axis):
-        return lax.all_to_all(value, axis, 0, 0, tiled=True)
-
-    def copies(value, count):
-        return jnp.broadcast_to(value[None], (count,) + value.shape)
-
-    part = exchange(sums.reshape(slabs, -1, sums.shape[1]), "gz").sum(0).astype(BF16)
-    part = exchange(copies(part, tiles), "xy").astype(F32).sum(0)
-    parts = exchange(copies(part, slabs), "gz")
-    return parts.reshape(sums.shape)
+def exchange(value, axis):
+    return lax.all_to_all(value, axis, 0, 0, tiled=True)
+
+
+def copies(value, count):
+    return jnp.broadcast_to(value[None], (count,) + value.shape)
 
 
 def shards(loaded_planes, first_kernel, first_bias, second_kernel, second_bias, cotangent):
@@ -582,19 +662,26 @@
     mid = lax.all_to_all(windows, "xy", split_axis=0, concat_axis=0, tiled=True)
 
     cot = cotangent.reshape(ch2, depth_z // 2, depth_y // 2)
-    left, right = shifted(cot, "xy", 1), shifted(cot, "xy", -1)
-    raw, shifts, ends, w1, odd, even = prep(left, cot, right, k1, first_bias[None], k2)
+    shifts, pairs, w1, odd, even = prepare_own(cot, k1, first_bias[None], k2)
+    left, right = shifted(pairs, "xy", 1), shifted(pairs, "xy", -1)
+    mid, left, right = lax.optimization_barrier((mid, left, right))
 
     rows = mid.shape[1]
-    upward = jnp.concatenate([mid[-2:].reshape(2 * rows, depth_y), ends[3 * ch2 :]], axis=0)
-    downward = jnp.concatenate([mid[:2].reshape(2 * rows, depth_y), ends[: 3 * ch2]], axis=0)
-    low, high = shifted(upward, "gz", 1), shifted(downward, "gz", -1)
-    hidden, grad, first, second = inner(place, mid, raw, shifts, w1)
-    hidden_edge, grad_edge, sums = edge(
-        place, low, mid, high, ends, odd, even, shifts, w1, hidden, first, second
+    downward = [mid[:2].reshape(2 * rows, depth_y), left[:ch2], shifts[ch2 : 2 * ch2], right[:ch2]]
+    high = shifted(jnp.concatenate(downward, axis=0), "gz", -1)
+    wide, *inner_values, first, second = inner(place, mid, left, shifts, right, odd, even, w1)
+    *edge_values, sums = edge(place, mid, high, wide, odd, even, shifts, w1, first, second)
+
+    part = exchange(sums.reshape(slabs, -1, sums.shape[1]), "gz").sum(0).astype(BF16)
+    upward = [mid[-2:].reshape(2 * rows, depth_y), left[-ch2:], shifts[-2 * ch2 : -ch2], right[-ch2:]]
+    part, upward = lax.optimization_barrier((part, jnp.concatenate(upward, axis=0)))
+    low = shifted(upward, "gz", 1)
+    part = exchange(copies(part, tiles), "xy").astype(F32).sum(0)
+    part, low = lax.optimization_barrier((part, low))
+    sums = exchange(copies(part, slabs), "gz").reshape(sums.shape)
+    features, input_grad = last(
+        place, low, mid, wide, w1, odd, even, inner_values, edge_values, k1, k2, second_bias[None]
     )
-    sums = total_over_devices(sums)
-    features, input_grad = last(hidden, hidden_edge, grad, grad_edge, k1, k2, second_bias[None])
     scale = 1.0 / math.sqrt(slabs * depth_z * width * depth_y)
     first_grad, first_bias_grad, second_grad, second_bias_grad = unpack(sums, scale, channels, ch1, ch2)
     return (

time: 92.9 us -> 87.6 us (0.943)
  blocking collectives: 31.2 us -> 0 us
  starting transfers between devices: 36.4 us -> 49.1 us
  waiting for transfers between devices: 11.6 us -> 22.9 us
  Pallas kernels: 8.81 us -> 10.2 us
    all_to_all x2 -> x0, blocking collectives: 31.2 us -> none  [exchange(): return lax.all_to_all(value, axis, 0, 0, tiled=True)]
    all_to_all x1 -> x3, starting transfers between devices: 5.16 us -> 19.1 us  [exchange(): return lax.all_to_all(value, axis, 0, 0, tiled=True)]
    all_to_all x1 -> x3, waiting for transfers between devices: 2.91 us -> 16.5 us  [exchange(): return lax.all_to_all(value, axis, 0, 0, tiled=True)]
    ppermute x4, waiting for transfers between devices: 6.72 us -> 2.28 us  [shifted(): lax.ppermute(value, axis, [(source, source + steps) for source in range(f...]
    all_to_all x1, waiting for transfers between devices: 1.95 us -> 4.11 us  [shards(): mid = lax.all_to_all(windows, 'xy', split_axis=0, concat_axis=0, tiled=True)]
    ppermute x4, starting transfers between devices: 14.6 us -> 13.3 us  [shifted(): lax.ppermute(value, axis, [(source, source + steps) for source in range(f...]
  transfers between devices with their start and end apart: 6 -> 8, of which waited for: 5 -> 6; matrix products, arithmetic and copies ran while one was open for 0% -> 0% of each run, Pallas kernels for 6% -> 7%
where the time goes in v3:
time: 87.6 us; the launch traced here: 87.1 us
  starting transfers between devices  49.1 us (56%)
  waiting for transfers between devices  22.9 us (26%)
  Pallas kernels  10.2 us (12%)
  local copies, waits for them, and re-layouts  4.02 us (5%)
    all_to_all x3, starting transfers between devices, exchange(): return lax.all_to_all(value, axis, 0, 0, tiled=True)  19.1 us
    all_to_all x1, starting transfers between devices, shards(): mid = lax.all_to_all(windows, 'xy', split_axis=0, concat_axis=0, tiled=True)  16.6 us
    all_to_all x3, waiting for transfers between devices, exchange(): return lax.all_to_all(value, axis, 0, 0, tiled=True)  16.5 us
    ppermute x4, starting transfers between devices, shifted(): lax.ppermute(value, axis, [(source, source + steps) for source in range(f...  13.3 us
    all_to_all x1, waiting for transfers between devices, shards(): mid = lax.all_to_all(windows, 'xy', split_axis=0, concat_axis=0, tiled=True)  4.11 us
    pallas_call x1, Pallas kernels, last(): pl.pallas_call(last_kernel, in_specs=[pl.BlockSpec(memory_space=pltpu.SME...  3.09 us
    unnamed x14, local copies, waits for them, and re-layouts  2.74 us
    pallas_call x1, Pallas kernels, inner(): pl.pallas_call(inner_kernel, in_specs=[pl.BlockSpec(memory_space=pltpu.SM...  2.35 us
  transfers between devices with their start and end apart: 8, of which 6 were waited for; matrix products, arithmetic and copies ran while one was open for 0% of the time, Pallas kernels for 7%

profile of v3, /device:TPU:1, one launch (start us, length us, event | category | flops | bytes accessed | tf_op | source)
XLA Modules:
  0.0 87.1 jit_solution(12788034272569902618)
XLA Ops:
  0.6 0.0 copy-start
  0.6 0.8 copy-done
  1.5 0.7 pack_windows.1
  2.2 0.0 copy-start.1
  2.2 0.0 copy-start.2
  2.2 0.0 copy-start.3
  2.2 16.6 %all-to-all-start = ((bf16[32,32,128]{2,1,0:T(8,128)(2,1)}), bf16[32,32,128]{2,1,0:T(8,128)(2,1)S(1)}, u32[]{:S(2)}, u32[]{:S(2)}) async-start(bf16[32,32,128]{2,1,0:T(8,128)(2,1)} %pack_windows.1), calls=%async_computation | async-start | bytes 524288 | tf_op jit(solution)/shard_map/all_to_all | solution.py:662
  18.9 0.0 copy-start.4
  18.9 0.0 copy-done.1
  18.9 0.0 copy-done.2
  18.9 0.0 copy-done.3
  18.9 0.6 copy-done.4
  19.5 0.4 spread_cotangent.1
  19.9 1.3 %collective-permute-start.1 = (bf16[256,128]{1,0:T(8,128)(2,1)S(1)}, bf16[256,128]{1,0:T(8,128)(2,1)S(1)}, u32[]{:S(2)}, u32[]{:S(2)}) collective-permute-start(bf16[256,128]{1,0:T(8,128)(2,1)S(1)} %get-tuple-element.32), channel_id=1, source_target_pairs={{1,0},{2,1},{3,2},{4,3},{5,4},{6,5},{7,6},{8,7},{9,8},{10,9},{11,1... | collective-permute-start | bytes 196616 | tf_op jit(solution)/shard_map/ppermute | solution.py:21
  21.2 4.0 %collective-permute-start = (bf16[256,128]{1,0:T(8,128)(2,1)S(1)}, bf16[256,128]{1,0:T(8,128)(2,1)S(1)}, u32[]{:S(2)}, u32[]{:S(2)}) collective-permute-start(bf16[256,128]{1,0:T(8,128)(2,1)S(1)} %get-tuple-element.32), channel_id=1, source_target_pairs={{0,1},{1,2},{2,3},{3,4},{4,5},{5,6},{6,7},{7,8},{8,9},{9,10},{10,1... | collective-permute-start | bytes 196616 | tf_op jit(solution)/shard_map/ppermute | solution.py:21
  25.3 0.1 add_convert_fusion.place_ref
  25.3 1.9 %collective-permute-done.1.right_ref = bf16[256,128]{1,0:T(8,128)(2,1)S(1)} collective-permute-done((bf16[256,128]{1,0:T(8,128)(2,1)S(1)}, bf16[256,128]{1,0:T(8,128)(2,1)S(1)}, u32[]{:S(2)}, u32[]{:S(2)}) %collective-permute-start.1) | collective-permute-done | bytes 65568 | tf_op jit(solution)/shard_map/ppermute | solution.py:21
  27.2 0.0 collective-permute-done.left_ref
  27.2 4.1 %all-to-all-done.mid_ref = bf16[32,32,128]{2,1,0:T(8,128)(2,1)S(1)} async-done(((bf16[32,32,128]{2,1,0:T(8,128)(2,1)}), bf16[32,32,128]{2,1,0:T(8,128)(2,1)S(1)}, u32[]{:S(2)}, u32[]{:S(2)}) %all-to-all-start) | async-done | bytes 262176 | tf_op jit(solution)/shard_map/all_to_all | solution.py:662
  31.3 5.3 %collective-permute-start.2 = (bf16[160,128]{1,0:T(8,128)(2,1)S(1)}, bf16[160,128]{1,0:T(8,128)(2,1)S(1)}, u32[]{:S(2)}, u32[]{:S(2)}) collective-permute-start(bf16[160,128]{1,0:T(8,128)(2,1)S(1)} %pad_maximum_fusion), channel_id=1, source_target_pairs={{32,0},{64,32},{96,64},{128,96},{160,128},{192,160},{224,192},{256... | collective-permute-start | bytes 122888 | tf_op jit(solution)/shard_map/ppermute | solution.py:21
  36.7 2.4 %inner_levels.1 = (bf16[1536,128]{1,0:T(8,128)(2,1)S(1)}, bf16[1920,128]{1,0:T(8,128)(2,1)S(1)}, bf16[1920,128]{1,0:T(8,128)(2,1)S(1)}, f32[96,96]{1,0:T(8,128)S(1)}, f32[192,96]{1,0:T(8,128)S(1)}) custom-call(s32[4]{0:T(128)S(1)} %add_convert_fusion.place_ref, bf16[32,32,128]{2,1,0:T(8,128)(2,1)S(1)} %all-to-all-done.mid_ref, ...), custom_call_target="tpu_custom_call" | custom-call | flops 800000000 | bytes 10000000 | tf_op jit(solution)/shard_map/inner_levels/pallas_call | solution.py:430
  39.0 0.4 collective-permute-done.2.high_ref
  39.4 1.9 %edge_levels_and_sums.1 = (bf16[128,128]{1,0:T(8,128)(2,1)S(1)}, bf16[128,128]{1,0:T(8,128)(2,1)S(1)}, f32[128,128]{1,0:T(8,128)}) custom-call(s32[4]{0:T(128)S(1)} %add_convert_fusion.place_ref, bf16[32,32,128]{2,1,0:T(8,128)(2,1)S(1)} %all-to-all-done.mid_ref, bf16[160,128]{1,0:T(8,128)(2,1)S(1)} %collective-permute-done.2.high_ref, ...), custom_call_target="tpu_custom_call" | custom-call | tf_op jit(solution)/shard_map/edge_levels_and_sums/pallas_call | solution.py:453
  41.3 5.0 %all-to-all-start.1 = ((f32[16,8,128]{2,1,0:T(8,128)}), f32[16,8,128]{2,1,0:T(8,128)S(1)}, u32[]{:S(2)}, u32[]{:S(2)}) async-start(f32[16,8,128]{2,1,0:T(8,128)} %bitcast.12), calls=%async_computation.1 | async-start | bytes 131072 | tf_op jit(solution)/shard_map/all_to_all | solution.py:643
  46.4 5.8 %all-to-all-done.1 = f32[16,8,128]{2,1,0:T(8,128)S(1)} async-done(((f32[16,8,128]{2,1,0:T(8,128)}), f32[16,8,128]{2,1,0:T(8,128)S(1)}, u32[]{:S(2)}, u32[]{:S(2)}) %all-to-all-start.1) | async-done | bytes 65568 | tf_op jit(solution)/shard_map/all_to_all | solution.py:643
  52.2 0.6 broadcast_in_dim.22
  52.9 8.9 %all-to-all-start.2 = ((bf16[32,8,128]{2,1,0:T(8,128)(2,1)}), bf16[32,8,128]{2,1,0:T(8,128)(2,1)S(1)}, u32[]{:S(2)}, u32[]{:S(2)}) async-start(bf16[32,8,128]{2,1,0:T(8,128)(2,1)} %broadcast_in_dim.22), calls=%async_computation.2 | async-start | bytes 131072 | tf_op jit(solution)/shard_map/all_to_all | solution.py:643
  61.8 2.8 %collective-permute-start.3 = (bf16[160,128]{1,0:T(8,128)(2,1)S(1)}, bf16[160,128]{1,0:T(8,128)(2,1)S(1)}, u32[]{:S(2)}, u32[]{:S(2)}) collective-permute-start(bf16[160,128]{1,0:T(8,128)(2,1)S(1)} %pad_maximum_fusion.1), channel_id=1, source_target_pairs={{0,32},{32,64},{64,96},{96,128},{128,160},{160,192},{192,224},{224... | collective-permute-start | bytes 122888 | tf_op jit(solution)/shard_map/ppermute | solution.py:21
  64.5 8.5 %all-to-all-done.2 = bf16[32,8,128]{2,1,0:T(8,128)(2,1)S(1)} async-done(((bf16[32,8,128]{2,1,0:T(8,128)(2,1)}), bf16[32,8,128]{2,1,0:T(8,128)(2,1)S(1)}, u32[]{:S(2)}, u32[]{:S(2)}) %all-to-all-start.2) | async-done | bytes 65568 | tf_op jit(solution)/shard_map/all_to_all | solution.py:643
  73.1 0.0 collective-permute-done.3.low_ref
  73.1 0.6 broadcast_in_dim.25
  73.7 5.2 %all-to-all-start.3 = ((f32[16,8,128]{2,1,0:T(8,128)}), f32[16,8,128]{2,1,0:T(8,128)S(1)}, u32[]{:S(2)}, u32[]{:S(2)}) async-start(f32[16,8,128]{2,1,0:T(8,128)} %broadcast_in_dim.25), calls=%async_computation.3 | async-start | bytes 131072 | tf_op jit(solution)/shard_map/all_to_all | solution.py:643
  78.9 0.0 copy-start.5
  78.9 0.6 copy-done.5
  79.5 3.1 %features_and_input_grad.1 = (bf16[32,16,64]{2,1,0:T(8,128)(2,1)}, bf16[4,64,128]{2,1,0:T(8,128)(2,1)}) custom-call(s32[4]{0:T(128)S(1)} %add_convert_fusion.place_ref, bf16[160,128]{1,0:T(8,128)(2,1)S(1)} %collective-permute-done.3.low_ref, bf16[32,32,128]{2,1,0:T(8,128)(2,1)S(1)} %all-to-all-done.mid_ref, ...), custom_call_target="tpu_custom_call" | custom-call | flops 800000000 | bytes 10000000 | tf_op jit(solution)/shard_map/features_and_input_grad/pallas_call | solution.py:583
  82.6 2.1 %all-to-all-done.3 = f32[16,8,128]{2,1,0:T(8,128)S(1)} async-done(((f32[16,8,128]{2,1,0:T(8,128)}), f32[16,8,128]{2,1,0:T(8,128)S(1)}, u32[]{:S(2)}, u32[]{:S(2)}) %all-to-all-start.3) | async-done | bytes 65568 | tf_op jit(solution)/shard_map/all_to_all | solution.py:643
  84.8 0.0 copy-start.6
  84.8 0.6 copy-done.6
  85.4 1.7 %unpack_sums.1 = (f32[27,4,16]{2,1,0:T(4,128)}, f32[27,16,32]{2,1,0:T(8,128)}, f32[1,16]{1,0:T(1,128)}, f32[1,32]{1,0:T(1,128)}) custom-call(f32[128,128]{1,0:T(8,128)} %bitcast.38), custom_call_target="tpu_custom_call" | custom-call | tf_op jit(solution)/shard_map/unpack_sums/pallas_call | solution.py:631
  (7 shorter events, 0.1 us)
Async XLA Ops:
  0.6 0.8 copy-start
  2.2 16.7 %copy-start.1 = (bf16[32,16,1,64]{3,1,2,0:T(8,128)(2,1)S(1)}, bf16[32,16,1,64]{3,1,2,0:T(8,128)(2,1)}, u32[]{:S(2)}) copy-start(bf16[32,16,1,64]{3,1,2,0:T(8,128)(2,1)} %param.11) | copy-start | bytes 196612
  2.2 16.7 %copy-start.2 = (bf16[32,16,3,3,3]{0,1,4,3,2:T(8,128)(2,1)S(1)}, bf16[32,16,3,3,3]{0,1,4,3,2:T(8,128)(2,1)}, u32[]{:S(2)}) copy-start(bf16[32,16,3,3,3]{0,1,4,3,2:T(8,128)(2,1)} %param.9) | copy-start | bytes 82948
  2.2 16.7 %copy-start.3 = (bf16[16,4,3,3,3]{0,1,4,3,2:T(4,128)(2,1)S(1)}, bf16[16,4,3,3,3]{0,1,4,3,2:T(4,128)(2,1)}, u32[]{:S(2)}) copy-start(bf16[16,4,3,3,3]{0,1,4,3,2:T(4,128)(2,1)} %param.7) | copy-start | bytes 10372
  2.2 29.1 %all-to-all-start = ((bf16[32,32,128]{2,1,0:T(8,128)(2,1)}), bf16[32,32,128]{2,1,0:T(8,128)(2,1)S(1)}, u32[]{:S(2)}, u32[]{:S(2)}) async-start(bf16[32,32,128]{2,1,0:T(8,128)(2,1)} %pack_windows.1), calls=%async_computation | async-start | bytes 524288 | tf_op jit(solution)/shard_map/all_to_all | solution.py:662
  18.9 0.7 copy-start.4
  19.9 7.3 %collective-permute-start.1 = (bf16[256,128]{1,0:T(8,128)(2,1)S(1)}, bf16[256,128]{1,0:T(8,128)(2,1)S(1)}, u32[]{:S(2)}, u32[]{:S(2)}) collective-permute-start(bf16[256,128]{1,0:T(8,128)(2,1)S(1)} %get-tuple-element.32), channel_id=1, source_target_pairs={{1,0},{2,1},{3,2},{4,3},{5,4},{6,5},{7,6},{8,7},{9,8},{10,9},{11,1... | collective-permute-start | bytes 196616 | tf_op jit(solution)/shard_map/ppermute | solution.py:21
  21.2 6.0 %collective-permute-start = (bf16[256,128]{1,0:T(8,128)(2,1)S(1)}, bf16[256,128]{1,0:T(8,128)(2,1)S(1)}, u32[]{:S(2)}, u32[]{:S(2)}) collective-permute-start(bf16[256,128]{1,0:T(8,128)(2,1)S(1)} %get-tuple-element.32), channel_id=1, source_target_pairs={{0,1},{1,2},{2,3},{3,4},{4,5},{5,6},{6,7},{7,8},{8,9},{9,10},{10,1... | collective-permute-start | bytes 196616 | tf_op jit(solution)/shard_map/ppermute | solution.py:21
  31.3 8.1 %collective-permute-start.2 = (bf16[160,128]{1,0:T(8,128)(2,1)S(1)}, bf16[160,128]{1,0:T(8,128)(2,1)S(1)}, u32[]{:S(2)}, u32[]{:S(2)}) collective-permute-start(bf16[160,128]{1,0:T(8,128)(2,1)S(1)} %pad_maximum_fusion), channel_id=1, source_target_pairs={{32,0},{64,32},{96,64},{128,96},{160,128},{192,160},{224,192},{256... | collective-permute-start | bytes 122888 | tf_op jit(solution)/shard_map/ppermute | solution.py:21
  41.3 10.9 %all-to-all-start.1 = ((f32[16,8,128]{2,1,0:T(8,128)}), f32[16,8,128]{2,1,0:T(8,128)S(1)}, u32[]{:S(2)}, u32[]{:S(2)}) async-start(f32[16,8,128]{2,1,0:T(8,128)} %bitcast.12), calls=%async_computation.1 | async-start | bytes 131072 | tf_op jit(solution)/shard_map/all_to_all | solution.py:643
  52.9 20.2 %all-to-all-start.2 = ((bf16[32,8,128]{2,1,0:T(8,128)(2,1)}), bf16[32,8,128]{2,1,0:T(8,128)(2,1)S(1)}, u32[]{:S(2)}, u32[]{:S(2)}) async-start(bf16[32,8,128]{2,1,0:T(8,128)(2,1)} %broadcast_in_dim.22), calls=%async_computation.2 | async-start | bytes 131072 | tf_op jit(solution)/shard_map/all_to_all | solution.py:643
  61.8 11.3 %collective-permute-start.3 = (bf16[160,128]{1,0:T(8,128)(2,1)S(1)}, bf16[160,128]{1,0:T(8,128)(2,1)S(1)}, u32[]{:S(2)}, u32[]{:S(2)}) collective-permute-start(bf16[160,128]{1,0:T(8,128)(2,1)S(1)} %pad_maximum_fusion.1), channel_id=1, source_target_pairs={{0,32},{32,64},{64,96},{96,128},{128,160},{160,192},{192,224},{224... | collective-permute-start | bytes 122888 | tf_op jit(solution)/shard_map/ppermute | solution.py:21
  73.7 11.1 %all-to-all-start.3 = ((f32[16,8,128]{2,1,0:T(8,128)}), f32[16,8,128]{2,1,0:T(8,128)S(1)}, u32[]{:S(2)}, u32[]{:S(2)}) async-start(f32[16,8,128]{2,1,0:T(8,128)} %broadcast_in_dim.25), calls=%async_computation.3 | async-start | bytes 131072 | tf_op jit(solution)/shard_map/all_to_all | solution.py:643
  78.9 0.7 copy-start.5
  84.8 0.6 copy-start.6

commit v4 on v3

--- a/solution.py
+++ b/solution.py
@@ -126,7 +126,53 @@
     return even_plane(from_right(pair))
 
 
-def own_kernel(mid_ref, k1_ref, b1_ref, k2_ref, shifts_ref, pairs_ref, w1_ref, odd_ref, even_ref, flat_ref, turned_ref):
+def second_matrix(kernel_ref, bias_ref, turned_ref):
+    _, ch1, ch2 = kernel_ref.shape
+    size = COLUMNS * ch1
+    turned_ref[...] = jnp.zeros_like(turned_ref)
+    for a in range(3):
+        for b in range(3):
+            for c in range(3):
+                at = a * size + b * ch1
+                turned_ref[at : at + ch1, c * ch2 : (c + 1) * ch2] = kernel_ref[9 * a + 3 * b + c].astype(F32)
+    for n, part in enumerate(split_bias(bias_ref[...])):
+        row = size + 3 * ch1 + n
+        turned_ref[row : row + 1, ch2 : 2 * ch2] = part
+    return turned_ref[...].T[: 3 * ch2].astype(BF16)
+
+
+def back_matrix(kernel_ref, flat_ref):
+    _, c_in, ch1 = kernel_ref.shape
+    size = COLUMNS * ch1
+    flat_ref[...] = jnp.zeros_like(flat_ref)
+    for a in range(3):
+        for b in range(3):
+            for c in range(3):
+                for x in range(2):
+                    down, right = (c * 2 + x) * c_in, (2 - a) * size + (x + 2 - b) * ch1
+                    block = kernel_ref[9 * a + 3 * b + c].astype(F32)
+                    flat_ref[down : down + c_in, right : right + ch1] = block
+    return flat_ref[...].astype(BF16)
+
+
+def own_kernel(
+    mid_ref,
+    k1_ref,
+    b1_ref,
+    k2_ref,
+    b2_ref,
+    shifts_ref,
+    pairs_ref,
+    w1_ref,
+    odd_ref,
+    even_ref,
+    w2_ref,
+    w4_ref,
+    flat_ref,
+    turned_ref,
+    turned2_ref,
+    flat4_ref,
+):
     ch2, cells, half_y = mid_ref.shape
     rows = 3 * ch2
     depth_y = 2 * half_y
@@ -148,9 +194,11 @@
     spread_matrix(k2_ref, odd_ref, 0, 2, 0)
     spread_matrix(k2_ref, odd_ref, 0, 0, rows)
     spread_matrix(k2_ref, even_ref, 0, 1, 0)
-
-
-def prepare_own(mid, k1, b1, k2):
+    w2_ref[...] = second_matrix(k2_ref, b2_ref, turned2_ref)
+    w4_ref[...] = back_matrix(k1_ref, flat4_ref)
+
+
+def prepare_own(mid, k1, b1, k2, b2):
     ch2, cells, half_y = mid.shape
     _, c_in, ch1 = k1.shape
     depth_y = 2 * half_y
@@ -163,34 +211,31 @@
             jax.ShapeDtypeStruct((3 * size, 3 * c_in * WINDOW), BF16),
             jax.ShapeDtypeStruct((3 * size, 2 * rows), BF16),
             jax.ShapeDtypeStruct((3 * size, rows), BF16),
+            jax.ShapeDtypeStruct((rows, 3 * size), BF16),
+            jax.ShapeDtypeStruct((6 * c_in, 3 * size), BF16),
         ),
         scratch_shapes=[
             pltpu.VMEM((ch2 * cells, half_y), F32),
             pltpu.VMEM((2, 3 * c_in * WINDOW, 128), F32),
+            pltpu.VMEM((3 * size, 128), F32),
+            pltpu.VMEM((6 * c_in, 3 * size), F32),
         ],
         compiler_params=pltpu.CompilerParams(vmem_limit_bytes=VMEM_LIMIT),
         cost_estimate=pl.CostEstimate(flops=100_000_000, bytes_accessed=2_000_000, transcendentals=0),
         name="spread_cotangent",
-    )(mid, k1, b1, k2)
-
-
-def spread_columns(left_ref, shifts_ref, right_ref, wide_ref, cells):
+    )(mid, k1, b1, k2, b2)
+
+
+def spread_columns(shifts_ref, right_ref, wide_ref, cells):
     rows = wide_ref.shape[0] // cells
     ch2 = rows // 3
     for k in range(cells // 2):
-        sides = [ref[k * ch2 : (k + 1) * ch2, :].astype(F32) for ref in (left_ref, right_ref)]
-        for n, plane in enumerate((even_plane, odd_plane)):
+        pair = right_ref[k * ch2 : (k + 1) * ch2, :].astype(F32)
+        for n, plane in enumerate((even_plane(pair), odd_plane(pair))):
             at = (2 * k + n) * rows
-            wide_ref[at : at + ch2, :] = plane(sides[0]).astype(BF16)
+            wide_ref[at : at + ch2, :] = jnp.zeros((ch2, pair.shape[1]), BF16)
             wide_ref[at + ch2 : at + 2 * ch2, :] = shifts_ref[at + ch2 : at + 2 * ch2, :]
-            wide_ref[at + 2 * ch2 : at + rows, :] = plane(sides[1]).astype(BF16)
-
-
-def rim_columns(ref, plane, first_row):
-    ch2 = (ref.shape[0] - first_row) // 3
-    left, own, right = (ref[first_row + k * ch2 : first_row + (k + 1) * ch2, :] for k in range(3))
-    left, right = (plane(pair.astype(F32)).astype(BF16) for pair in (left, right))
-    return jnp.concatenate([left, own, right], axis=0)
+            wide_ref[at + 2 * ch2 : at + rows, :] = plane.astype(BF16)
 
 
 def raw_levels(wide_ref, odd_ref, even_ref, raw_ref, cells):
@@ -231,7 +276,8 @@
             if z == depth_z:
                 keep = inside * jnp.where(at_last_z != 0, 0.0, 1.0)
             kept = sigma * keep
-            store(z, (pre * kept)[: 3 * ch1], raw(z) * (kept * (1.0 + pre * (1.0 - sigma))))
+            slope = kept * (1.0 + pre * (1.0 - sigma))
+            store(z, (pre * kept)[: 3 * ch1], raw(z) * slope, slope)
 
 
 def side_by_side(grad, ch1):
@@ -263,7 +309,6 @@
 def inner_kernel(
     place_ref,
     mid_ref,
-    left_ref,
     shifts_ref,
     right_ref,
     odd_ref,
@@ -272,6 +317,7 @@
     wide_ref,
     hidden_ref,
     grad_ref,
+    slope_ref,
     first_ref,
     second_ref,
     raw_ref,
@@ -283,11 +329,12 @@
     levels = list(range(1, depth_z - 1))
     six = 6 * ch1
     three = shifts_ref.shape[0] // (depth_z // 2)
-    spread_columns(left_ref, shifts_ref, right_ref, wide_ref, depth_z // 2)
+    spread_columns(shifts_ref, right_ref, wide_ref, depth_z // 2)
     raw_levels(wide_ref, odd_ref, even_ref, raw_ref, depth_z // 2)
 
-    def store(z, hidden, grad):
+    def store(z, hidden, grad, slope):
         store_level(hidden_ref, grad_ref, z - 1, hidden, grad, ch1)
+        slope_ref[(z - 1) * ch1 : z * ch1, :] = slope[:ch1]
         moved_ref[(z - 1) * six : z * six, :] = side_by_side(grad, ch1)
 
     def plane(z):
@@ -335,6 +382,7 @@
     second_ref,
     hidden_ref,
     grad_ref,
+    slope_ref,
     sums_ref,
     begin_ref,
     moved_ref,
@@ -347,7 +395,8 @@
     spread_rows = wide_ref.shape[0] // cells
     ch2 = spread_rows // 3
     end = wide_ref[(cells - 1) * spread_rows :, :]
-    above = rim_columns(high_ref, even_plane, 2 * rows)
+    right = even_plane(high_ref[2 * rows + ch2 :, :].astype(F32)).astype(BF16)
+    above = jnp.concatenate([jnp.zeros((ch2, depth_y), BF16), high_ref[2 * rows : 2 * rows + ch2, :], right], axis=0)
     even = mm(even_ref[...], lanes([wide_ref[:spread_rows, :], above]))
     raws = {
         0: unspread(even[:, :depth_y]),
@@ -364,10 +413,11 @@
             return high_ref[(z - depth_z) * rows : (z - depth_z + 1) * rows, :]
         return mid_ref[z]
 
-    def store(z, hidden, grad):
+    def store(z, hidden, grad, slope):
         at = places[z]
         if z > 0:
             store_level(hidden_ref, grad_ref, at, hidden, grad, ch1)
+            slope_ref[at * ch1 : (at + 1) * ch1, :] = slope[:ch1]
         else:
             begin_ref[: 3 * ch1, :] = hidden.astype(BF16)
             begin_ref[3 * ch1 :, :] = jnp.ones((ch1, depth_y), BF16)
@@ -420,7 +470,7 @@
     sums_ref[main + groups + 1 : main + groups + 2, :ch2] = second[at : at + 1, ch2 : 2 * ch2]
 
 
-def inner(place, mid, left, shifts, right, odd, even, w1):
+def inner(place, mid, shifts, right, odd, even, w1):
     depth_z, rows, depth_y = mid.shape
     size = w1.shape[0] // 3
     ch1 = size // COLUMNS
@@ -429,20 +479,21 @@
     count = depth_z - 2
     return pl.pallas_call(
         inner_kernel,
-        in_specs=[pl.BlockSpec(memory_space=pltpu.SMEM)] + [vmem] * 7,
-        out_specs=(vmem,) * 5,
+        in_specs=[pl.BlockSpec(memory_space=pltpu.SMEM)] + [vmem] * 6,
+        out_specs=(vmem,) * 6,
         out_shape=(
             jax.ShapeDtypeStruct(shifts.shape, BF16),
             jax.ShapeDtypeStruct((count * size, depth_y), BF16),
             jax.ShapeDtypeStruct((count * size, depth_y), BF16),
+            jax.ShapeDtypeStruct((count * ch1, depth_y), F32),
             jax.ShapeDtypeStruct((3 * rows, 6 * ch1), F32),
             jax.ShapeDtypeStruct((3 * size, 3 * ch2), F32),
         ),
         scratch_shapes=[pltpu.VMEM((count * size, depth_y), F32), pltpu.VMEM((count * 6 * ch1, depth_y), BF16)],
         compiler_params=pltpu.CompilerParams(vmem_limit_bytes=VMEM_LIMIT),
-        cost_estimate=pl.CostEstimate(flops=800_000_000, bytes_accessed=10_000_000, transcendentals=500_000),
+        cost_estimate=pl.CostEstimate(flops=0, bytes_accessed=0, transcendentals=0),
         name="inner_levels",
-    )(place, mid, left, shifts, right, odd, even, w1)
+    )(place, mid, shifts, right, odd, even, w1)
 
 
 def edge(place, mid, high, wide, odd, even, shifts, w1, first, second):
@@ -453,10 +504,11 @@
     return pl.pallas_call(
         edge_kernel,
         in_specs=[pl.BlockSpec(memory_space=pltpu.SMEM)] + [vmem] * 9,
-        out_specs=(vmem,) * 3,
+        out_specs=(vmem,) * 4,
         out_shape=(
             jax.ShapeDtypeStruct((2 * size, depth_y), BF16),
             jax.ShapeDtypeStruct((2 * size, depth_y), BF16),
+            jax.ShapeDtypeStruct((2 * ch1, depth_y), F32),
             jax.ShapeDtypeStruct((8 * ch1, 128), F32),
         ),
         scratch_shapes=[
@@ -473,45 +525,88 @@
     place_ref,
     low_ref,
     mid_ref,
+    high_ref,
+    left_ref,
+    corner_ref,
     wide_ref,
     w1_ref,
     odd_ref,
     even_ref,
     hidden_ref,
     grad_ref,
+    slope_ref,
     hidden_edge_ref,
     grad_edge_ref,
-    k1_ref,
-    k2_ref,
-    b2_ref,
+    slope_edge_ref,
+    w2_ref,
+    w4_ref,
     feat_ref,
     gin_ref,
+    leftw_ref,
     hidden_low_ref,
     grad_low_ref,
+    fixed_ref,
     featw_ref,
     ginw_ref,
-    turned_ref,
-    w4_ref,
 ):
     ch2, depth_q, half_y = feat_ref.shape
     c_in, _, depth_y = gin_ref.shape
     depth_z, rows, _ = mid_ref.shape
     size = hidden_edge_ref.shape[0] // 2
     ch1 = size // COLUMNS
+    spread_rows = 3 * ch2
+
+    def spread(q, count):
+        left = leftw_ref[(q + 1) * ch2 : (q + 2) * ch2, :]
+        if q < 0:
+            rest = low_ref[2 * rows + ch2 : 2 * rows + count * ch2, :]
+        elif q >= depth_q:
+            rest = high_ref[2 * rows : 2 * rows + ch2, :]
+        else:
+            rest = wide_ref[q * spread_rows + ch2 : q * spread_rows + count * ch2, :]
+        return jnp.concatenate([left, rest], axis=0)
 
     def plane(z):
         return low_ref[(z + 2) * rows : (z + 3) * rows, :] if z < 0 else mid_ref[z]
 
-    below, here = rim_columns(low_ref, odd_plane, 2 * rows), wide_ref[: 3 * ch2, :]
+    leftw_ref[:ch2, :] = odd_plane(low_ref[2 * rows : 2 * rows + ch2, :].astype(F32)).astype(BF16)
+    for k in range(depth_q // 2):
+        pair = left_ref[k * ch2 : (k + 1) * ch2, :].astype(F32)
+        at = (2 * k + 1) * ch2
+        leftw_ref[at : at + ch2, :] = even_plane(pair).astype(BF16)
+        leftw_ref[at + ch2 : at + 2 * ch2, :] = odd_plane(pair).astype(BF16)
+    leftw_ref[(depth_q + 1) * ch2 :, :] = even_plane(corner_ref[...].astype(F32)).astype(BF16)
+    below, here = spread(-1, 3), spread(0, 3)
     raws = {
         -1: unspread(mm(odd_ref[...], jnp.concatenate([below, here], axis=0))),
         0: unspread(mm(even_ref[...], here)),
     }
 
-    def store(z, hidden, grad):
+    def store(z, hidden, grad, slope):
         store_level(hidden_low_ref, grad_low_ref, z + 1, hidden, grad, ch1)
 
     activate([[-1, 0]], plane, lambda z: raws[z], place_ref, w1_ref, depth_z, store)
+
+    two = 2 * ch2
+    odd = jnp.concatenate([odd_ref[c * size : c * size + ch1, :] for c in range(3)], axis=0)
+    odd = jnp.concatenate([odd[:, :two], odd[:, spread_rows : spread_rows + two]], axis=1)
+    even = jnp.concatenate([even_ref[c * size : c * size + ch1, :] for c in range(3)], axis=0)[:, :two]
+
+    def fix(z, raw):
+        if z < depth_z - 1:
+            slope = slope_ref[(z - 1) * ch1 : z * ch1, :]
+        else:
+            slope = slope_edge_ref[(z - depth_z + 1) * ch1 : (z - depth_z + 2) * ch1, :]
+        fixed_ref[(z - 1) * ch1 : z * ch1, :] = (raw * slope).astype(BF16)
+
+    for q in range(0, depth_q, 2):
+        cells = [spread(k, 2) for k in (q, q + 1, q + 2)]
+        pairs = lanes([jnp.concatenate(cells[n : n + 2], axis=0) for n in range(2)])
+        odds, evens = mm(odd, pairs), mm(even, lanes(cells[1:]))
+        for n in range(2):
+            at = slice(n * depth_y, (n + 1) * depth_y)
+            fix(2 * (q + n) + 1, unspread(odds[:, at]))
+            fix(2 * (q + n) + 2, unspread(evens[:, at]))
 
     def hidden(z):
         if z < 1:
@@ -524,28 +619,14 @@
         if z < 1:
             return grad_low_ref[(z + 1) * size : (z + 2) * size, :]
         if z < depth_z - 1:
-            return grad_ref[(z - 1) * size : z * size, :]
-        return grad_edge_ref[(z - depth_z + 1) * size : (z - depth_z + 2) * size, :]
+            rest = grad_ref[(z - 1) * size + ch1 : z * size, :]
+        else:
+            rest = grad_edge_ref[(z - depth_z + 1) * size + ch1 : (z - depth_z + 2) * size, :]
+        return jnp.concatenate([fixed_ref[(z - 1) * ch1 : z * ch1, :], rest], axis=0)
 
     def window(level, z):
         return jnp.concatenate([level(z + a) for a in (-1, 0, 1)], axis=0)
 
-    turned_ref[...] = jnp.zeros_like(turned_ref)
-    w4_ref[...] = jnp.zeros_like(w4_ref)
-    for a in range(3):
-        for b in range(3):
-            for c in range(3):
-                k = 9 * a + 3 * b + c
-                down = a * size + b * ch1
-                turned_ref[down : down + ch1, c * ch2 : (c + 1) * ch2] = k2_ref[k].astype(F32)
-                for x in range(2):
-                    down, right = (c * 2 + x) * c_in, (2 - a) * size + (x + 2 - b) * ch1
-                    w4_ref[down : down + c_in, right : right + ch1] = k1_ref[k].astype(F32)
-    for n, part in enumerate(split_bias(b2_ref[...])):
-        row = size + 3 * ch1 + n
-        turned_ref[row : row + 1, ch2 : 2 * ch2] = part
-    w2 = turned_ref[...].T[: 3 * ch2].astype(BF16)
-    w4 = w4_ref[...].astype(BF16)
     pick = (
         lax.broadcasted_iota(jnp.int32, (depth_y, half_y), 0)
         == 2 * lax.broadcasted_iota(jnp.int32, (depth_y, half_y), 1)
@@ -553,7 +634,7 @@
 
     for q in range(0, depth_q, 2):
         source = lanes([window(hidden, 2 * k) for k in (q, q + 1)])
-        products = mm(w2, source)
+        products = mm(w2_ref[...], source)
         for n in range(2):
             terms = products[:, n * depth_y : (n + 1) * depth_y]
             full = from_left(terms[:ch2]) + terms[ch2 : 2 * ch2] + from_right(terms[2 * ch2 :])
@@ -563,7 +644,7 @@
     two = 2 * c_in
     for z in range(0, depth_z, 2):
         source = lanes([window(grad, k) for k in (z, z + 1)])
-        products = mm(w4, source)
+        products = mm(w4_ref[...], source)
         for n in range(2):
             terms = products[:, n * depth_y : (n + 1) * depth_y]
             full = from_right(terms[:two]) + terms[two : 2 * two] + from_left(terms[2 * two :])
@@ -573,33 +654,33 @@
     gin_ref[...] = ginw_ref[...].reshape(gin_ref.shape).astype(BF16)
 
 
-def last(place, low, mid, wide, w1, odd, even, inner_values, edge_values, k1, k2, b2):
+def last(place, low, mid, high, left, corner, wide, w1, odd, even, inner_values, edge_values, w2, w4):
     depth_z, _, depth_y = mid.shape
-    _, c_in, ch1 = k1.shape
-    ch2 = k2.shape[2]
-    size = COLUMNS * ch1
+    ch2, c_in = w2.shape[0] // 3, w4.shape[0] // 6
+    size = w1.shape[0] // 3
+    ch1 = size // COLUMNS
     depth_q = depth_z // 2
     vmem = pl.BlockSpec(memory_space=pltpu.VMEM)
     return pl.pallas_call(
         last_kernel,
-        in_specs=[pl.BlockSpec(memory_space=pltpu.SMEM)] + [vmem] * 13,
+        in_specs=[pl.BlockSpec(memory_space=pltpu.SMEM)] + [vmem] * 17,
         out_specs=(vmem, vmem),
         out_shape=(
             jax.ShapeDtypeStruct((ch2, depth_q, depth_y // 2), BF16),
             jax.ShapeDtypeStruct((c_in, 2 * depth_z, depth_y), BF16),
         ),
         scratch_shapes=[
+            pltpu.VMEM(((depth_q + 2) * ch2, depth_y), BF16),
             pltpu.VMEM((2 * size, depth_y), BF16),
             pltpu.VMEM((2 * size, depth_y), BF16),
+            pltpu.VMEM((depth_z * ch1, depth_y), BF16),
             pltpu.VMEM((ch2 * depth_q, depth_y // 2), F32),
             pltpu.VMEM((c_in * 2 * depth_z, depth_y), F32),
-            pltpu.VMEM((3 * size, 128), F32),
-            pltpu.VMEM((3 * 2 * c_in, 3 * size), F32),
         ],
         compiler_params=pltpu.CompilerParams(vmem_limit_bytes=VMEM_LIMIT),
         cost_estimate=pl.CostEstimate(flops=800_000_000, bytes_accessed=10_000_000, transcendentals=0),
         name="features_and_input_grad",
-    )(place, low, mid, wide, w1, odd, even, *inner_values, *edge_values, k1, k2, b2)
+    )(place, low, mid, high, left, corner, wide, w1, odd, even, *inner_values, *edge_values, w2, w4)
 
 
 def unpack_kernel(sums_ref, first_ref, second_ref, bias1_ref, bias2_ref, *, scale):
@@ -632,6 +713,7 @@
         functools.partial(unpack_kernel, scale=scale),
         in_specs=[pl.BlockSpec(memory_space=pltpu.VMEM)],
         out_shape=(first, second, bias1, bias2),
+        compiler_params=pltpu.CompilerParams(vmem_limit_bytes=VMEM_LIMIT),
         name="unpack_sums",
     )(sums)
     first = first.reshape(3, 3, 3, c_in, ch1).transpose(4, 3, 0, 1, 2)
@@ -662,25 +744,26 @@
     mid = lax.all_to_all(windows, "xy", split_axis=0, concat_axis=0, tiled=True)
 
     cot = cotangent.reshape(ch2, depth_z // 2, depth_y // 2)
-    shifts, pairs, w1, odd, even = prepare_own(cot, k1, first_bias[None], k2)
+    shifts, pairs, w1, odd, even, w2, w4 = prepare_own(cot, k1, first_bias[None], k2, second_bias[None])
     left, right = shifted(pairs, "xy", 1), shifted(pairs, "xy", -1)
-    mid, left, right = lax.optimization_barrier((mid, left, right))
+    mid, right = lax.optimization_barrier((mid, right))
 
     rows = mid.shape[1]
-    downward = [mid[:2].reshape(2 * rows, depth_y), left[:ch2], shifts[ch2 : 2 * ch2], right[:ch2]]
-    high = shifted(jnp.concatenate(downward, axis=0), "gz", -1)
-    wide, *inner_values, first, second = inner(place, mid, left, shifts, right, odd, even, w1)
+    downward = jnp.concatenate([mid[:2].reshape(2 * rows, depth_y), shifts[ch2 : 2 * ch2], right[:ch2]], axis=0)
+    high = shifted(downward, "gz", -1)
+    wide, *inner_values, first, second = inner(place, mid, shifts, right, odd, even, w1)
+    high, left = lax.optimization_barrier((high, left))
     *edge_values, sums = edge(place, mid, high, wide, odd, even, shifts, w1, first, second)
 
     part = exchange(sums.reshape(slabs, -1, sums.shape[1]), "gz").sum(0).astype(BF16)
-    upward = [mid[-2:].reshape(2 * rows, depth_y), left[-ch2:], shifts[-2 * ch2 : -ch2], right[-ch2:]]
-    part, upward = lax.optimization_barrier((part, jnp.concatenate(upward, axis=0)))
-    low = shifted(upward, "gz", 1)
+    upward = [mid[-2:].reshape(2 * rows, depth_y), left[-ch2:], wide[-2 * ch2 :]]
+    part, upward, corner = lax.optimization_barrier((part, jnp.concatenate(upward, axis=0), left[:ch2]))
+    low, corner = shifted(upward, "gz", 1), shifted(corner, "gz", -1)
     part = exchange(copies(part, tiles), "xy").astype(F32).sum(0)
-    part, low = lax.optimization_barrier((part, low))
+    part, low, corner = lax.optimization_barrier((part, low, corner))
     sums = exchange(copies(part, slabs), "gz").reshape(sums.shape)
     features, input_grad = last(
-        place, low, mid, wide, w1, odd, even, inner_values, edge_values, k1, k2, second_bias[None]
+        place, low, mid, high, left, corner, wide, w1, odd, even, inner_values, edge_values, w2, w4
     )
     scale = 1.0 / math.sqrt(slabs * depth_z * width * depth_y)
     first_grad, first_bias_grad, second_grad, second_bias_grad = unpack(sums, scale, channels, ch1, ch2)

time: 87.6 us -> 82.9 us (0.946)
  waiting for transfers between devices: 22.9 us -> 21.4 us
  starting transfers between devices: 49.1 us -> 47.8 us
  local copies, waits for them, and re-layouts: 4.02 us -> 2.76 us
    all_to_all x3, starting transfers between devices: 19.1 us -> 15.9 us  [exchange(): return lax.all_to_all(value, axis, 0, 0, tiled=True)]
    ppermute x4 -> x5, starting transfers between devices: 13.3 us -> 15.3 us  [shifted(): lax.ppermute(value, axis, [(source, source + steps) for source in range(f...]
    all_to_all x3, waiting for transfers between devices: 16.5 us -> 15.2 us  [exchange(): return lax.all_to_all(value, axis, 0, 0, tiled=True)]
    unnamed x14 -> x12, local copies, waits for them, and re-layouts: 2.74 us -> 1.47 us
    ppermute x4 -> x5, waiting for transfers between devices: 2.28 us -> 2.06 us  [shifted(): lax.ppermute(value, axis, [(source, source + steps) for source in range(f...]
  transfers between devices with their start and end apart: 8 -> 9, of which waited for: 6 -> 6; matrix products, arithmetic and copies ran while one was open for 0% -> 0% of each run, Pallas kernels for 7% -> 7%
where the time goes in v4:
time: 82.9 us; the launch traced here: 82.3 us
  starting transfers between devices  47.8 us (58%)
  waiting for transfers between devices  21.4 us (26%)
  Pallas kernels  9.44 us (11%)
  local copies, waits for them, and re-layouts  2.76 us (3%)
    all_to_all x1, starting transfers between devices, shards(): mid = lax.all_to_all(windows, 'xy', split_axis=0, concat_axis=0, tiled=True)  16.6 us
    all_to_all x3, starting transfers between devices, exchange(): return lax.all_to_all(value, axis, 0, 0, tiled=True)  15.9 us
    ppermute x5, starting transfers between devices, shifted(): lax.ppermute(value, axis, [(source, source + steps) for source in range(f...  15.3 us
    all_to_all x3, waiting for transfers between devices, exchange(): return lax.all_to_all(value, axis, 0, 0, tiled=True)  15.2 us
    all_to_all x1, waiting for transfers between devices, shards(): mid = lax.all_to_all(windows, 'xy', split_axis=0, concat_axis=0, tiled=True)  4.1 us
    pallas_call x1, Pallas kernels, last(): pl.pallas_call(last_kernel, in_specs=[pl.BlockSpec(memory_space=pltpu.SME...  3.1 us
    pallas_call x1, Pallas kernels, inner(): pl.pallas_call(inner_kernel, in_specs=[pl.BlockSpec(memory_space=pltpu.SM...  2.33 us
    ppermute x5, waiting for transfers between devices, shifted(): lax.ppermute(value, axis, [(source, source + steps) for source in range(f...  2.06 us
  transfers between devices with their start and end apart: 9, of which 6 were waited for; matrix products, arithmetic and copies ran while one was open for 0% of the time, Pallas kernels for 7%

profile of v4, /device:TPU:1, one launch (start us, length us, event | category | flops | bytes accessed | tf_op | source)
XLA Modules:
  0.0 82.3 jit_solution(3845250994596487640)
XLA Ops:
  0.6 0.0 copy-start
  0.6 0.8 %copy-done = bf16[4,1,1,1,64,128]{5,4,3,2,1,0:T(8,128)(2,1)S(1)} copy-done((bf16[4,1,1,1,64,128]{5,4,3,2,1,0:T(8,128)(2,1)S(1)}, bf16[4,1,1,1,64,128]{5,4,3,2,1,0:T(8,128)(2,1)}, u32[]{:S(2)}) %copy-start) | copy-done | bytes 65560
  1.5 0.7 pack_windows.1
  2.2 0.0 copy-start.1
  2.2 0.0 copy-start.2
  2.2 0.0 copy-start.3
  2.2 16.6 %all-to-all-start = ((bf16[32,32,128]{2,1,0:T(8,128)(2,1)}), bf16[32,32,128]{2,1,0:T(8,128)(2,1)S(1)}, u32[]{:S(2)}, u32[]{:S(2)}) async-start(bf16[32,32,128]{2,1,0:T(8,128)(2,1)} %pack_windows.1), calls=%async_computation | async-start | bytes 524288 | tf_op jit(solution)/shard_map/all_to_all | solution.py:744
  18.9 0.0 copy-start.4
  18.9 0.0 copy-start.5
  18.9 0.0 copy-done.1
  18.9 0.0 copy-done.2
  18.9 0.0 copy-done.3
  18.9 0.6 copy-done.4
  19.5 0.0 copy-done.5
  19.5 0.5 spread_cotangent.1
  20.1 1.3 %collective-permute-start = (bf16[256,128]{1,0:T(8,128)(2,1)S(1)}, bf16[256,128]{1,0:T(8,128)(2,1)S(1)}, u32[]{:S(2)}, u32[]{:S(2)}) collective-permute-start(bf16[256,128]{1,0:T(8,128)(2,1)S(1)} %get-tuple-element.39), channel_id=1, source_target_pairs={{1,0},{2,1},{3,2},{4,3},{5,4},{6,5},{7,6},{8,7},{9,8},{10,9},{11,1... | collective-permute-start | bytes 196616 | tf_op jit(solution)/shard_map/ppermute | solution.py:21
  21.4 4.0 %collective-permute-start.2 = (bf16[256,128]{1,0:T(8,128)(2,1)S(1)}, bf16[256,128]{1,0:T(8,128)(2,1)S(1)}, u32[]{:S(2)}, u32[]{:S(2)}) collective-permute-start(bf16[256,128]{1,0:T(8,128)(2,1)S(1)} %get-tuple-element.39), channel_id=1, source_target_pairs={{0,1},{1,2},{2,3},{3,4},{4,5},{5,6},{6,7},{7,8},{8,9},{9,10},{10,1... | collective-permute-start | bytes 196616 | tf_op jit(solution)/shard_map/ppermute | solution.py:21
  25.4 1.8 %collective-permute-done.right_ref = bf16[256,128]{1,0:T(8,128)(2,1)S(1)} collective-permute-done((bf16[256,128]{1,0:T(8,128)(2,1)S(1)}, bf16[256,128]{1,0:T(8,128)(2,1)S(1)}, u32[]{:S(2)}, u32[]{:S(2)}) %collective-permute-start) | collective-permute-done | bytes 65568 | tf_op jit(solution)/shard_map/ppermute | solution.py:21
  27.2 4.1 %all-to-all-done.mid_ref = bf16[32,32,128]{2,1,0:T(8,128)(2,1)S(1)} async-done(((bf16[32,32,128]{2,1,0:T(8,128)(2,1)}), bf16[32,32,128]{2,1,0:T(8,128)(2,1)S(1)}, u32[]{:S(2)}, u32[]{:S(2)}) %all-to-all-start) | async-done | bytes 262176 | tf_op jit(solution)/shard_map/all_to_all | solution.py:744
  31.3 5.3 %collective-permute-start.1 = (bf16[128,128]{1,0:T(8,128)(2,1)S(1)}, bf16[128,128]{1,0:T(8,128)(2,1)S(1)}, u32[]{:S(2)}, u32[]{:S(2)}) collective-permute-start(bf16[128,128]{1,0:T(8,128)(2,1)S(1)} %pad_maximum_fusion.1), channel_id=1, source_target_pairs={{32,0},{64,32},{96,64},{128,96},{160,128},{192,160},{224,192},{256... | collective-permute-start | bytes 98312 | tf_op jit(solution)/shard_map/ppermute | solution.py:21
  36.7 0.1 add_convert_fusion.place_ref
  36.7 2.3 %inner_levels.1 = (bf16[1536,128]{1,0:T(8,128)(2,1)S(1)}, bf16[1920,128]{1,0:T(8,128)(2,1)S(1)}, bf16[1920,128]{1,0:T(8,128)(2,1)S(1)}, f32[480,128]{1,0:T(8,128...) custom-call(s32[4]{0:T(128)S(1)} %add_convert_fusion.place_ref, bf16[32,32,128]{2,1,0:T(8,128)(2,1)S(1)} %all-to-all-done.mid_ref, ...), custom_call_target="tpu_custom_call" | custom-call | tf_op jit(solution)/shard_map/inner_levels/pallas_call | solution.py:480
  39.1 0.0 collective-permute-done.2.left_ref
  39.1 0.2 collective-permute-done.1.high_ref
  39.3 1.9 %edge_levels_and_sums.1 = (bf16[128,128]{1,0:T(8,128)(2,1)S(1)}, bf16[128,128]{1,0:T(8,128)(2,1)S(1)}, f32[32,128]{1,0:T(8,128)S(1)}, f32[128,128]{1,0:T(8,128)}) custom-call(s32[4]{0:T(128)S(1)} %add_convert_fusion.place_ref, bf16[32,32,128]{2,1,0:T(8,128)(2,1)S(1)} %all-to-all-done.mid_ref, bf16[128,128]{1,0:T(8,128)(2,1)S(1)} %collective-permute-done.1.high_ref, ...), custom_call_target="tpu_custom_call" | custom-call | tf_op jit(solution)/shard_map/edge_levels_and_sums/pallas_call | solution.py:504
  41.2 5.1 %all-to-all-start.1 = ((f32[16,8,128]{2,1,0:T(8,128)}), f32[16,8,128]{2,1,0:T(8,128)S(1)}, u32[]{:S(2)}, u32[]{:S(2)}) async-start(f32[16,8,128]{2,1,0:T(8,128)} %bitcast.13), calls=%async_computation.1 | async-start | bytes 131072 | tf_op jit(solution)/shard_map/all_to_all | solution.py:725
  46.4 5.8 %all-to-all-done.1 = f32[16,8,128]{2,1,0:T(8,128)S(1)} async-done(((f32[16,8,128]{2,1,0:T(8,128)}), f32[16,8,128]{2,1,0:T(8,128)S(1)}, u32[]{:S(2)}, u32[]{:S(2)}) %all-to-all-start.1) | async-done | bytes 65568 | tf_op jit(solution)/shard_map/all_to_all | solution.py:725
  52.2 0.6 broadcast_in_dim.23
  52.8 5.6 %all-to-all-start.2 = ((bf16[32,8,128]{2,1,0:T(8,128)(2,1)}), bf16[32,8,128]{2,1,0:T(8,128)(2,1)S(1)}, u32[]{:S(2)}, u32[]{:S(2)}) async-start(bf16[32,8,128]{2,1,0:T(8,128)(2,1)} %broadcast_in_dim.23), calls=%async_computation.2 | async-start | bytes 131072 | tf_op jit(solution)/shard_map/all_to_all | solution.py:725
  58.5 2.8 %collective-permute-start.3 = (bf16[160,128]{1,0:T(8,128)(2,1)S(1)}, bf16[160,128]{1,0:T(8,128)(2,1)S(1)}, u32[]{:S(2)}, u32[]{:S(2)}) collective-permute-start(bf16[160,128]{1,0:T(8,128)(2,1)S(1)} %pad_maximum_fusion), channel_id=1, source_target_pairs={{0,32},{32,64},{64,96},{96,128},{128,160},{160,192},{192,224},{224... | collective-permute-start | bytes 122888 | tf_op jit(solution)/shard_map/ppermute | solution.py:21
  61.2 1.9 %collective-permute-start.4 = (bf16[32,128]{1,0:T(8,128)(2,1)S(1)}, bf16[32,128]{1,0:T(8,128)(2,1)S(1)}, u32[]{:S(2)}, u32[]{:S(2)}) collective-permute-start(bf16[32,128]{1,0:T(8,128)(2,1)S(1)} %get-tuple-element.54), channel_id=1, source_target_pairs={{32,0},{64,32},{96,64},{128,96},{160,128},{192,160},{224,192},{256... | collective-permute-start | bytes 24584 | tf_op jit(solution)/shard_map/ppermute | solution.py:21
  63.2 6.6 %all-to-all-done.2 = bf16[32,8,128]{2,1,0:T(8,128)(2,1)S(1)} async-done(((bf16[32,8,128]{2,1,0:T(8,128)(2,1)}), bf16[32,8,128]{2,1,0:T(8,128)(2,1)S(1)}, u32[]{:S(2)}, u32[]{:S(2)}) %all-to-all-start.2) | async-done | bytes 65568 | tf_op jit(solution)/shard_map/all_to_all | solution.py:725
  69.8 0.0 collective-permute-done.4.corner_ref
  69.8 0.0 collective-permute-done.3.low_ref
  69.8 0.6 broadcast_in_dim.25
  70.4 5.2 %all-to-all-start.3 = ((f32[16,8,128]{2,1,0:T(8,128)}), f32[16,8,128]{2,1,0:T(8,128)S(1)}, u32[]{:S(2)}, u32[]{:S(2)}) async-start(f32[16,8,128]{2,1,0:T(8,128)} %broadcast_in_dim.25), calls=%async_computation.3 | async-start | bytes 131072 | tf_op jit(solution)/shard_map/all_to_all | solution.py:725
  75.6 3.1 %features_and_input_grad.1 = (bf16[32,16,64]{2,1,0:T(8,128)(2,1)}, bf16[4,64,128]{2,1,0:T(8,128)(2,1)}) custom-call(s32[4]{0:T(128)S(1)} %add_convert_fusion.place_ref, bf16[160,128]{1,0:T(8,128)(2,1)S(1)} %collective-permute-done.3.low_ref, bf16[32,32,128]{2,1,0:T(8,128)(2,1)S(1)} %all-to-all-done.mid_ref, ...), custom_call_target="tpu_custom_call" | custom-call | flops 800000000 | bytes 10000000 | tf_op jit(solution)/shard_map/features_and_input_grad/pallas_call | solution.py:664
  78.7 2.8 %all-to-all-done.3 = f32[16,8,128]{2,1,0:T(8,128)S(1)} async-done(((f32[16,8,128]{2,1,0:T(8,128)}), f32[16,8,128]{2,1,0:T(8,128)S(1)}, u32[]{:S(2)}, u32[]{:S(2)}) %all-to-all-start.3) | async-done | bytes 65568 | tf_op jit(solution)/shard_map/all_to_all | solution.py:725
  81.5 0.8 %unpack_sums.1 = (f32[27,4,16]{2,1,0:T(4,128)}, f32[27,16,32]{2,1,0:T(8,128)}, f32[1,16]{1,0:T(1,128)}, f32[1,32]{1,0:T(1,128)}) custom-call(f32[128,128]{1,0:T(8,128)S(1)} %bitcast.30), custom_call_target="tpu_custom_call" | custom-call | tf_op jit(solution)/shard_map/unpack_sums/pallas_call | solution.py:712
  (9 shorter events, 0.1 us)
Async XLA Ops:
  0.6 0.8 %copy-start = (bf16[4,1,1,1,64,128]{5,4,3,2,1,0:T(8,128)(2,1)S(1)}, bf16[4,1,1,1,64,128]{5,4,3,2,1,0:T(8,128)(2,1)}, u32[]{:S(2)}) copy-start(bf16[4,1,1,1,64,128]{5,4,3,2,1,0:T(8,128)(2,1)} %param.6) | copy-start | bytes 196612
  2.2 16.7 %copy-start.1 = (bf16[32,16,1,64]{3,1,2,0:T(8,128)(2,1)S(1)}, bf16[32,16,1,64]{3,1,2,0:T(8,128)(2,1)}, u32[]{:S(2)}) copy-start(bf16[32,16,1,64]{3,1,2,0:T(8,128)(2,1)} %param.11) | copy-start | bytes 196612
  2.2 16.7 %copy-start.2 = (bf16[32,16,3,3,3]{0,1,4,3,2:T(8,128)(2,1)S(1)}, bf16[32,16,3,3,3]{0,1,4,3,2:T(8,128)(2,1)}, u32[]{:S(2)}) copy-start(bf16[32,16,3,3,3]{0,1,4,3,2:T(8,128)(2,1)} %param.9) | copy-start | bytes 82948
  2.2 16.7 %copy-start.3 = (bf16[16,4,3,3,3]{0,1,4,3,2:T(4,128)(2,1)S(1)}, bf16[16,4,3,3,3]{0,1,4,3,2:T(4,128)(2,1)}, u32[]{:S(2)}) copy-start(bf16[16,4,3,3,3]{0,1,4,3,2:T(4,128)(2,1)} %param.7) | copy-start | bytes 10372
  2.2 29.1 %all-to-all-start = ((bf16[32,32,128]{2,1,0:T(8,128)(2,1)}), bf16[32,32,128]{2,1,0:T(8,128)(2,1)S(1)}, u32[]{:S(2)}, u32[]{:S(2)}) async-start(bf16[32,32,128]{2,1,0:T(8,128)(2,1)} %pack_windows.1), calls=%async_computation | async-start | bytes 524288 | tf_op jit(solution)/shard_map/all_to_all | solution.py:744
  18.9 0.7 copy-start.4
  18.9 0.7 copy-start.5
  20.1 7.1 %collective-permute-start = (bf16[256,128]{1,0:T(8,128)(2,1)S(1)}, bf16[256,128]{1,0:T(8,128)(2,1)S(1)}, u32[]{:S(2)}, u32[]{:S(2)}) collective-permute-start(bf16[256,128]{1,0:T(8,128)(2,1)S(1)} %get-tuple-element.39), channel_id=1, source_target_pairs={{1,0},{2,1},{3,2},{4,3},{5,4},{6,5},{7,6},{8,7},{9,8},{10,9},{11,1... | collective-permute-start | bytes 196616 | tf_op jit(solution)/shard_map/ppermute | solution.py:21
  21.4 17.7 %collective-permute-start.2 = (bf16[256,128]{1,0:T(8,128)(2,1)S(1)}, bf16[256,128]{1,0:T(8,128)(2,1)S(1)}, u32[]{:S(2)}, u32[]{:S(2)}) collective-permute-start(bf16[256,128]{1,0:T(8,128)(2,1)S(1)} %get-tuple-element.39), channel_id=1, source_target_pairs={{0,1},{1,2},{2,3},{3,4},{4,5},{5,6},{6,7},{7,8},{8,9},{9,10},{10,1... | collective-permute-start | bytes 196616 | tf_op jit(solution)/shard_map/ppermute | solution.py:21
  31.3 8.0 %collective-permute-start.1 = (bf16[128,128]{1,0:T(8,128)(2,1)S(1)}, bf16[128,128]{1,0:T(8,128)(2,1)S(1)}, u32[]{:S(2)}, u32[]{:S(2)}) collective-permute-start(bf16[128,128]{1,0:T(8,128)(2,1)S(1)} %pad_maximum_fusion.1), channel_id=1, source_target_pairs={{32,0},{64,32},{96,64},{128,96},{160,128},{192,160},{224,192},{256... | collective-permute-start | bytes 98312 | tf_op jit(solution)/shard_map/ppermute | solution.py:21
  41.2 10.9 %all-to-all-start.1 = ((f32[16,8,128]{2,1,0:T(8,128)}), f32[16,8,128]{2,1,0:T(8,128)S(1)}, u32[]{:S(2)}, u32[]{:S(2)}) async-start(f32[16,8,128]{2,1,0:T(8,128)} %bitcast.13), calls=%async_computation.1 | async-start | bytes 131072 | tf_op jit(solution)/shard_map/all_to_all | solution.py:725
  52.8 16.9 %all-to-all-start.2 = ((bf16[32,8,128]{2,1,0:T(8,128)(2,1)}), bf16[32,8,128]{2,1,0:T(8,128)(2,1)S(1)}, u32[]{:S(2)}, u32[]{:S(2)}) async-start(bf16[32,8,128]{2,1,0:T(8,128)(2,1)} %broadcast_in_dim.23), calls=%async_computation.2 | async-start | bytes 131072 | tf_op jit(solution)/shard_map/all_to_all | solution.py:725
  58.5 11.3 %collective-permute-start.3 = (bf16[160,128]{1,0:T(8,128)(2,1)S(1)}, bf16[160,128]{1,0:T(8,128)(2,1)S(1)}, u32[]{:S(2)}, u32[]{:S(2)}) collective-permute-start(bf16[160,128]{1,0:T(8,128)(2,1)S(1)} %pad_maximum_fusion), channel_id=1, source_target_pairs={{0,32},{32,64},{64,96},{96,128},{128,160},{160,192},{192,224},{224... | collective-permute-start | bytes 122888 | tf_op jit(solution)/shard_map/ppermute | solution.py:21
  61.2 8.6 %collective-permute-start.4 = (bf16[32,128]{1,0:T(8,128)(2,1)S(1)}, bf16[32,128]{1,0:T(8,128)(2,1)S(1)}, u32[]{:S(2)}, u32[]{:S(2)}) collective-permute-start(bf16[32,128]{1,0:T(8,128)(2,1)S(1)} %get-tuple-element.54), channel_id=1, source_target_pairs={{32,0},{64,32},{96,64},{128,96},{160,128},{192,160},{224,192},{256... | collective-permute-start | bytes 24584 | tf_op jit(solution)/shard_map/ppermute | solution.py:21
  70.4 11.1 %all-to-all-start.3 = ((f32[16,8,128]{2,1,0:T(8,128)}), f32[16,8,128]{2,1,0:T(8,128)S(1)}, u32[]{:S(2)}, u32[]{:S(2)}) async-start(f32[16,8,128]{2,1,0:T(8,128)} %broadcast_in_dim.25), calls=%async_computation.3 | async-start | bytes 131072 | tf_op jit(solution)/shard_map/all_to_all | solution.py:725

commit v5 on v4

--- a/solution.py
+++ b/solution.py
@@ -755,11 +755,13 @@
     high, left = lax.optimization_barrier((high, left))
     *edge_values, sums = edge(place, mid, high, wide, odd, even, shifts, w1, first, second)
 
-    part = exchange(sums.reshape(slabs, -1, sums.shape[1]), "gz").sum(0).astype(BF16)
     upward = [mid[-2:].reshape(2 * rows, depth_y), left[-ch2:], wide[-2 * ch2 :]]
-    part, upward, corner = lax.optimization_barrier((part, jnp.concatenate(upward, axis=0), left[:ch2]))
+    upward, corner = jnp.concatenate(upward, axis=0), left[:ch2]
+    sums, upward, corner = lax.optimization_barrier((sums, upward, corner))
+    part = exchange(sums.reshape(slabs, -1, sums.shape[1]), "gz").sum(0)
+    part, upward, corner = lax.optimization_barrier((part, upward, corner))
     low, corner = shifted(upward, "gz", 1), shifted(corner, "gz", -1)
-    part = exchange(copies(part, tiles), "xy").astype(F32).sum(0)
+    part = exchange(copies(part, tiles), "xy").sum(0)
     part, low, corner = lax.optimization_barrier((part, low, corner))
     sums = exchange(copies(part, slabs), "gz").reshape(sums.shape)
     features, input_grad = last(

time: 82.9 us -> 82.6 us (level)
  blocking collectives: 0 us -> 10.7 us
  waiting for transfers between devices: 21.4 us -> 15.9 us
  starting transfers between devices: 47.8 us -> 42.9 us
    all_to_all x0 -> x1, blocking collectives: none -> 10.7 us  [exchange(): return lax.all_to_all(value, axis, 0, 0, tiled=True)]
    all_to_all x3 -> x2, waiting for transfers between devices: 15.2 us -> 9.69 us  [exchange(): return lax.all_to_all(value, axis, 0, 0, tiled=True)]
    all_to_all x3 -> x2, starting transfers between devices: 15.9 us -> 11 us  [exchange(): return lax.all_to_all(value, axis, 0, 0, tiled=True)]
  transfers between devices with their start and end apart: 9 -> 8, of which waited for: 6 -> 5; matrix products, arithmetic and copies ran while one was open for 0% -> 0% of each run, Pallas kernels for 7% -> 7%
where the time goes in v5:
time: 82.6 us; the launch traced here: 82 us
  starting transfers between devices  42.9 us (52%)
  waiting for transfers between devices  15.9 us (19%)
  blocking collectives  10.7 us (13%)
  Pallas kernels  8.82 us (11%)
  local copies, waits for them, and re-layouts  2.79 us (3%)
    all_to_all x1, starting transfers between devices, shards(): mid = lax.all_to_all(windows, 'xy', split_axis=0, concat_axis=0, tiled=True)  16.6 us
    ppermute x5, starting transfers between devices, shifted(): lax.ppermute(value, axis, [(source, source + steps) for source in range(f...  15.3 us
    all_to_all x2, starting transfers between devices, exchange(): return lax.all_to_all(value, axis, 0, 0, tiled=True)  11 us
    all_to_all x1, blocking collectives, exchange(): return lax.all_to_all(value, axis, 0, 0, tiled=True)  10.7 us
    all_to_all x2, waiting for transfers between devices, exchange(): return lax.all_to_all(value, axis, 0, 0, tiled=True)  9.69 us
    all_to_all x1, waiting for transfers between devices, shards(): mid = lax.all_to_all(windows, 'xy', split_axis=0, concat_axis=0, tiled=True)  4.1 us
    pallas_call x1, Pallas kernels, last(): pl.pallas_call(last_kernel, in_specs=[pl.BlockSpec(memory_space=pltpu.SME...  3.1 us
    pallas_call x1, Pallas kernels, inner(): pl.pallas_call(inner_kernel, in_specs=[pl.BlockSpec(memory_space=pltpu.SM...  2.33 us
  transfers between devices with their start and end apart: 8, of which 5 were waited for; matrix products, arithmetic and copies ran while one was open for 0% of the time, Pallas kernels for 7%

profile of v5, /device:TPU:1, one launch (start us, length us, event | category | flops | bytes accessed | tf_op | source)
XLA Modules:
  0.0 82.0 jit_solution(4847336433064638577)
XLA Ops:
  0.6 0.0 copy-start
  0.6 0.8 %copy-done = bf16[4,1,1,1,64,128]{5,4,3,2,1,0:T(8,128)(2,1)S(1)} copy-done((bf16[4,1,1,1,64,128]{5,4,3,2,1,0:T(8,128)(2,1)S(1)}, bf16[4,1,1,1,64,128]{5,4,3,2,1,0:T(8,128)(2,1)}, u32[]{:S(2)}) %copy-start) | copy-done | bytes 65560
  1.5 0.7 pack_windows.1
  2.2 0.0 copy-start.1
  2.2 0.0 copy-start.2
  2.2 0.0 copy-start.3
  2.2 16.6 %all-to-all-start = ((bf16[32,32,128]{2,1,0:T(8,128)(2,1)}), bf16[32,32,128]{2,1,0:T(8,128)(2,1)S(1)}, u32[]{:S(2)}, u32[]{:S(2)}) async-start(bf16[32,32,128]{2,1,0:T(8,128)(2,1)} %pack_windows.1), calls=%async_computation | async-start | bytes 524288 | tf_op jit(solution)/shard_map/all_to_all | solution.py:744
  18.9 0.0 copy-start.4
  18.9 0.0 copy-start.5
  18.9 0.0 copy-done.1
  18.9 0.0 copy-done.2
  18.9 0.0 copy-done.3
  18.9 0.6 copy-done.4
  19.5 0.0 copy-done.5
  19.5 0.5 spread_cotangent.1
  20.1 1.3 %collective-permute-start = (bf16[256,128]{1,0:T(8,128)(2,1)S(1)}, bf16[256,128]{1,0:T(8,128)(2,1)S(1)}, u32[]{:S(2)}, u32[]{:S(2)}) collective-permute-start(bf16[256,128]{1,0:T(8,128)(2,1)S(1)} %get-tuple-element.42), channel_id=1, source_target_pairs={{1,0},{2,1},{3,2},{4,3},{5,4},{6,5},{7,6},{8,7},{9,8},{10,9},{11,1... | collective-permute-start | bytes 196616 | tf_op jit(solution)/shard_map/ppermute | solution.py:21
  21.4 4.0 %collective-permute-start.2 = (bf16[256,128]{1,0:T(8,128)(2,1)S(1)}, bf16[256,128]{1,0:T(8,128)(2,1)S(1)}, u32[]{:S(2)}, u32[]{:S(2)}) collective-permute-start(bf16[256,128]{1,0:T(8,128)(2,1)S(1)} %get-tuple-element.42), channel_id=1, source_target_pairs={{0,1},{1,2},{2,3},{3,4},{4,5},{5,6},{6,7},{7,8},{8,9},{9,10},{10,1... | collective-permute-start | bytes 196616 | tf_op jit(solution)/shard_map/ppermute | solution.py:21
  25.4 1.8 %collective-permute-done.right_ref = bf16[256,128]{1,0:T(8,128)(2,1)S(1)} collective-permute-done((bf16[256,128]{1,0:T(8,128)(2,1)S(1)}, bf16[256,128]{1,0:T(8,128)(2,1)S(1)}, u32[]{:S(2)}, u32[]{:S(2)}) %collective-permute-start) | collective-permute-done | bytes 65568 | tf_op jit(solution)/shard_map/ppermute | solution.py:21
  27.2 4.1 %all-to-all-done.mid_ref = bf16[32,32,128]{2,1,0:T(8,128)(2,1)S(1)} async-done(((bf16[32,32,128]{2,1,0:T(8,128)(2,1)}), bf16[32,32,128]{2,1,0:T(8,128)(2,1)S(1)}, u32[]{:S(2)}, u32[]{:S(2)}) %all-to-all-start) | async-done | bytes 262176 | tf_op jit(solution)/shard_map/all_to_all | solution.py:744
  31.3 5.3 %collective-permute-start.1 = (bf16[128,128]{1,0:T(8,128)(2,1)S(1)}, bf16[128,128]{1,0:T(8,128)(2,1)S(1)}, u32[]{:S(2)}, u32[]{:S(2)}) collective-permute-start(bf16[128,128]{1,0:T(8,128)(2,1)S(1)} %pad_maximum_fusion.1), channel_id=1, source_target_pairs={{32,0},{64,32},{96,64},{128,96},{160,128},{192,160},{224,192},{256... | collective-permute-start | bytes 98312 | tf_op jit(solution)/shard_map/ppermute | solution.py:21
  36.7 0.1 add_convert_fusion.place_ref
  36.7 2.3 %inner_levels.1 = (bf16[1536,128]{1,0:T(8,128)(2,1)S(1)}, bf16[1920,128]{1,0:T(8,128)(2,1)S(1)}, bf16[1920,128]{1,0:T(8,128)(2,1)S(1)}, f32[480,128]{1,0:T(8,128...) custom-call(s32[4]{0:T(128)S(1)} %add_convert_fusion.place_ref, bf16[32,32,128]{2,1,0:T(8,128)(2,1)S(1)} %all-to-all-done.mid_ref, ...), custom_call_target="tpu_custom_call" | custom-call | tf_op jit(solution)/shard_map/inner_levels/pallas_call | solution.py:480
  39.1 0.0 collective-permute-done.2.left_ref
  39.1 0.2 collective-permute-done.1.high_ref
  39.3 1.3 %edge_levels_and_sums.1 = (bf16[128,128]{1,0:T(8,128)(2,1)S(1)}, bf16[128,128]{1,0:T(8,128)(2,1)S(1)}, f32[32,128]{1,0:T(8,128)S(1)}, f32[128,128]{1,0:T(8,128)S(1)}) custom-call(s32[4]{0:T(128)S(1)} %add_convert_fusion.place_ref, bf16[32,32,128]{2,1,0:T(8,128)(2,1)S(1)} %all-to-all-done.mid_ref, bf16[128,128]{1,0:T(8,128)(2,1)S(1)} %collective-permute-done.1.high_ref, ...), custom_call_target="tpu_custom_call" | custom-call | tf_op jit(solution)/shard_map/edge_levels_and_sums/pallas_call | solution.py:504
  40.6 10.7 %all_to_all.20 = f32[16,8,128]{2,1,0:T(8,128)S(1)} all-to-all(f32[16,8,128]{2,1,0:T(8,128)S(1)} %bitcast.32), channel_id=1, replica_groups=mesh['gz'=16,'xy'=32] {'gz'}, dimensions={0} | all-to-all | bytes 131072 | tf_op jit(solution)/shard_map/all_to_all | solution.py:725
  51.4 0.7 broadcast_in_dim.23
  52.0 5.6 %all-to-all-start.2 = ((f32[32,8,128]{2,1,0:T(8,128)}), f32[32,8,128]{2,1,0:T(8,128)S(1)}, u32[]{:S(2)}, u32[]{:S(2)}) async-start(f32[32,8,128]{2,1,0:T(8,128)} %broadcast_in_dim.23), calls=%async_computation.2 | async-start | bytes 262144 | tf_op jit(solution)/shard_map/all_to_all | solution.py:725
  57.7 2.8 %collective-permute-start.3 = (bf16[160,128]{1,0:T(8,128)(2,1)S(1)}, bf16[160,128]{1,0:T(8,128)(2,1)S(1)}, u32[]{:S(2)}, u32[]{:S(2)}) collective-permute-start(bf16[160,128]{1,0:T(8,128)(2,1)S(1)} %pad_maximum_fusion), channel_id=1, source_target_pairs={{0,32},{32,64},{64,96},{96,128},{128,160},{160,192},{192,224},{224... | collective-permute-start | bytes 122888 | tf_op jit(solution)/shard_map/ppermute | solution.py:21
  60.4 1.9 %collective-permute-start.4 = (bf16[32,128]{1,0:T(8,128)(2,1)S(1)}, bf16[32,128]{1,0:T(8,128)(2,1)S(1)}, u32[]{:S(2)}, u32[]{:S(2)}) collective-permute-start(bf16[32,128]{1,0:T(8,128)(2,1)S(1)} %get-tuple-element.60), channel_id=1, source_target_pairs={{32,0},{64,32},{96,64},{128,96},{160,128},{192,160},{224,192},{256... | collective-permute-start | bytes 24584 | tf_op jit(solution)/shard_map/ppermute | solution.py:21
  62.4 6.9 %all-to-all-done.2 = f32[32,8,128]{2,1,0:T(8,128)S(1)} async-done(((f32[32,8,128]{2,1,0:T(8,128)}), f32[32,8,128]{2,1,0:T(8,128)S(1)}, u32[]{:S(2)}, u32[]{:S(2)}) %all-to-all-start.2) | async-done | bytes 131104 | tf_op jit(solution)/shard_map/all_to_all | solution.py:725
  69.3 0.0 collective-permute-done.4.corner_ref
  69.3 0.0 collective-permute-done.3.low_ref
  69.3 0.6 broadcast_in_dim.25
  70.0 5.4 %all-to-all-start.3 = ((f32[16,8,128]{2,1,0:T(8,128)}), f32[16,8,128]{2,1,0:T(8,128)S(1)}, u32[]{:S(2)}, u32[]{:S(2)}) async-start(f32[16,8,128]{2,1,0:T(8,128)} %broadcast_in_dim.25), calls=%async_computation.3 | async-start | bytes 131072 | tf_op jit(solution)/shard_map/all_to_all | solution.py:725
  75.3 3.1 %features_and_input_grad.1 = (bf16[32,16,64]{2,1,0:T(8,128)(2,1)}, bf16[4,64,128]{2,1,0:T(8,128)(2,1)}) custom-call(s32[4]{0:T(128)S(1)} %add_convert_fusion.place_ref, bf16[160,128]{1,0:T(8,128)(2,1)S(1)} %collective-permute-done.3.low_ref, bf16[32,32,128]{2,1,0:T(8,128)(2,1)S(1)} %all-to-all-done.mid_ref, ...), custom_call_target="tpu_custom_call" | custom-call | flops 800000000 | bytes 10000000 | tf_op jit(solution)/shard_map/features_and_input_grad/pallas_call | solution.py:664
  78.4 2.8 %all-to-all-done.3 = f32[16,8,128]{2,1,0:T(8,128)S(1)} async-done(((f32[16,8,128]{2,1,0:T(8,128)}), f32[16,8,128]{2,1,0:T(8,128)S(1)}, u32[]{:S(2)}, u32[]{:S(2)}) %all-to-all-start.3) | async-done | bytes 65568 | tf_op jit(solution)/shard_map/all_to_all | solution.py:725
  81.2 0.8 %unpack_sums.1 = (f32[27,4,16]{2,1,0:T(4,128)}, f32[27,16,32]{2,1,0:T(8,128)}, f32[1,16]{1,0:T(1,128)}, f32[1,32]{1,0:T(1,128)}) custom-call(f32[128,128]{1,0:T(8,128)S(1)} %bitcast.30), custom_call_target="tpu_custom_call" | custom-call | tf_op jit(solution)/shard_map/unpack_sums/pallas_call | solution.py:712
  (9 shorter events, 0.1 us)
Async XLA Ops:
  0.6 0.8 %copy-start = (bf16[4,1,1,1,64,128]{5,4,3,2,1,0:T(8,128)(2,1)S(1)}, bf16[4,1,1,1,64,128]{5,4,3,2,1,0:T(8,128)(2,1)}, u32[]{:S(2)}) copy-start(bf16[4,1,1,1,64,128]{5,4,3,2,1,0:T(8,128)(2,1)} %param.6) | copy-start | bytes 196612
  2.2 16.7 %copy-start.1 = (bf16[32,16,1,64]{3,1,2,0:T(8,128)(2,1)S(1)}, bf16[32,16,1,64]{3,1,2,0:T(8,128)(2,1)}, u32[]{:S(2)}) copy-start(bf16[32,16,1,64]{3,1,2,0:T(8,128)(2,1)} %param.11) | copy-start | bytes 196612
  2.2 16.7 %copy-start.2 = (bf16[32,16,3,3,3]{0,1,4,3,2:T(8,128)(2,1)S(1)}, bf16[32,16,3,3,3]{0,1,4,3,2:T(8,128)(2,1)}, u32[]{:S(2)}) copy-start(bf16[32,16,3,3,3]{0,1,4,3,2:T(8,128)(2,1)} %param.9) | copy-start | bytes 82948
  2.2 16.7 %copy-start.3 = (bf16[16,4,3,3,3]{0,1,4,3,2:T(4,128)(2,1)S(1)}, bf16[16,4,3,3,3]{0,1,4,3,2:T(4,128)(2,1)}, u32[]{:S(2)}) copy-start(bf16[16,4,3,3,3]{0,1,4,3,2:T(4,128)(2,1)} %param.7) | copy-start | bytes 10372
  2.2 29.1 %all-to-all-start = ((bf16[32,32,128]{2,1,0:T(8,128)(2,1)}), bf16[32,32,128]{2,1,0:T(8,128)(2,1)S(1)}, u32[]{:S(2)}, u32[]{:S(2)}) async-start(bf16[32,32,128]{2,1,0:T(8,128)(2,1)} %pack_windows.1), calls=%async_computation | async-start | bytes 524288 | tf_op jit(solution)/shard_map/all_to_all | solution.py:744
  18.9 0.7 copy-start.4
  18.9 0.7 copy-start.5
  20.1 7.1 %collective-permute-start = (bf16[256,128]{1,0:T(8,128)(2,1)S(1)}, bf16[256,128]{1,0:T(8,128)(2,1)S(1)}, u32[]{:S(2)}, u32[]{:S(2)}) collective-permute-start(bf16[256,128]{1,0:T(8,128)(2,1)S(1)} %get-tuple-element.42), channel_id=1, source_target_pairs={{1,0},{2,1},{3,2},{4,3},{5,4},{6,5},{7,6},{8,7},{9,8},{10,9},{11,1... | collective-permute-start | bytes 196616 | tf_op jit(solution)/shard_map/ppermute | solution.py:21
  21.4 17.7 %collective-permute-start.2 = (bf16[256,128]{1,0:T(8,128)(2,1)S(1)}, bf16[256,128]{1,0:T(8,128)(2,1)S(1)}, u32[]{:S(2)}, u32[]{:S(2)}) collective-permute-start(bf16[256,128]{1,0:T(8,128)(2,1)S(1)} %get-tuple-element.42), channel_id=1, source_target_pairs={{0,1},{1,2},{2,3},{3,4},{4,5},{5,6},{6,7},{7,8},{8,9},{9,10},{10,1... | collective-permute-start | bytes 196616 | tf_op jit(solution)/shard_map/ppermute | solution.py:21
  31.3 8.0 %collective-permute-start.1 = (bf16[128,128]{1,0:T(8,128)(2,1)S(1)}, bf16[128,128]{1,0:T(8,128)(2,1)S(1)}, u32[]{:S(2)}, u32[]{:S(2)}) collective-permute-start(bf16[128,128]{1,0:T(8,128)(2,1)S(1)} %pad_maximum_fusion.1), channel_id=1, source_target_pairs={{32,0},{64,32},{96,64},{128,96},{160,128},{192,160},{224,192},{256... | collective-permute-start | bytes 98312 | tf_op jit(solution)/shard_map/ppermute | solution.py:21
  52.0 17.2 %all-to-all-start.2 = ((f32[32,8,128]{2,1,0:T(8,128)}), f32[32,8,128]{2,1,0:T(8,128)S(1)}, u32[]{:S(2)}, u32[]{:S(2)}) async-start(f32[32,8,128]{2,1,0:T(8,128)} %broadcast_in_dim.23), calls=%async_computation.2 | async-start | bytes 262144 | tf_op jit(solution)/shard_map/all_to_all | solution.py:725
  57.7 11.6 %collective-permute-start.3 = (bf16[160,128]{1,0:T(8,128)(2,1)S(1)}, bf16[160,128]{1,0:T(8,128)(2,1)S(1)}, u32[]{:S(2)}, u32[]{:S(2)}) collective-permute-start(bf16[160,128]{1,0:T(8,128)(2,1)S(1)} %pad_maximum_fusion), channel_id=1, source_target_pairs={{0,32},{32,64},{64,96},{96,128},{128,160},{160,192},{192,224},{224... | collective-permute-start | bytes 122888 | tf_op jit(solution)/shard_map/ppermute | solution.py:21
  60.4 8.9 %collective-permute-start.4 = (bf16[32,128]{1,0:T(8,128)(2,1)S(1)}, bf16[32,128]{1,0:T(8,128)(2,1)S(1)}, u32[]{:S(2)}, u32[]{:S(2)}) collective-permute-start(bf16[32,128]{1,0:T(8,128)(2,1)S(1)} %get-tuple-element.60), channel_id=1, source_target_pairs={{32,0},{64,32},{96,64},{128,96},{160,128},{192,160},{224,192},{256... | collective-permute-start | bytes 24584 | tf_op jit(solution)/shard_map/ppermute | solution.py:21
  70.0 11.3 %all-to-all-start.3 = ((f32[16,8,128]{2,1,0:T(8,128)}), f32[16,8,128]{2,1,0:T(8,128)S(1)}, u32[]{:S(2)}, u32[]{:S(2)}) async-start(f32[16,8,128]{2,1,0:T(8,128)} %broadcast_in_dim.25), calls=%async_computation.3 | async-start | bytes 131072 | tf_op jit(solution)/shard_map/all_to_all | solution.py:725

commit v6 on v5

--- a/solution.py
+++ b/solution.py
@@ -166,6 +166,8 @@
     w1_ref,
     odd_ref,
     even_ref,
+    odd_own_ref,
+    even_own_ref,
     w2_ref,
     w4_ref,
     flat_ref,
@@ -194,6 +196,12 @@
     spread_matrix(k2_ref, odd_ref, 0, 2, 0)
     spread_matrix(k2_ref, odd_ref, 0, 0, rows)
     spread_matrix(k2_ref, even_ref, 0, 1, 0)
+    size = even_ref.shape[0] // 3
+    ch1 = size // COLUMNS
+    odd = jnp.concatenate([odd_ref[c * size + ch1 : (c + 1) * size, :] for c in range(3)], axis=0)
+    odd_own_ref[...] = jnp.concatenate([odd[:, ch2:rows], odd[:, rows + ch2 :]], axis=1)
+    even = jnp.concatenate([even_ref[c * size + ch1 : (c + 1) * size, :] for c in range(3)], axis=0)
+    even_own_ref[...] = even[:, ch2:]
     w2_ref[...] = second_matrix(k2_ref, b2_ref, turned2_ref)
     w4_ref[...] = back_matrix(k1_ref, flat4_ref)
 
@@ -211,6 +219,8 @@
             jax.ShapeDtypeStruct((3 * size, 3 * c_in * WINDOW), BF16),
             jax.ShapeDtypeStruct((3 * size, 2 * rows), BF16),
             jax.ShapeDtypeStruct((3 * size, rows), BF16),
+            jax.ShapeDtypeStruct((3 * (size - ch1), 4 * ch2), BF16),
+            jax.ShapeDtypeStruct((3 * (size - ch1), 2 * ch2), BF16),
             jax.ShapeDtypeStruct((rows, 3 * size), BF16),
             jax.ShapeDtypeStruct((6 * c_in, 3 * size), BF16),
         ),
@@ -226,36 +236,33 @@
     )(mid, k1, b1, k2, b2)
 
 
-def spread_columns(shifts_ref, right_ref, wide_ref, cells):
-    rows = wide_ref.shape[0] // cells
-    ch2 = rows // 3
-    for k in range(cells // 2):
-        pair = right_ref[k * ch2 : (k + 1) * ch2, :].astype(F32)
-        for n, plane in enumerate((even_plane(pair), odd_plane(pair))):
-            at = (2 * k + n) * rows
-            wide_ref[at : at + ch2, :] = jnp.zeros((ch2, pair.shape[1]), BF16)
-            wide_ref[at + ch2 : at + 2 * ch2, :] = shifts_ref[at + ch2 : at + 2 * ch2, :]
-            wide_ref[at + 2 * ch2 : at + rows, :] = plane.astype(BF16)
-
-
-def raw_levels(wide_ref, odd_ref, even_ref, raw_ref, cells):
+def raw_levels(shifts_ref, right_ref, odd_ref, even_ref, raw_ref, wide_ref):
+    ch2 = even_ref.shape[1] // 2
+    cells = right_ref.shape[0] // ch2 * 2
     size = even_ref.shape[0] // 3
-    rows = wide_ref.shape[0] // cells
-    depth_y = wide_ref.shape[1]
+    rows = 2 * ch2
+    depth_y = shifts_ref.shape[1]
+    for q in range(cells):
+        at = (3 * q + 1) * ch2
+        wide_ref[q * rows : q * rows + ch2, :] = shifts_ref[at : at + ch2, :]
+        pair = right_ref[q // 2 * ch2 : (q // 2 + 1) * ch2, :].astype(F32)
+        plane = odd_plane(pair) if q % 2 else even_plane(pair)
+        wide_ref[q * rows + ch2 : (q + 1) * rows, :] = plane.astype(BF16)
 
     def store(z, terms):
-        raw_ref[(z - 1) * size : z * size, :] = unspread(terms)
-
-    for m in range(0, cells - 1, 2):
+        raw_ref[z * size : (z + 1) * size, :] = unspread(terms)
+
+    for m in range(0, cells, 2):
+        even = mm(even_ref[...], lanes([wide_ref[k * rows : (k + 1) * rows, :] for k in (m, m + 1)]))
         group = [k for k in (m, m + 1) if k < cells - 1]
         odd = mm(odd_ref[...], lanes([wide_ref[k * rows : (k + 2) * rows, :] for k in group]))
-        even = mm(even_ref[...], lanes([wide_ref[(k + 1) * rows : (k + 2) * rows, :] for k in group]))
+        for n, k in enumerate((m, m + 1)):
+            store(2 * k, even[:, n * depth_y : (n + 1) * depth_y])
         for n, k in enumerate(group):
             store(2 * k + 1, odd[:, n * depth_y : (n + 1) * depth_y])
-            store(2 * k + 2, even[:, n * depth_y : (n + 1) * depth_y])
-
-
-def activate(groups, plane, raw, place_ref, w1_ref, depth_z, store):
+
+
+def activate(groups, plane, place_ref, w1_ref, depth_z, store):
     size = w1_ref.shape[0] // 3
     ch1 = size // COLUMNS
     at_first_z, at_last_z, at_first_x, at_last_x = (place_ref[k] for k in range(4))
@@ -277,11 +284,11 @@
                 keep = inside * jnp.where(at_last_z != 0, 0.0, 1.0)
             kept = sigma * keep
             slope = kept * (1.0 + pre * (1.0 - sigma))
-            store(z, (pre * kept)[: 3 * ch1], raw(z) * slope, slope)
+            store(z, (pre * kept)[: 3 * ch1], slope)
 
 
 def side_by_side(grad, ch1):
-    own = grad[ch1 : 3 * ch1]
+    own = grad[: 2 * ch1]
     parts = [from_right(own), own, from_left(own)]
     sides = [part[x * ch1 : (x + 1) * ch1] for x in range(2) for part in parts]
     return jnp.concatenate(sides, axis=0).astype(BF16)
@@ -303,7 +310,7 @@
     size = COLUMNS * ch1
     hidden_ref[at * size : at * size + 3 * ch1, :] = hidden.astype(BF16)
     hidden_ref[at * size + 3 * ch1 : (at + 1) * size, :] = jnp.ones((ch1, hidden.shape[1]), BF16)
-    grad_ref[at * size : (at + 1) * size, :] = grad.astype(BF16)
+    grad_ref[at * grad.shape[0] : (at + 1) * grad.shape[0], :] = grad.astype(BF16)
 
 
 def inner_kernel(
@@ -314,37 +321,39 @@
     odd_ref,
     even_ref,
     w1_ref,
-    wide_ref,
     hidden_ref,
     grad_ref,
     slope_ref,
     first_ref,
     second_ref,
     raw_ref,
+    wide_ref,
+    begin_ref,
     moved_ref,
 ):
-    depth_z = mid_ref.shape[0]
+    depth_z, rows, depth_y = mid_ref.shape
     size = w1_ref.shape[0] // 3
     ch1 = size // COLUMNS
-    levels = list(range(1, depth_z - 1))
     six = 6 * ch1
+    known = size - ch1
     three = shifts_ref.shape[0] // (depth_z // 2)
-    spread_columns(shifts_ref, right_ref, wide_ref, depth_z // 2)
-    raw_levels(wide_ref, odd_ref, even_ref, raw_ref, depth_z // 2)
-
-    def store(z, hidden, grad, slope):
-        store_level(hidden_ref, grad_ref, z - 1, hidden, grad, ch1)
-        slope_ref[(z - 1) * ch1 : z * ch1, :] = slope[:ch1]
-        moved_ref[(z - 1) * six : z * six, :] = side_by_side(grad, ch1)
+    raw_levels(shifts_ref, right_ref, odd_ref, even_ref, raw_ref, wide_ref)
 
     def plane(z):
-        return mid_ref[z]
-
-    def raw(z):
-        return raw_ref[(z - 1) * size : z * size, :]
+        return mid_ref[z] if z >= 0 else jnp.zeros((rows, depth_y), BF16)
+
+    def store(z, hidden, slope):
+        grad = raw_ref[z * known : (z + 1) * known, :] * slope[ch1:]
+        moved_ref[z * six : (z + 1) * six, :] = side_by_side(grad, ch1)
+        if z == 0:
+            begin_ref[: 3 * ch1, :] = hidden.astype(BF16)
+            begin_ref[3 * ch1 :, :] = jnp.ones((ch1, depth_y), BF16)
+        else:
+            store_level(hidden_ref, grad_ref, z - 1, hidden, grad, ch1)
+            slope_ref[(z - 1) * ch1 : z * ch1, :] = slope[:ch1]
 
     def moved(z):
-        return moved_ref[(z - 1) * six : z * six, :]
+        return moved_ref[z * six : (z + 1) * six, :]
 
     def hidden(z):
         return hidden_ref[(z - 1) * size : z * size, :]
@@ -352,12 +361,13 @@
     def shifts(q):
         return shifts_ref[q * three : (q + 1) * three, :]
 
+    levels = list(range(1, depth_z - 1))
     pairs = [levels[k : k + 2] for k in range(0, len(levels), 2)]
-    activate(pairs, plane, raw, place_ref, w1_ref, depth_z, store)
-    total = None
+    activate([[0]] + pairs, plane, place_ref, w1_ref, depth_z, store)
+    at_bottom = jnp.where(place_ref[0] != 0, 1.0, 0.0)
+    total = at_bottom * first_terms([0], plane, moved)
     for pair in pairs:
-        term = first_terms(pair, plane, moved)
-        total = term if total is None else total + term
+        total = total + first_terms(pair, plane, moved)
     first_ref[...] = total
     upper = lower = None
     cells = list(range(depth_z // 2 - 1))
@@ -365,7 +375,8 @@
         add_upper, add_lower = second_terms(cells[k : k + 2], hidden, shifts)
         upper = add_upper if upper is None else upper + add_upper
         lower = add_lower if lower is None else lower + add_lower
-    second_ref[: 2 * size, :] = upper
+    second_ref[:size, :] = upper[:size]
+    second_ref[size : 2 * size, :] = upper[size:] + at_bottom * mm_nt(begin_ref[...], shifts(0))
     second_ref[2 * size :, :] = lower
 
 
@@ -373,7 +384,7 @@
     place_ref,
     mid_ref,
     high_ref,
-    wide_ref,
+    right_ref,
     odd_ref,
     even_ref,
     shifts_ref,
@@ -384,7 +395,6 @@
     grad_ref,
     slope_ref,
     sums_ref,
-    begin_ref,
     moved_ref,
     fold_ref,
 ):
@@ -392,35 +402,31 @@
     size = w1_ref.shape[0] // 3
     ch1 = size // COLUMNS
     cells = depth_z // 2
-    spread_rows = wide_ref.shape[0] // cells
-    ch2 = spread_rows // 3
-    end = wide_ref[(cells - 1) * spread_rows :, :]
-    right = even_plane(high_ref[2 * rows + ch2 :, :].astype(F32)).astype(BF16)
-    above = jnp.concatenate([jnp.zeros((ch2, depth_y), BF16), high_ref[2 * rows : 2 * rows + ch2, :], right], axis=0)
-    even = mm(even_ref[...], lanes([wide_ref[:spread_rows, :], above]))
+    ch2 = even_ref.shape[1] // 2
+    spread_rows = 3 * ch2
+    own = high_ref[2 * rows : 2 * rows + ch2, :]
+    beyond = even_plane(high_ref[2 * rows + ch2 :, :].astype(F32)).astype(BF16)
+    above = jnp.concatenate([own, beyond], axis=0)
+    at = (3 * cells - 2) * ch2
+    last_right = odd_plane(right_ref[...][-ch2:].astype(F32)).astype(BF16)
+    end = jnp.concatenate([shifts_ref[at : at + ch2, :], last_right], axis=0)
     raws = {
-        0: unspread(even[:, :depth_y]),
         depth_z - 1: unspread(mm(odd_ref[...], jnp.concatenate([end, above], axis=0))),
-        depth_z: unspread(even[:, depth_y:]),
+        depth_z: unspread(mm(even_ref[...], above)),
     }
-    places = {depth_z - 1: 0, depth_z: 1, 0: 2}
+    places = {depth_z - 1: 0, depth_z: 1}
     six = 6 * ch1
 
     def plane(z):
-        if z < 0:
-            return jnp.zeros((rows, depth_y), BF16)
         if z >= depth_z:
             return high_ref[(z - depth_z) * rows : (z - depth_z + 1) * rows, :]
         return mid_ref[z]
 
-    def store(z, hidden, grad, slope):
+    def store(z, hidden, slope):
         at = places[z]
-        if z > 0:
-            store_level(hidden_ref, grad_ref, at, hidden, grad, ch1)
-            slope_ref[at * ch1 : (at + 1) * ch1, :] = slope[:ch1]
-        else:
-            begin_ref[: 3 * ch1, :] = hidden.astype(BF16)
-            begin_ref[3 * ch1 :, :] = jnp.ones((ch1, depth_y), BF16)
+        grad = raws[z] * slope[ch1:]
+        store_level(hidden_ref, grad_ref, at, hidden, grad, ch1)
+        slope_ref[at * ch1 : (at + 1) * ch1, :] = slope[:ch1]
         moved_ref[at * six : (at + 1) * six, :] = side_by_side(grad, ch1)
 
     def moved(z):
@@ -432,16 +438,12 @@
     def shifts(q):
         if q < cells:
             return shifts_ref[q * spread_rows : (q + 1) * spread_rows, :]
-        return moved_three(above[ch2 : 2 * ch2].astype(F32))
-
-    groups = [[depth_z - 1, depth_z], [0]]
-    activate(groups, plane, lambda z: raws[z], place_ref, w1_ref, depth_z, store)
-    at_bottom = jnp.where(place_ref[0] != 0, 1.0, 0.0)
+        return moved_three(own.astype(F32))
+
+    activate([[depth_z - 1, depth_z]], plane, place_ref, w1_ref, depth_z, store)
     first = first_ref[...] + first_terms([depth_z - 1, depth_z], plane, moved)
-    first = first + at_bottom * first_terms([0], plane, moved)
     upper, lower = second_terms([cells - 1], hidden, shifts)
-    bottom = at_bottom * mm_nt(begin_ref[...], shifts(0))
-    second = second_ref[...] + jnp.concatenate([upper[:size], upper[size:] + bottom, lower], axis=0)
+    second = second_ref[...] + jnp.concatenate([upper, lower], axis=0)
     three = 3 * ch1
     wide = 3 * ch2
     main = 7 * ch1
@@ -480,23 +482,27 @@
     return pl.pallas_call(
         inner_kernel,
         in_specs=[pl.BlockSpec(memory_space=pltpu.SMEM)] + [vmem] * 6,
-        out_specs=(vmem,) * 6,
+        out_specs=(vmem,) * 5,
         out_shape=(
-            jax.ShapeDtypeStruct(shifts.shape, BF16),
             jax.ShapeDtypeStruct((count * size, depth_y), BF16),
-            jax.ShapeDtypeStruct((count * size, depth_y), BF16),
+            jax.ShapeDtypeStruct((count * (size - ch1), depth_y), BF16),
             jax.ShapeDtypeStruct((count * ch1, depth_y), F32),
             jax.ShapeDtypeStruct((3 * rows, 6 * ch1), F32),
             jax.ShapeDtypeStruct((3 * size, 3 * ch2), F32),
         ),
-        scratch_shapes=[pltpu.VMEM((count * size, depth_y), F32), pltpu.VMEM((count * 6 * ch1, depth_y), BF16)],
+        scratch_shapes=[
+            pltpu.VMEM(((count + 1) * (size - ch1), depth_y), F32),
+            pltpu.VMEM((depth_z * ch2, depth_y), BF16),
+            pltpu.VMEM((size, depth_y), BF16),
+            pltpu.VMEM(((count + 1) * 6 * ch1, depth_y), BF16),
+        ],
         compiler_params=pltpu.CompilerParams(vmem_limit_bytes=VMEM_LIMIT),
         cost_estimate=pl.CostEstimate(flops=0, bytes_accessed=0, transcendentals=0),
         name="inner_levels",
     )(place, mid, shifts, right, odd, even, w1)
 
 
-def edge(place, mid, high, wide, odd, even, shifts, w1, first, second):
+def edge(place, mid, high, right, odd, even, shifts, w1, first, second):
     _, rows, depth_y = mid.shape
     size = w1.shape[0] // 3
     ch1 = size // COLUMNS
@@ -507,18 +513,17 @@
         out_specs=(vmem,) * 4,
         out_shape=(
             jax.ShapeDtypeStruct((2 * size, depth_y), BF16),
-            jax.ShapeDtypeStruct((2 * size, depth_y), BF16),
+            jax.ShapeDtypeStruct((2 * (size - ch1), depth_y), BF16),
             jax.ShapeDtypeStruct((2 * ch1, depth_y), F32),
             jax.ShapeDtypeStruct((8 * ch1, 128), F32),
         ),
         scratch_shapes=[
-            pltpu.VMEM((size, depth_y), BF16),
-            pltpu.VMEM((3 * 6 * ch1, depth_y), BF16),
+            pltpu.VMEM((2 * 6 * ch1, depth_y), BF16),
             pltpu.VMEM((3 * rows, 3 * ch1), F32),
         ],
         compiler_params=pltpu.CompilerParams(vmem_limit_bytes=VMEM_LIMIT),
         name="edge_levels_and_sums",
-    )(place, mid, high, wide, odd, even, shifts, w1, first, second)
+    )(place, mid, high, right, odd, even, shifts, w1, first, second)
 
 
 def last_kernel(
@@ -528,7 +533,8 @@
     high_ref,
     left_ref,
     corner_ref,
-    wide_ref,
+    right_ref,
+    shifts_ref,
     w1_ref,
     odd_ref,
     even_ref,
@@ -556,15 +562,15 @@
     ch1 = size // COLUMNS
     spread_rows = 3 * ch2
 
-    def spread(q, count):
+    def spread(q):
         left = leftw_ref[(q + 1) * ch2 : (q + 2) * ch2, :]
         if q < 0:
-            rest = low_ref[2 * rows + ch2 : 2 * rows + count * ch2, :]
+            own = low_ref[2 * rows + ch2 : 2 * rows + 2 * ch2, :]
         elif q >= depth_q:
-            rest = high_ref[2 * rows : 2 * rows + ch2, :]
+            own = high_ref[2 * rows : 2 * rows + ch2, :]
         else:
-            rest = wide_ref[q * spread_rows + ch2 : q * spread_rows + count * ch2, :]
-        return jnp.concatenate([left, rest], axis=0)
+            own = shifts_ref[(3 * q + 1) * ch2 : (3 * q + 2) * ch2, :]
+        return jnp.concatenate([left, own], axis=0)
 
     def plane(z):
         return low_ref[(z + 2) * rows : (z + 3) * rows, :] if z < 0 else mid_ref[z]
@@ -576,16 +582,18 @@
         leftw_ref[at : at + ch2, :] = even_plane(pair).astype(BF16)
         leftw_ref[at + ch2 : at + 2 * ch2, :] = odd_plane(pair).astype(BF16)
     leftw_ref[(depth_q + 1) * ch2 :, :] = even_plane(corner_ref[...].astype(F32)).astype(BF16)
-    below, here = spread(-1, 3), spread(0, 3)
+    below = odd_plane(low_ref[2 * rows + 2 * ch2 :, :].astype(F32)).astype(BF16)
+    here = even_plane(right_ref[:ch2, :].astype(F32)).astype(BF16)
+    below, here = (jnp.concatenate([spread(q), side], axis=0) for q, side in ((-1, below), (0, here)))
     raws = {
         -1: unspread(mm(odd_ref[...], jnp.concatenate([below, here], axis=0))),
         0: unspread(mm(even_ref[...], here)),
     }
 
-    def store(z, hidden, grad, slope):
-        store_level(hidden_low_ref, grad_low_ref, z + 1, hidden, grad, ch1)
-
-    activate([[-1, 0]], plane, lambda z: raws[z], place_ref, w1_ref, depth_z, store)
+    def store(z, hidden, slope):
+        store_level(hidden_low_ref, grad_low_ref, z + 1, hidden, raws[z] * slope, ch1)
+
+    activate([[-1, 0]], plane, place_ref, w1_ref, depth_z, store)
 
     two = 2 * ch2
     odd = jnp.concatenate([odd_ref[c * size : c * size + ch1, :] for c in range(3)], axis=0)
@@ -600,7 +608,7 @@
         fixed_ref[(z - 1) * ch1 : z * ch1, :] = (raw * slope).astype(BF16)
 
     for q in range(0, depth_q, 2):
-        cells = [spread(k, 2) for k in (q, q + 1, q + 2)]
+        cells = [spread(k) for k in (q, q + 1, q + 2)]
         pairs = lanes([jnp.concatenate(cells[n : n + 2], axis=0) for n in range(2)])
         odds, evens = mm(odd, pairs), mm(even, lanes(cells[1:]))
         for n in range(2):
@@ -615,13 +623,15 @@
             return hidden_ref[(z - 1) * size : z * size, :]
         return hidden_edge_ref[(z - depth_z + 1) * size : (z - depth_z + 2) * size, :]
 
+    known = size - ch1
+
     def grad(z):
         if z < 1:
             return grad_low_ref[(z + 1) * size : (z + 2) * size, :]
         if z < depth_z - 1:
-            rest = grad_ref[(z - 1) * size + ch1 : z * size, :]
+            rest = grad_ref[(z - 1) * known : z * known, :]
         else:
-            rest = grad_edge_ref[(z - depth_z + 1) * size + ch1 : (z - depth_z + 2) * size, :]
+            rest = grad_edge_ref[(z - depth_z + 1) * known : (z - depth_z + 2) * known, :]
         return jnp.concatenate([fixed_ref[(z - 1) * ch1 : z * ch1, :], rest], axis=0)
 
     def window(level, z):
@@ -654,7 +664,7 @@
     gin_ref[...] = ginw_ref[...].reshape(gin_ref.shape).astype(BF16)
 
 
-def last(place, low, mid, high, left, corner, wide, w1, odd, even, inner_values, edge_values, w2, w4):
+def last(place, low, mid, high, left, corner, right, shifts, w1, odd, even, inner_values, edge_values, w2, w4):
     depth_z, _, depth_y = mid.shape
     ch2, c_in = w2.shape[0] // 3, w4.shape[0] // 6
     size = w1.shape[0] // 3
@@ -663,7 +673,7 @@
     vmem = pl.BlockSpec(memory_space=pltpu.VMEM)
     return pl.pallas_call(
         last_kernel,
-        in_specs=[pl.BlockSpec(memory_space=pltpu.SMEM)] + [vmem] * 17,
+        in_specs=[pl.BlockSpec(memory_space=pltpu.SMEM)] + [vmem] * 18,
         out_specs=(vmem, vmem),
         out_shape=(
             jax.ShapeDtypeStruct((ch2, depth_q, depth_y // 2), BF16),
@@ -680,7 +690,7 @@
         compiler_params=pltpu.CompilerParams(vmem_limit_bytes=VMEM_LIMIT),
         cost_estimate=pl.CostEstimate(flops=800_000_000, bytes_accessed=10_000_000, transcendentals=0),
         name="features_and_input_grad",
-    )(place, low, mid, high, left, corner, wide, w1, odd, even, *inner_values, *edge_values, w2, w4)
+    )(place, low, mid, high, left, corner, right, shifts, w1, odd, even, *inner_values, *edge_values, w2, w4)
 
 
 def unpack_kernel(sums_ref, first_ref, second_ref, bias1_ref, bias2_ref, *, scale):
@@ -744,18 +754,20 @@
     mid = lax.all_to_all(windows, "xy", split_axis=0, concat_axis=0, tiled=True)
 
     cot = cotangent.reshape(ch2, depth_z // 2, depth_y // 2)
-    shifts, pairs, w1, odd, even, w2, w4 = prepare_own(cot, k1, first_bias[None], k2, second_bias[None])
+    shifts, pairs, w1, odd, even, odd_own, even_own, w2, w4 = prepare_own(
+        cot, k1, first_bias[None], k2, second_bias[None]
+    )
     left, right = shifted(pairs, "xy", 1), shifted(pairs, "xy", -1)
     mid, right = lax.optimization_barrier((mid, right))
 
     rows = mid.shape[1]
     downward = jnp.concatenate([mid[:2].reshape(2 * rows, depth_y), shifts[ch2 : 2 * ch2], right[:ch2]], axis=0)
     high = shifted(downward, "gz", -1)
-    wide, *inner_values, first, second = inner(place, mid, shifts, right, odd, even, w1)
+    *inner_values, first, second = inner(place, mid, shifts, right, odd_own, even_own, w1)
     high, left = lax.optimization_barrier((high, left))
-    *edge_values, sums = edge(place, mid, high, wide, odd, even, shifts, w1, first, second)
-
-    upward = [mid[-2:].reshape(2 * rows, depth_y), left[-ch2:], wide[-2 * ch2 :]]
+    *edge_values, sums = edge(place, mid, high, right, odd_own, even_own, shifts, w1, first, second)
+
+    upward = [mid[-2:].reshape(2 * rows, depth_y), left[-ch2:], shifts[-2 * ch2 : -ch2], right[-ch2:]]
     upward, corner = jnp.concatenate(upward, axis=0), left[:ch2]
     sums, upward, corner = lax.optimization_barrier((sums, upward, corner))
     part = exchange(sums.reshape(slabs, -1, sums.shape[1]), "gz").sum(0)
@@ -765,7 +777,7 @@
     part, low, corner = lax.optimization_barrier((part, low, corner))
     sums = exchange(copies(part, slabs), "gz").reshape(sums.shape)
     features, input_grad = last(
-        place, low, mid, high, left, corner, wide, w1, odd, even, inner_values, edge_values, w2, w4
+        place, low, mid, high, left, corner, right, shifts, w1, odd, even, inner_values, edge_values, w2, w4
     )
     scale = 1.0 / math.sqrt(slabs * depth_z * width * depth_y)
     first_grad, first_bias_grad, second_grad, second_bias_grad = unpack(sums, scale, channels, ch1, ch2)

time: 82.6 us -> 82.6 us (level)
  no operation moved by 1% of the time
where the time goes in v6:
time: 82.6 us; the launch traced here: 82 us
  starting transfers between devices  43 us (52%)
  waiting for transfers between devices  15.9 us (19%)
  blocking collectives  10.6 us (13%)
  Pallas kernels  8.77 us (11%)
  local copies, waits for them, and re-layouts  2.78 us (3%)
    all_to_all x1, starting transfers between devices, shards(): mid = lax.all_to_all(windows, 'xy', split_axis=0, concat_axis=0, tiled=True)  16.6 us
    ppermute x5, starting transfers between devices, shifted(): lax.ppermute(value, axis, [(source, source + steps) for source in range(f...  15.3 us
    all_to_all x2, starting transfers between devices, exchange(): return lax.all_to_all(value, axis, 0, 0, tiled=True)  11.1 us
    all_to_all x1, blocking collectives, exchange(): return lax.all_to_all(value, axis, 0, 0, tiled=True)  10.6 us
    all_to_all x2, waiting for transfers between devices, exchange(): return lax.all_to_all(value, axis, 0, 0, tiled=True)  9.71 us
    all_to_all x1, waiting for transfers between devices, shards(): mid = lax.all_to_all(windows, 'xy', split_axis=0, concat_axis=0, tiled=True)  4.05 us
    pallas_call x1, Pallas kernels, last(): pl.pallas_call(last_kernel, in_specs=[pl.BlockSpec(memory_space=pltpu.SME...  3.08 us
    pallas_call x1, Pallas kernels, inner(): pl.pallas_call(inner_kernel, in_specs=[pl.BlockSpec(memory_space=pltpu.SM...  2.24 us
  transfers between devices with their start and end apart: 8, of which 5 were waited for; matrix products, arithmetic and copies ran while one was open for 0% of the time, Pallas kernels for 7%

profile of v6, /device:TPU:1, one launch (start us, length us, event | category | flops | bytes accessed | tf_op | source)
XLA Modules:
  0.0 82.0 jit_solution(10081185227811008297)
XLA Ops:
  0.6 0.0 copy-start
  0.6 0.8 %copy-done = bf16[4,1,1,1,64,128]{5,4,3,2,1,0:T(8,128)(2,1)S(1)} copy-done((bf16[4,1,1,1,64,128]{5,4,3,2,1,0:T(8,128)(2,1)S(1)}, bf16[4,1,1,1,64,128]{5,4,3,2,1,0:T(8,128)(2,1)}, u32[]{:S(2)}) %copy-start) | copy-done | bytes 65560
  1.5 0.7 pack_windows.1
  2.2 0.0 copy-start.1
  2.2 0.0 copy-start.2
  2.2 0.0 copy-start.3
  2.2 16.6 %all-to-all-start = ((bf16[32,32,128]{2,1,0:T(8,128)(2,1)}), bf16[32,32,128]{2,1,0:T(8,128)(2,1)S(1)}, u32[]{:S(2)}, u32[]{:S(2)}) async-start(bf16[32,32,128]{2,1,0:T(8,128)(2,1)} %pack_windows.1), calls=%async_computation | async-start | bytes 524288 | tf_op jit(solution)/shard_map/all_to_all | solution.py:754
  18.9 0.0 copy-start.4
  18.9 0.0 copy-start.5
  18.9 0.0 copy-done.1
  18.9 0.0 copy-done.2
  18.9 0.0 copy-done.3
  18.9 0.6 copy-done.4
  19.5 0.0 copy-done.5
  19.5 0.6 spread_cotangent.1
  20.2 1.3 %collective-permute-start = (bf16[256,128]{1,0:T(8,128)(2,1)S(1)}, bf16[256,128]{1,0:T(8,128)(2,1)S(1)}, u32[]{:S(2)}, u32[]{:S(2)}) collective-permute-start(bf16[256,128]{1,0:T(8,128)(2,1)S(1)} %get-tuple-element.43), channel_id=1, source_target_pairs={{1,0},{2,1},{3,2},{4,3},{5,4},{6,5},{7,6},{8,7},{9,8},{10,9},{11,1... | collective-permute-start | bytes 196616 | tf_op jit(solution)/shard_map/ppermute | solution.py:21
  21.5 4.0 %collective-permute-start.2 = (bf16[256,128]{1,0:T(8,128)(2,1)S(1)}, bf16[256,128]{1,0:T(8,128)(2,1)S(1)}, u32[]{:S(2)}, u32[]{:S(2)}) collective-permute-start(bf16[256,128]{1,0:T(8,128)(2,1)S(1)} %get-tuple-element.43), channel_id=1, source_target_pairs={{0,1},{1,2},{2,3},{3,4},{4,5},{5,6},{6,7},{7,8},{8,9},{9,10},{10,1... | collective-permute-start | bytes 196616 | tf_op jit(solution)/shard_map/ppermute | solution.py:21
  25.5 1.8 %collective-permute-done.right_ref = bf16[256,128]{1,0:T(8,128)(2,1)S(1)} collective-permute-done((bf16[256,128]{1,0:T(8,128)(2,1)S(1)}, bf16[256,128]{1,0:T(8,128)(2,1)S(1)}, u32[]{:S(2)}, u32[]{:S(2)}) %collective-permute-start) | collective-permute-done | bytes 65568 | tf_op jit(solution)/shard_map/ppermute | solution.py:21
  27.3 4.1 %all-to-all-done.mid_ref = bf16[32,32,128]{2,1,0:T(8,128)(2,1)S(1)} async-done(((bf16[32,32,128]{2,1,0:T(8,128)(2,1)}), bf16[32,32,128]{2,1,0:T(8,128)(2,1)S(1)}, u32[]{:S(2)}, u32[]{:S(2)}) %all-to-all-start) | async-done | bytes 262176 | tf_op jit(solution)/shard_map/all_to_all | solution.py:754
  31.4 5.3 %collective-permute-start.1 = (bf16[128,128]{1,0:T(8,128)(2,1)S(1)}, bf16[128,128]{1,0:T(8,128)(2,1)S(1)}, u32[]{:S(2)}, u32[]{:S(2)}) collective-permute-start(bf16[128,128]{1,0:T(8,128)(2,1)S(1)} %pad_maximum_fusion.1), channel_id=1, source_target_pairs={{32,0},{64,32},{96,64},{128,96},{160,128},{192,160},{224,192},{256... | collective-permute-start | bytes 98312 | tf_op jit(solution)/shard_map/ppermute | solution.py:21
  36.7 0.1 add_convert_fusion.place_ref
  36.7 2.2 %inner_levels.1 = (bf16[1920,128]{1,0:T(8,128)(2,1)S(1)}, bf16[1440,128]{1,0:T(8,128)(2,1)S(1)}, f32[480,128]{1,0:T(8,128)S(1)}, f32[96,96]{1,0:T(8,128)S(1)}, f32[192,96]{1,0:T(8,128)S(1)}) custom-call(s32[4]{0:T(128)S(1)} %add_convert_fusion.place_ref, bf16[32,32,128]{2,1,0:T(8,128)(2,1)S(1)} %all-to-all-done.mid_ref, ...), custom_call_target="tpu_custom_call" | custom-call | tf_op jit(solution)/shard_map/inner_levels/pallas_call | solution.py:482
  39.0 0.0 collective-permute-done.2.left_ref
  39.0 0.3 collective-permute-done.1.high_ref
  39.3 1.2 %edge_levels_and_sums.1 = (bf16[128,128]{1,0:T(8,128)(2,1)S(1)}, bf16[96,128]{1,0:T(8,128)(2,1)S(1)}, f32[32,128]{1,0:T(8,128)S(1)}, f32[128,128]{1,0:T(8,128)S(1)}) custom-call(s32[4]{0:T(128)S(1)} %add_convert_fusion.place_ref, bf16[32,32,128]{2,1,0:T(8,128)(2,1)S(1)} %all-to-all-done.mid_ref, bf16[128,128]{1,0:T(8,128)(2,1)S(1)} %collective-permute-done.1.high_ref, ...), custom_call_target="tpu_custom_call" | custom-call | tf_op jit(solution)/shard_map/edge_levels_and_sums/pallas_call | solution.py:510
  40.6 10.6 %all_to_all.20 = f32[16,8,128]{2,1,0:T(8,128)S(1)} all-to-all(f32[16,8,128]{2,1,0:T(8,128)S(1)} %bitcast.32), channel_id=1, replica_groups=mesh['gz'=16,'xy'=32] {'gz'}, dimensions={0} | all-to-all | bytes 131072 | tf_op jit(solution)/shard_map/all_to_all | solution.py:735
  51.3 0.7 broadcast_in_dim.23
  51.9 5.7 %all-to-all-start.2 = ((f32[32,8,128]{2,1,0:T(8,128)}), f32[32,8,128]{2,1,0:T(8,128)S(1)}, u32[]{:S(2)}, u32[]{:S(2)}) async-start(f32[32,8,128]{2,1,0:T(8,128)} %broadcast_in_dim.23), calls=%async_computation.2 | async-start | bytes 262144 | tf_op jit(solution)/shard_map/all_to_all | solution.py:735
  57.7 2.8 %collective-permute-start.3 = (bf16[160,128]{1,0:T(8,128)(2,1)S(1)}, bf16[160,128]{1,0:T(8,128)(2,1)S(1)}, u32[]{:S(2)}, u32[]{:S(2)}) collective-permute-start(bf16[160,128]{1,0:T(8,128)(2,1)S(1)} %pad_maximum_fusion), channel_id=1, source_target_pairs={{0,32},{32,64},{64,96},{96,128},{128,160},{160,192},{192,224},{224... | collective-permute-start | bytes 122888 | tf_op jit(solution)/shard_map/ppermute | solution.py:21
  60.4 1.9 %collective-permute-start.4 = (bf16[32,128]{1,0:T(8,128)(2,1)S(1)}, bf16[32,128]{1,0:T(8,128)(2,1)S(1)}, u32[]{:S(2)}, u32[]{:S(2)}) collective-permute-start(bf16[32,128]{1,0:T(8,128)(2,1)S(1)} %get-tuple-element.60), channel_id=1, source_target_pairs={{32,0},{64,32},{96,64},{128,96},{160,128},{192,160},{224,192},{256... | collective-permute-start | bytes 24584 | tf_op jit(solution)/shard_map/ppermute | solution.py:21
  62.4 6.9 %all-to-all-done.2 = f32[32,8,128]{2,1,0:T(8,128)S(1)} async-done(((f32[32,8,128]{2,1,0:T(8,128)}), f32[32,8,128]{2,1,0:T(8,128)S(1)}, u32[]{:S(2)}, u32[]{:S(2)}) %all-to-all-start.2) | async-done | bytes 131104 | tf_op jit(solution)/shard_map/all_to_all | solution.py:735
  69.3 0.0 collective-permute-done.4.corner_ref
  69.3 0.0 collective-permute-done.3.low_ref
  69.3 0.6 broadcast_in_dim.25
  69.9 5.4 %all-to-all-start.3 = ((f32[16,8,128]{2,1,0:T(8,128)}), f32[16,8,128]{2,1,0:T(8,128)S(1)}, u32[]{:S(2)}, u32[]{:S(2)}) async-start(f32[16,8,128]{2,1,0:T(8,128)} %broadcast_in_dim.25), calls=%async_computation.3 | async-start | bytes 131072 | tf_op jit(solution)/shard_map/all_to_all | solution.py:735
  75.3 3.1 %features_and_input_grad.1 = (bf16[32,16,64]{2,1,0:T(8,128)(2,1)}, bf16[4,64,128]{2,1,0:T(8,128)(2,1)}) custom-call(s32[4]{0:T(128)S(1)} %add_convert_fusion.place_ref, bf16[160,128]{1,0:T(8,128)(2,1)S(1)} %collective-permute-done.3.low_ref, bf16[32,32,128]{2,1,0:T(8,128)(2,1)S(1)} %all-to-all-done.mid_ref, ...), custom_call_target="tpu_custom_call" | custom-call | flops 800000000 | bytes 10000000 | tf_op jit(solution)/shard_map/features_and_input_grad/pallas_call | solution.py:674
  78.4 2.8 %all-to-all-done.3 = f32[16,8,128]{2,1,0:T(8,128)S(1)} async-done(((f32[16,8,128]{2,1,0:T(8,128)}), f32[16,8,128]{2,1,0:T(8,128)S(1)}, u32[]{:S(2)}, u32[]{:S(2)}) %all-to-all-start.3) | async-done | bytes 65568 | tf_op jit(solution)/shard_map/all_to_all | solution.py:735
  81.2 0.8 %unpack_sums.1 = (f32[27,4,16]{2,1,0:T(4,128)}, f32[27,16,32]{2,1,0:T(8,128)}, f32[1,16]{1,0:T(1,128)}, f32[1,32]{1,0:T(1,128)}) custom-call(f32[128,128]{1,0:T(8,128)S(1)} %bitcast.30), custom_call_target="tpu_custom_call" | custom-call | tf_op jit(solution)/shard_map/unpack_sums/pallas_call | solution.py:722
  (8 shorter events, 0.1 us)
Async XLA Ops:
  0.6 0.8 %copy-start = (bf16[4,1,1,1,64,128]{5,4,3,2,1,0:T(8,128)(2,1)S(1)}, bf16[4,1,1,1,64,128]{5,4,3,2,1,0:T(8,128)(2,1)}, u32[]{:S(2)}) copy-start(bf16[4,1,1,1,64,128]{5,4,3,2,1,0:T(8,128)(2,1)} %param.6) | copy-start | bytes 196612
  2.2 16.7 %copy-start.1 = (bf16[32,16,1,64]{3,1,2,0:T(8,128)(2,1)S(1)}, bf16[32,16,1,64]{3,1,2,0:T(8,128)(2,1)}, u32[]{:S(2)}) copy-start(bf16[32,16,1,64]{3,1,2,0:T(8,128)(2,1)} %param.11) | copy-start | bytes 196612
  2.2 16.7 %copy-start.2 = (bf16[32,16,3,3,3]{0,1,4,3,2:T(8,128)(2,1)S(1)}, bf16[32,16,3,3,3]{0,1,4,3,2:T(8,128)(2,1)}, u32[]{:S(2)}) copy-start(bf16[32,16,3,3,3]{0,1,4,3,2:T(8,128)(2,1)} %param.9) | copy-start | bytes 82948
  2.2 16.7 %copy-start.3 = (bf16[16,4,3,3,3]{0,1,4,3,2:T(4,128)(2,1)S(1)}, bf16[16,4,3,3,3]{0,1,4,3,2:T(4,128)(2,1)}, u32[]{:S(2)}) copy-start(bf16[16,4,3,3,3]{0,1,4,3,2:T(4,128)(2,1)} %param.7) | copy-start | bytes 10372
  2.2 29.1 %all-to-all-start = ((bf16[32,32,128]{2,1,0:T(8,128)(2,1)}), bf16[32,32,128]{2,1,0:T(8,128)(2,1)S(1)}, u32[]{:S(2)}, u32[]{:S(2)}) async-start(bf16[32,32,128]{2,1,0:T(8,128)(2,1)} %pack_windows.1), calls=%async_computation | async-start | bytes 524288 | tf_op jit(solution)/shard_map/all_to_all | solution.py:754
  18.9 0.7 copy-start.4
  18.9 0.7 copy-start.5
  20.2 7.1 %collective-permute-start = (bf16[256,128]{1,0:T(8,128)(2,1)S(1)}, bf16[256,128]{1,0:T(8,128)(2,1)S(1)}, u32[]{:S(2)}, u32[]{:S(2)}) collective-permute-start(bf16[256,128]{1,0:T(8,128)(2,1)S(1)} %get-tuple-element.43), channel_id=1, source_target_pairs={{1,0},{2,1},{3,2},{4,3},{5,4},{6,5},{7,6},{8,7},{9,8},{10,9},{11,1... | collective-permute-start | bytes 196616 | tf_op jit(solution)/shard_map/ppermute | solution.py:21
  21.5 17.5 %collective-permute-start.2 = (bf16[256,128]{1,0:T(8,128)(2,1)S(1)}, bf16[256,128]{1,0:T(8,128)(2,1)S(1)}, u32[]{:S(2)}, u32[]{:S(2)}) collective-permute-start(bf16[256,128]{1,0:T(8,128)(2,1)S(1)} %get-tuple-element.43), channel_id=1, source_target_pairs={{0,1},{1,2},{2,3},{3,4},{4,5},{5,6},{6,7},{7,8},{8,9},{9,10},{10,1... | collective-permute-start | bytes 196616 | tf_op jit(solution)/shard_map/ppermute | solution.py:21
  31.4 8.0 %collective-permute-start.1 = (bf16[128,128]{1,0:T(8,128)(2,1)S(1)}, bf16[128,128]{1,0:T(8,128)(2,1)S(1)}, u32[]{:S(2)}, u32[]{:S(2)}) collective-permute-start(bf16[128,128]{1,0:T(8,128)(2,1)S(1)} %pad_maximum_fusion.1), channel_id=1, source_target_pairs={{32,0},{64,32},{96,64},{128,96},{160,128},{192,160},{224,192},{256... | collective-permute-start | bytes 98312 | tf_op jit(solution)/shard_map/ppermute | solution.py:21
  51.9 17.3 %all-to-all-start.2 = ((f32[32,8,128]{2,1,0:T(8,128)}), f32[32,8,128]{2,1,0:T(8,128)S(1)}, u32[]{:S(2)}, u32[]{:S(2)}) async-start(f32[32,8,128]{2,1,0:T(8,128)} %broadcast_in_dim.23), calls=%async_computation.2 | async-start | bytes 262144 | tf_op jit(solution)/shard_map/all_to_all | solution.py:735
  57.7 11.6 %collective-permute-start.3 = (bf16[160,128]{1,0:T(8,128)(2,1)S(1)}, bf16[160,128]{1,0:T(8,128)(2,1)S(1)}, u32[]{:S(2)}, u32[]{:S(2)}) collective-permute-start(bf16[160,128]{1,0:T(8,128)(2,1)S(1)} %pad_maximum_fusion), channel_id=1, source_target_pairs={{0,32},{32,64},{64,96},{96,128},{128,160},{160,192},{192,224},{224... | collective-permute-start | bytes 122888 | tf_op jit(solution)/shard_map/ppermute | solution.py:21
  60.4 8.9 %collective-permute-start.4 = (bf16[32,128]{1,0:T(8,128)(2,1)S(1)}, bf16[32,128]{1,0:T(8,128)(2,1)S(1)}, u32[]{:S(2)}, u32[]{:S(2)}) collective-permute-start(bf16[32,128]{1,0:T(8,128)(2,1)S(1)} %get-tuple-element.60), channel_id=1, source_target_pairs={{32,0},{64,32},{96,64},{128,96},{160,128},{192,160},{224,192},{256... | collective-permute-start | bytes 24584 | tf_op jit(solution)/shard_map/ppermute | solution.py:21
  69.9 11.3 %all-to-all-start.3 = ((f32[16,8,128]{2,1,0:T(8,128)}), f32[16,8,128]{2,1,0:T(8,128)S(1)}, u32[]{:S(2)}, u32[]{:S(2)}) async-start(f32[16,8,128]{2,1,0:T(8,128)} %broadcast_in_dim.25), calls=%async_computation.3 | async-start | bytes 131072 | tf_op jit(solution)/shard_map/all_to_all | solution.py:735
